TPU v7x, 32 devices: a whole 2x2x4 slice. The times are simulated.
32 devices in a mesh: dp: 8 (over y, x, core), tensor: 4 (over z).
Axes of the slice: x: 2, y: 2, z: 4, core: 2. Of those that a mesh axis runs over, the one named last changes fastest.
Arguments:
- latents: bfloat16 [4096, 1536], P('dp'), may hold values from -6 to 6
- context: bfloat16 [1024, 1536], P('dp'), may hold values from -6 to 6
- time_embed: float32 [2, 6, 1536], replicated, may hold values from -3 to 3
- teacher: bfloat16 [4096, 1536], P('dp'), may hold values from -6 to 6
- lengths: int32 [2], replicated, may hold values from 1844 to 2048, as said below
- block_order: int32 [8], P('dp'), may hold values from 0 to 3, as said below
- positions: int32 [3, 4096], P(None, 'dp'), may hold values from 0 to 63
- self_proj: bfloat16 [2, 3, 1536, 1536], P(None, None, 'dp', 'tensor'), may hold values from -0.15625 to 0.15625
- cross_proj: bfloat16 [2, 3, 1536, 1536], P(None, None, 'dp', 'tensor'), may hold values from -0.15625 to 0.15625
- out_proj: bfloat16 [2, 2, 1536, 1536], P(None, None, 'tensor', 'dp'), may hold values from -0.625 to 0.625
- ffn_up: bfloat16 [2, 1536, 8960], P(None, 'dp', 'tensor'), may hold values from -0.15625 to 0.15625
- ffn_down: bfloat16 [2, 8960, 1536], P(None, 'tensor', 'dp'), may hold values from -0.0625 to 0.0625
- proj_bias: float32 [2, 5, 1536], P(None, None, 'tensor'), may hold values from -2 to 2
- key_bias: float32 [2, 1536], P(None, 'tensor'), may hold values from -2 to 2
- norm_gains: float32 [2, 4, 1536], P(None, None, 'tensor'), may hold values from 0.25 to 1.75
- ffn_bias: float32 [2, 8960], P(None, 'tensor'), may hold values from -2 to 2
- out_bias: float32 [2, 3, 1536], replicated, may hold values from -2 to 2
- cross_gain: float32 [2, 1536], replicated, may hold values from 0.25 to 1.75
- cross_shift: float32 [2, 1536], replicated, may hold values from -2 to 2
- modulation: float32 [2, 6, 1536], replicated, may hold values from -3 to 3
Outputs:
- output: float32 [4096, 1536], P('dp')
- loss: float32 [], replicated
- latents_grad: float32 [4096, 1536], P('dp')
- context_grad: float32 [1024, 1536], P('dp')
- time_grad: float32 [2, 6, 1536], replicated
- self_proj_grad: float32 [2, 3, 1536, 1536], P(None, None, 'dp', 'tensor')
- cross_proj_grad: float32 [2, 3, 1536, 1536], P(None, None, 'dp', 'tensor')
- out_proj_grad: float32 [2, 2, 1536, 1536], P(None, None, 'tensor', 'dp')
- ffn_up_grad: float32 [2, 1536, 8960], P(None, 'dp', 'tensor')
- ffn_down_grad: float32 [2, 8960, 1536], P(None, 'tensor', 'dp')
- proj_bias_grad: float32 [2, 5, 1536], P(None, None, 'tensor')
- key_bias_grad: float32 [2, 1536], P(None, 'tensor')
- norm_gains_grad: float32 [2, 4, 1536], P(None, None, 'tensor')
- ffn_bias_grad: float32 [2, 8960], P(None, 'tensor')
- out_bias_grad: float32 [2, 3, 1536], replicated
- cross_gain_grad: float32 [2, 1536], replicated
- cross_shift_grad: float32 [2, 1536], replicated
- modulation_grad: float32 [2, 6, 1536], replicated
Inputs may be any that keep to these rules, and one draw needn't show every extreme that they name: `lengths`: every clip has at least 1844 valid slots; in every draw exactly one clip has all 2048 slots valid. `block_order`: within each group of 4 consecutive devices of dp the values are a permutation of 0 to 3.
All inputs are finite; a program needn't handle non-finite values.
Results may differ from a plain program's by a relative error of at most 0.038.
Values may be sent and summed in bfloat16 or wider, within the bound.
A program may use at most 320 MiB of HBM per device.

v0:
```python
import math

import jax
import jax.numpy as jnp
import numpy as np
from jax import lax
from jax.sharding import PartitionSpec as P

HEAD_DIM = 128
HOLD = 4
LAYERS = 2


highest = lax.Precision.HIGHEST
epsilon = 1e-06
masked_fill = -1e30


def from_partner(block, axis, distance):
    count = lax.axis_size(axis)
    route = []
    for low in range(count):
        high = low | 1 << distance
        if high != low and high < count:
            route += [(low, high), (high, low)]
    return lax.ppermute(block, axis, route)


def rope_table(head_size):
    third = head_size // 6
    spans = [head_size - 4 * third, 2 * third, 2 * third]
    table = np.zeros((3, head_size), np.float32)
    start_col = 0
    for component in range(3):
        for pair_index in range(spans[component] // 2):
            freq_value = 10000.0 ** (-(2.0 * pair_index) / spans[component])
            table[component, start_col + 2 * pair_index] = freq_value
            table[component, start_col + 2 * pair_index + 1] = freq_value
        start_col += spans[component]
    return table


def turn_matrix(head_size):
    matrix = np.zeros((head_size, head_size), np.float32)
    for pair_index in range(head_size // 2):
        matrix[2 * pair_index + 1, 2 * pair_index] = -1.0
        matrix[2 * pair_index, 2 * pair_index + 1] = 1.0
    return matrix


def rope_angles(positions, head_size):
    table = rope_table(head_size)
    places = positions.astype(jnp.float32)
    angles = (
        places[0][:, None] * table[0][None, :]
        + places[1][:, None] * table[1][None, :]
        + places[2][:, None] * table[2][None, :]
    )
    return (jnp.cos(angles), jnp.sin(angles))


def rotate(values, cosine, sine_rows):
    turned = jnp.einsum("nhd,de->nhe", values, turn_matrix(values.shape[-1]), precision=highest)
    return values * cosine[:, None, :] + turned * sine_rows[:, None, :]


def rotate_back(grads, cosine, sine_rows):
    turned = jnp.einsum(
        "nhe,de->nhd",
        grads * sine_rows[:, None, :],
        turn_matrix(grads.shape[-1]),
        precision=highest,
    )
    return grads * cosine[:, None, :] + turned


def layer_norm(values):
    center = values - jnp.mean(values, axis=-1, keepdims=True)
    return center * lax.rsqrt(jnp.mean(center * center, axis=-1, keepdims=True) + epsilon)


def modulated(values, shift_row, scale_row):
    return layer_norm(values) * (1.0 + scale_row) + shift_row


def affine_norm(values, gain_row, shift_row):
    return layer_norm(values) * gain_row + shift_row


def gelu_tanh(values):
    return (
        0.5
        * values
        * (1.0 + jnp.tanh(0.7978845608028654 * (values + 0.044715 * values * values * values)))
    )


def rms_back(proj_rows, inverse, gain_row, grad_rows, total_term, model_width):
    cubed = inverse * inverse * inverse
    return (
        inverse[:, None] * gain_row * grad_rows
        - proj_rows * (cubed * total_term / model_width)[:, None]
    )


def head_total(partial_rows):
    return lax.psum(partial_rows.astype(jnp.bfloat16), "tensor").astype(jnp.float32)


def input_total(partial_rows):
    return lax.psum(partial_rows.astype(jnp.bfloat16), "tensor").astype(jnp.float32)


def norm_total(partial_rows):
    return lax.psum(partial_rows, "tensor")


def norm_grad_total(partial_rows):
    return lax.psum(partial_rows, "tensor")


def gather_clip(key_rot, value_heads, key_flags, text_key, text_value):
    for bit_index in range(HOLD.bit_length() - 1):
        other = from_partner(
            (key_rot, value_heads, key_flags, text_key, text_value), "dp", bit_index
        )
        key_rot = jnp.concatenate([key_rot, other[0]], axis=0)
        value_heads = jnp.concatenate([value_heads, other[1]], axis=0)
        key_flags = jnp.concatenate([key_flags, other[2]], axis=0)
        text_key = jnp.concatenate([text_key, other[3]], axis=0)
        text_value = jnp.concatenate([text_value, other[4]], axis=0)
    return (key_rot, value_heads, key_flags, text_key, text_value)


def reduce_clip(key_grad, value_grad, text_key_grad, text_value_grad):
    for bit_index in reversed(range(HOLD.bit_length() - 1)):
        half_keys = key_grad.shape[0] // 2
        half_text = text_key_grad.shape[0] // 2
        arrived = (
            from_partner(key_grad[half_keys:].astype(jnp.bfloat16), "dp", bit_index).astype(
                jnp.float32
            ),
            from_partner(value_grad[half_keys:].astype(jnp.bfloat16), "dp", bit_index).astype(
                jnp.float32
            ),
            from_partner(text_key_grad[half_text:].astype(jnp.bfloat16), "dp", bit_index).astype(
                jnp.float32
            ),
            from_partner(text_value_grad[half_text:].astype(jnp.bfloat16), "dp", bit_index).astype(
                jnp.float32
            ),
        )
        key_grad = key_grad[:half_keys] + arrived[0]
        value_grad = value_grad[:half_keys] + arrived[1]
        text_key_grad = text_key_grad[:half_text] + arrived[2]
        text_value_grad = text_value_grad[:half_text] + arrived[3]
    return (key_grad, value_grad, text_key_grad, text_value_grad)


def score_block(query_b, key_b, key_flags):
    scaling = 1.0 / math.sqrt(query_b.shape[-1])
    scores = (
        jnp.einsum("qhd,khd->hqk", query_b, key_b, preferred_element_type=jnp.float32) * scaling
    )
    if key_flags is None:
        return scores
    return jnp.where(key_flags[None, None, :] > 0.5, scores, masked_fill)


def attend_forward(query_b, key_b, value_b, key_flags):
    scores = score_block(query_b, key_b, key_flags)
    row_max = jnp.max(scores, axis=-1, keepdims=True)
    shifted = jnp.exp(scores - row_max)
    row_total = jnp.sum(shifted, axis=-1, keepdims=True)
    weights = (shifted / row_total).astype(jnp.bfloat16)
    result = jnp.einsum("hqk,khd->qhd", weights, value_b, preferred_element_type=jnp.float32)
    return (result, row_max + jnp.log(row_total))


def attend_backward(query_b, key_b, value_b, key_flags, log_total, out_grad_b):
    scaling = 1.0 / math.sqrt(query_b.shape[-1])
    scores = score_block(query_b, key_b, key_flags)
    probs = jnp.exp(scores - log_total)
    probs_b = probs.astype(jnp.bfloat16)
    prob_grad = jnp.einsum("qhd,khd->hqk", out_grad_b, value_b, preferred_element_type=jnp.float32)
    score_grad = probs * (prob_grad - jnp.sum(probs * prob_grad, axis=-1, keepdims=True))
    score_b = (score_grad * scaling).astype(jnp.bfloat16)
    query_grad = jnp.einsum("hqk,khd->qhd", score_b, key_b, preferred_element_type=jnp.float32)
    key_grad = jnp.einsum("hqk,qhd->khd", score_b, query_b, preferred_element_type=jnp.float32)
    value_grad = jnp.einsum("hqk,qhd->khd", probs_b, out_grad_b, preferred_element_type=jnp.float32)
    return (query_grad, key_grad, value_grad)


def forward_layer(
    hidden, weights, vectors, time_row, key_flags, cosine, sine_rows, context_rows, model_width
):
    self_weight, cross_weight, out_weight, up_weight, down_weight = weights
    bias_rows, key_row, gain_rows, up_bias, out_rows, norm_gain, norm_shift, mod_rows = vectors
    tok_count = hidden.shape[0]
    text_count = context_rows.shape[0]
    local_width = bias_rows.shape[-1]
    head_count = local_width // HEAD_DIM
    mod_terms = mod_rows + time_row
    first_in = modulated(hidden, mod_terms[0], mod_terms[1]).astype(jnp.bfloat16)
    self_bias = jnp.stack([bias_rows[0], key_row, bias_rows[1]])
    projected = (
        jnp.einsum("td,cdh->cth", first_in, self_weight, preferred_element_type=jnp.float32)
        + self_bias[:, None, :]
    )
    text_proj = (
        jnp.einsum(
            "td,cdh->cth", context_rows, cross_weight[1:3], preferred_element_type=jnp.float32
        )
        + bias_rows[3:5][:, None, :]
    )
    joined_sq = norm_total(
        jnp.concatenate(
            [
                jnp.sum(projected[0] * projected[0], axis=-1),
                jnp.sum(projected[1] * projected[1], axis=-1),
                jnp.sum(text_proj[0] * text_proj[0], axis=-1),
            ],
            axis=0,
        )
    )
    query_sq = joined_sq[:tok_count]
    key_sq = joined_sq[tok_count : 2 * tok_count]
    text_sq = joined_sq[2 * tok_count :]
    query_inv = lax.rsqrt(query_sq / model_width + epsilon)
    key_inv = lax.rsqrt(key_sq / model_width + epsilon)
    text_inv = lax.rsqrt(text_sq / model_width + epsilon)
    query_rot = rotate(
        (projected[0] * query_inv[:, None] * gain_rows[0]).reshape(tok_count, head_count, HEAD_DIM),
        cosine,
        sine_rows,
    ).astype(jnp.bfloat16)
    key_rot = rotate(
        (projected[1] * key_inv[:, None] * gain_rows[1]).reshape(tok_count, head_count, HEAD_DIM),
        cosine,
        sine_rows,
    ).astype(jnp.bfloat16)
    value_heads = projected[2].astype(jnp.bfloat16).reshape(tok_count, head_count, HEAD_DIM)
    text_key = (
        (text_proj[0] * text_inv[:, None] * gain_rows[3])
        .astype(jnp.bfloat16)
        .reshape(text_count, head_count, HEAD_DIM)
    )
    text_value = text_proj[1].astype(jnp.bfloat16).reshape(text_count, head_count, HEAD_DIM)
    all_keys, all_values, all_flags, all_text_keys, all_text_values = gather_clip(
        key_rot, value_heads, key_flags, text_key, text_value
    )
    attended, self_lse = attend_forward(query_rot, all_keys, all_values, all_flags)
    attended_b = attended.reshape(tok_count, local_width).astype(jnp.bfloat16)
    self_branch = (
        head_total(jnp.dot(attended_b, out_weight[0], preferred_element_type=jnp.float32))
        + out_rows[0]
    )
    after_self = hidden + self_branch * mod_terms[2]
    cross_in = affine_norm(after_self, norm_gain, norm_shift).astype(jnp.bfloat16)
    cross_query = (
        jnp.dot(cross_in, cross_weight[0], preferred_element_type=jnp.float32) + bias_rows[2]
    )
    cross_sq = norm_total(jnp.sum(cross_query * cross_query, axis=-1))
    cross_inv = lax.rsqrt(cross_sq / model_width + epsilon)
    cross_heads = (
        (cross_query * cross_inv[:, None] * gain_rows[2])
        .astype(jnp.bfloat16)
        .reshape(tok_count, head_count, HEAD_DIM)
    )
    cross_out, cross_lse = attend_forward(cross_heads, all_text_keys, all_text_values, None)
    cross_b = cross_out.reshape(tok_count, local_width).astype(jnp.bfloat16)
    cross_branch = (
        head_total(jnp.dot(cross_b, out_weight[1], preferred_element_type=jnp.float32))
        + out_rows[1]
    )
    after_cross = after_self + cross_branch
    ffn_in = modulated(after_cross, mod_terms[3], mod_terms[4]).astype(jnp.bfloat16)
    inner = jnp.dot(ffn_in, up_weight, preferred_element_type=jnp.float32) + up_bias
    gelu_b = gelu_tanh(inner).astype(jnp.bfloat16)
    ffn_branch = (
        head_total(jnp.dot(gelu_b, down_weight, preferred_element_type=jnp.float32)) + out_rows[2]
    )
    result = after_cross + ffn_branch * mod_terms[5]
    saved = {
        "hidden": hidden,
        "first_in": first_in,
        "projected": projected,
        "text_proj": text_proj,
        "query_inv": query_inv,
        "key_inv": key_inv,
        "text_inv": text_inv,
        "query_rot": query_rot,
        "all_keys": all_keys,
        "all_values": all_values,
        "all_flags": all_flags,
        "self_lse": self_lse,
        "attended_b": attended_b,
        "self_branch": self_branch,
        "after_self": after_self,
        "cross_in": cross_in,
        "cross_query": cross_query,
        "cross_inv": cross_inv,
        "cross_heads": cross_heads,
        "all_text_keys": all_text_keys,
        "all_text_values": all_text_values,
        "cross_lse": cross_lse,
        "cross_b": cross_b,
        "after_cross": after_cross,
        "ffn_in": ffn_in,
        "inner": inner,
        "gelu_b": gelu_b,
        "ffn_branch": ffn_branch,
    }
    return (result, saved)


def backward_layer(
    grad, saved, weights, vectors, time_row, cosine, sine_rows, context_rows, model_width
):
    self_weight, cross_weight, out_weight, up_weight, down_weight = weights
    bias_rows, key_row, gain_rows, up_bias, out_rows, norm_gain, norm_shift, mod_rows = vectors
    tok_count = grad.shape[0]
    text_count = context_rows.shape[0]
    local_width = bias_rows.shape[-1]
    head_count = local_width // HEAD_DIM
    mod_terms = mod_rows + time_row
    down_in = (grad * mod_terms[5]).astype(jnp.bfloat16)
    mod_five = jnp.sum(grad * saved["ffn_branch"], axis=0)
    out_bias_two = jnp.sum(down_in.astype(jnp.float32), axis=0)
    down_grad = jnp.einsum(
        "tf,td->fd", saved["gelu_b"], down_in, preferred_element_type=jnp.float32
    )
    gelu_grad = jnp.einsum("td,fd->tf", down_in, down_weight, preferred_element_type=jnp.float32)
    unused_out, gelu_pull = jax.vjp(gelu_tanh, saved["inner"])
    inner_b = gelu_pull(gelu_grad)[0].astype(jnp.bfloat16)
    up_bias_grad = jnp.sum(inner_b.astype(jnp.float32), axis=0)
    up_grad = jnp.einsum("td,tf->df", saved["ffn_in"], inner_b, preferred_element_type=jnp.float32)
    ffn_in_grad = input_total(
        jnp.einsum("tf,df->td", inner_b, up_weight, preferred_element_type=jnp.float32)
    )
    unused_out, ffn_pull = jax.vjp(modulated, saved["after_cross"], mod_terms[3], mod_terms[4])
    hidden_part, mod_three, mod_four = ffn_pull(ffn_in_grad)
    grad = grad + hidden_part
    cross_down = grad.astype(jnp.bfloat16)
    out_bias_one = jnp.sum(cross_down.astype(jnp.float32), axis=0)
    cross_out_grad = jnp.einsum(
        "th,td->hd", saved["cross_b"], cross_down, preferred_element_type=jnp.float32
    )
    cross_att_grad = (
        jnp.einsum("td,hd->th", cross_down, out_weight[1], preferred_element_type=jnp.float32)
        .astype(jnp.bfloat16)
        .reshape(tok_count, head_count, HEAD_DIM)
    )
    cross_q_grad, text_key_all, text_value_all = attend_backward(
        saved["cross_heads"],
        saved["all_text_keys"],
        saved["all_text_values"],
        None,
        saved["cross_lse"],
        cross_att_grad,
    )
    cross_q_grad = cross_q_grad.reshape(tok_count, local_width)
    cross_query = saved["cross_query"]
    cross_inv = saved["cross_inv"]
    cross_term = norm_grad_total(jnp.sum(cross_query * gain_rows[2] * cross_q_grad, axis=-1))
    cross_gain_grad = jnp.sum(cross_query * cross_inv[:, None] * cross_q_grad, axis=0)
    cross_proj_b = rms_back(
        cross_query, cross_inv, gain_rows[2], cross_q_grad, cross_term, model_width
    ).astype(jnp.bfloat16)
    cross_bias_grad = jnp.sum(cross_proj_b.astype(jnp.float32), axis=0)
    cross_q_weight = jnp.einsum(
        "td,th->dh", saved["cross_in"], cross_proj_b, preferred_element_type=jnp.float32
    )
    cross_in_grad = input_total(
        jnp.einsum("th,dh->td", cross_proj_b, cross_weight[0], preferred_element_type=jnp.float32)
    )
    unused_out, affine_pull = jax.vjp(affine_norm, saved["after_self"], norm_gain, norm_shift)
    hidden_part, norm_gain_grad, norm_shift_grad = affine_pull(cross_in_grad)
    grad = grad + hidden_part
    self_down = (grad * mod_terms[2]).astype(jnp.bfloat16)
    mod_two = jnp.sum(grad * saved["self_branch"], axis=0)
    out_bias_zero = jnp.sum(self_down.astype(jnp.float32), axis=0)
    self_out_grad = jnp.einsum(
        "th,td->hd", saved["attended_b"], self_down, preferred_element_type=jnp.float32
    )
    self_att_grad = (
        jnp.einsum("td,hd->th", self_down, out_weight[0], preferred_element_type=jnp.float32)
        .astype(jnp.bfloat16)
        .reshape(tok_count, head_count, HEAD_DIM)
    )
    query_rot_grad, key_all_grad, value_all_grad = attend_backward(
        saved["query_rot"],
        saved["all_keys"],
        saved["all_values"],
        saved["all_flags"],
        saved["self_lse"],
        self_att_grad,
    )
    key_rot_grad, value_grad, text_key_grad, text_value_grad = reduce_clip(
        key_all_grad, value_all_grad, text_key_all, text_value_all
    )
    query_n_grad = rotate_back(query_rot_grad, cosine, sine_rows).reshape(tok_count, local_width)
    key_n_grad = rotate_back(key_rot_grad, cosine, sine_rows).reshape(tok_count, local_width)
    text_n_grad = text_key_grad.reshape(text_count, local_width)
    projected = saved["projected"]
    text_proj = saved["text_proj"]
    joined_terms = norm_grad_total(
        jnp.concatenate(
            [
                jnp.sum(projected[0] * gain_rows[0] * query_n_grad, axis=-1),
                jnp.sum(projected[1] * gain_rows[1] * key_n_grad, axis=-1),
                jnp.sum(text_proj[0] * gain_rows[3] * text_n_grad, axis=-1),
            ],
            axis=0,
        )
    )
    query_term = joined_terms[:tok_count]
    key_term = joined_terms[tok_count : 2 * tok_count]
    text_term = joined_terms[2 * tok_count :]
    query_gain = jnp.sum(projected[0] * saved["query_inv"][:, None] * query_n_grad, axis=0)
    key_gain = jnp.sum(projected[1] * saved["key_inv"][:, None] * key_n_grad, axis=0)
    text_gain = jnp.sum(text_proj[0] * saved["text_inv"][:, None] * text_n_grad, axis=0)
    self_proj_b = jnp.stack(
        [
            rms_back(
                projected[0],
                saved["query_inv"],
                gain_rows[0],
                query_n_grad,
                query_term,
                model_width,
            ),
            rms_back(
                projected[1], saved["key_inv"], gain_rows[1], key_n_grad, key_term, model_width
            ),
            value_grad.reshape(tok_count, local_width),
        ]
    ).astype(jnp.bfloat16)
    self_bias_grad = jnp.sum(self_proj_b.astype(jnp.float32), axis=1)
    self_weight_grad = jnp.einsum(
        "td,cth->cdh", saved["first_in"], self_proj_b, preferred_element_type=jnp.float32
    )
    first_grad = input_total(
        jnp.einsum("cth,cdh->td", self_proj_b, self_weight, preferred_element_type=jnp.float32)
    )
    unused_out, first_pull = jax.vjp(modulated, saved["hidden"], mod_terms[0], mod_terms[1])
    hidden_part, mod_zero, mod_one = first_pull(first_grad)
    grad = grad + hidden_part
    text_b = jnp.stack(
        [
            rms_back(
                text_proj[0], saved["text_inv"], gain_rows[3], text_n_grad, text_term, model_width
            ),
            text_value_grad.reshape(text_count, local_width),
        ]
    ).astype(jnp.bfloat16)
    text_bias_grad = jnp.sum(text_b.astype(jnp.float32), axis=1)
    text_weight_grad = jnp.einsum(
        "td,cth->cdh", context_rows, text_b, preferred_element_type=jnp.float32
    )
    context_part = jnp.einsum(
        "cth,cdh->td", text_b, cross_weight[1:3], preferred_element_type=jnp.float32
    )
    matrix_grads = (
        self_weight_grad,
        jnp.concatenate([cross_q_weight[None], text_weight_grad], axis=0),
        jnp.stack([self_out_grad, cross_out_grad]),
        up_grad,
        down_grad,
    )
    bias_grads = jnp.concatenate(
        [self_bias_grad[0:1], self_bias_grad[2:3], cross_bias_grad[None], text_bias_grad], axis=0
    )
    vector_grads = (
        bias_grads,
        self_bias_grad[1],
        jnp.stack([query_gain, key_gain, cross_gain_grad, text_gain]),
        up_bias_grad,
        jnp.stack([out_bias_zero, out_bias_one, out_bias_two]),
        norm_gain_grad,
        norm_shift_grad,
        jnp.stack([mod_zero, mod_one, mod_two, mod_three, mod_four, mod_five]),
    )
    return (grad, matrix_grads, vector_grads, context_part)


def per_device(
    latents,
    context,
    time_embed,
    teacher,
    lengths,
    block_order,
    positions,
    self_proj,
    cross_proj,
    out_proj,
    ffn_up,
    ffn_down,
    proj_bias,
    key_bias,
    norm_gains,
    ffn_bias,
    out_bias,
    cross_gain,
    cross_shift,
    modulation,
):
    tok_count, model_width = latents.shape
    clip_count = time_embed.shape[0]
    clip_index = lax.axis_index("dp") // HOLD
    seq_place = block_order[0] * tok_count + jnp.arange(tok_count, dtype=jnp.int32)
    clip_length = lax.dynamic_index_in_dim(lengths, clip_index, 0, keepdims=False)
    token_valid = (seq_place < clip_length).astype(jnp.float32)
    key_flags = token_valid.astype(jnp.bfloat16)
    time_row = lax.dynamic_index_in_dim(time_embed, clip_index, 0, keepdims=False)
    cosine, sine_rows = rope_angles(positions, HEAD_DIM)
    vector_args = (
        proj_bias,
        key_bias,
        norm_gains,
        ffn_bias,
        out_bias,
        cross_gain,
        cross_shift,
        modulation,
    )
    hidden = latents.astype(jnp.float32)
    saved_layers = []
    kept_layers = []
    for layer_index in range(LAYERS):
        gathered = (
            lax.all_gather(self_proj[layer_index], "dp", axis=1, tiled=True),
            lax.all_gather(cross_proj[layer_index], "dp", axis=1, tiled=True),
            lax.all_gather(out_proj[layer_index], "dp", axis=2, tiled=True),
            lax.all_gather(ffn_up[layer_index], "dp", axis=0, tiled=True),
            lax.all_gather(ffn_down[layer_index], "dp", axis=1, tiled=True),
        )
        vectors = tuple((item[layer_index] for item in vector_args))
        hidden, saved = forward_layer(
            hidden, gathered, vectors, time_row, key_flags, cosine, sine_rows, context, model_width
        )
        saved_layers.append(saved)
        kept_layers.append(None)
    error = hidden - teacher.astype(jnp.float32)
    sse_local = jnp.sum(token_valid[:, None] * error * error)
    grad = token_valid[:, None] * error
    context_sum = jnp.zeros(context.shape, jnp.float32)
    layer_results = [None] * LAYERS
    vector_layers = [None] * LAYERS
    for layer_index in reversed(range(LAYERS)):
        weights = (
            lax.all_gather(self_proj[layer_index], "dp", axis=1, tiled=True),
            lax.all_gather(cross_proj[layer_index], "dp", axis=1, tiled=True),
            lax.all_gather(out_proj[layer_index], "dp", axis=2, tiled=True),
            lax.all_gather(ffn_up[layer_index], "dp", axis=0, tiled=True),
            lax.all_gather(ffn_down[layer_index], "dp", axis=1, tiled=True),
        )
        vectors = tuple((item[layer_index] for item in vector_args))
        grad, matrix_grads, vector_grads, context_part = backward_layer(
            grad,
            saved_layers[layer_index],
            weights,
            vectors,
            time_row,
            cosine,
            sine_rows,
            context,
            model_width,
        )
        context_sum = context_sum + context_part
        vector_layers[layer_index] = vector_grads
        layer_results[layer_index] = (
            lax.psum_scatter(
                matrix_grads[0].astype(jnp.bfloat16), "dp", scatter_dimension=1, tiled=True
            ).astype(jnp.float32),
            lax.psum_scatter(
                matrix_grads[1].astype(jnp.bfloat16), "dp", scatter_dimension=1, tiled=True
            ).astype(jnp.float32),
            lax.psum_scatter(
                matrix_grads[2].astype(jnp.bfloat16), "dp", scatter_dimension=2, tiled=True
            ).astype(jnp.float32),
            lax.psum_scatter(
                matrix_grads[3].astype(jnp.bfloat16), "dp", scatter_dimension=0, tiled=True
            ).astype(jnp.float32),
            lax.psum_scatter(
                matrix_grads[4].astype(jnp.bfloat16), "dp", scatter_dimension=1, tiled=True
            ).astype(jnp.float32),
        )
    stacked = tuple(
        (
            jnp.stack([layer_results[layer_index][member] for layer_index in range(LAYERS)])
            for member in range(5)
        )
    )
    vector_stack = tuple(
        (
            jnp.stack([vector_layers[layer_index][member] for layer_index in range(LAYERS)])
            for member in range(8)
        )
    )
    clip_onehot = (jnp.arange(clip_count, dtype=jnp.int32) == clip_index).astype(jnp.float32)
    clip_mods = clip_onehot[None, :, None, None] * vector_stack[7][:, None, :, :]
    summed = (
        lax.psum(vector_stack[0].astype(jnp.bfloat16), "dp").astype(jnp.float32),
        lax.psum(vector_stack[1].astype(jnp.bfloat16), "dp").astype(jnp.float32),
        lax.psum(vector_stack[2].astype(jnp.bfloat16), "dp").astype(jnp.float32),
        lax.psum(vector_stack[3].astype(jnp.bfloat16), "dp").astype(jnp.float32),
        lax.psum(vector_stack[4].astype(jnp.bfloat16), "dp").astype(jnp.float32),
        lax.psum(vector_stack[5].astype(jnp.bfloat16), "dp").astype(jnp.float32),
        lax.psum(vector_stack[6].astype(jnp.bfloat16), "dp").astype(jnp.float32),
        lax.psum(clip_mods.astype(jnp.bfloat16), "dp").astype(jnp.float32),
        lax.psum(sse_local.astype(jnp.bfloat16), "dp").astype(jnp.float32),
    )
    context_grad = lax.psum(context_sum.astype(jnp.bfloat16), "tensor").astype(jnp.float32)
    loss = summed[8] / (jnp.sum(lengths).astype(jnp.float32) * model_width)
    time_grad = jnp.sum(summed[7], axis=0)
    modulation_grad = jnp.sum(summed[7], axis=1)
    return (
        hidden,
        loss,
        grad,
        context_grad,
        time_grad,
        stacked[0],
        stacked[1],
        stacked[2],
        stacked[3],
        stacked[4],
        summed[0],
        summed[1],
        summed[2],
        summed[3],
        summed[4],
        summed[5],
        summed[6],
        modulation_grad,
    )


def solution(mesh):
    return jax.shard_map(
        per_device,
        mesh=mesh,
        in_specs=(
            P("dp", None),
            P("dp", None),
            P(),
            P("dp", None),
            P(),
            P("dp"),
            P(None, "dp"),
            P(None, None, "dp", "tensor"),
            P(None, None, "dp", "tensor"),
            P(None, None, "tensor", "dp"),
            P(None, "dp", "tensor"),
            P(None, "tensor", "dp"),
            P(None, None, "tensor"),
            P(None, "tensor"),
            P(None, None, "tensor"),
            P(None, "tensor"),
            P(),
            P(),
            P(),
            P(),
        ),
        out_specs=(
            P("dp", None),
            P(),
            P("dp", None),
            P("dp", None),
            P(),
            P(None, None, "dp", "tensor"),
            P(None, None, "dp", "tensor"),
            P(None, None, "tensor", "dp"),
            P(None, "dp", "tensor"),
            P(None, "tensor", "dp"),
            P(None, None, "tensor"),
            P(None, "tensor"),
            P(None, None, "tensor"),
            P(None, "tensor"),
            P(),
            P(),
            P(),
            P(),
        ),
        check_vma=False,
    )
```

profile of v0, /device:TPU:8, one launch (start us, length us, event | category | flops | bytes accessed | tf_op | source)
XLA Modules:
  0.0 2377.9 jit_solution(16999783620081852477)
XLA Ops:
  18.3 27.4 %all-gather.23.cloned.1.call-done = bf16[1,3,1536,384]{3,2,1,0:T(8,128)(2,1)} async-done(((bf16[1,3,192,384]{3,2,1,0:T(8,128)(2,1)}), bf16[1,3,1536,384]{3,2,1,0:T(8,128)(2,1)}) %all-gather.23.cloned.1.call-update) | async-done | bytes 3538960 | tf_op jit(solution)/shard_map/all_gather | solution.py:534
  48.3 33.9 %all-gather.21.cloned.1.call-done = bf16[1,3,1536,384]{3,2,1,0:T(8,128)(2,1)} async-done(((bf16[1,3,192,384]{3,2,1,0:T(8,128)(2,1)}), bf16[1,3,1536,384]{3,2,1,0:T(8,128)(2,1)}) %all-gather.21.cloned.1.call-update) | async-done | bytes 3538960 | tf_op jit(solution)/shard_map/all_gather | solution.py:533
  112.6 15.5 collective-permute-done.3
  172.6 59.8 %all-reduce.19.cloned.1.call-done = bf16[512,1536]{1,0:T(8,128)(2,1)} async-done(((bf16[512,1536]{1,0:T(8,128)(2,1)}), bf16[512,1536]{1,0:T(8,128)(2,1)}) %all-reduce.19.cloned.1.call-update) | async-done | bytes 1572880 | tf_op jit(solution)/shard_map/psum | solution.py:107
  270.6 59.6 %all-reduce.21.cloned.1.call-done = bf16[512,1536]{1,0:T(8,128)(2,1)} async-done(((bf16[512,1536]{1,0:T(8,128)(2,1)}), bf16[512,1536]{1,0:T(8,128)(2,1)}) %all-reduce.21.cloned.1.call-update) | async-done | bytes 1572880 | tf_op jit(solution)/shard_map/psum | solution.py:107
  335.4 46.0 %all-gather.27.cloned.1.call-done = bf16[1,1536,2240]{2,1,0:T(8,128)(2,1)} async-done(((bf16[1,192,2240]{2,1,0:T(8,128)(2,1)}), bf16[1,1536,2240]{2,1,0:T(8,128)(2,1)}) %all-gather.27.cloned.1.call-update) | async-done | bytes 6881296 | tf_op jit(solution)/shard_map/all_gather | solution.py:536
  391.7 41.0 %all-gather.29.cloned.1.call-done = bf16[1,2240,1536]{1,2,0:T(8,128)(2,1)} async-done(((bf16[1,2240,192]{1,2,0:T(8,128)(2,1)}), bf16[1,2240,1536]{1,2,0:T(8,128)(2,1)}) %all-gather.29.cloned.1.call-update) | async-done | bytes 6881296 | tf_op jit(solution)/shard_map/all_gather | solution.py:537
  445.0 24.2 %all-gather.33.cloned.1.call-done = bf16[1,3,1536,384]{3,2,1,0:T(8,128)(2,1)} async-done(((bf16[1,3,192,384]{3,2,1,0:T(8,128)(2,1)}), bf16[1,3,1536,384]{3,2,1,0:T(8,128)(2,1)}) %all-gather.33.cloned.1.call-update) | async-done | bytes 3538960 | tf_op jit(solution)/shard_map/all_gather | solution.py:534
  473.6 66.8 %all-reduce.23.cloned.1.call-done = bf16[512,1536]{1,0:T(8,128)(2,1)} async-done(((bf16[512,1536]{1,0:T(8,128)(2,1)}), bf16[512,1536]{1,0:T(8,128)(2,1)}) %all-reduce.23.cloned.1.call-update) | async-done | bytes 1572880 | tf_op jit(solution)/shard_map/psum | solution.py:107
  545.7 30.4 %all-gather.31.cloned.1.call-done = bf16[1,3,1536,384]{3,2,1,0:T(8,128)(2,1)} async-done(((bf16[1,3,192,384]{3,2,1,0:T(8,128)(2,1)}), bf16[1,3,1536,384]{3,2,1,0:T(8,128)(2,1)}) %all-gather.31.cloned.1.call-update) | async-done | bytes 3538960 | tf_op jit(solution)/shard_map/all_gather | solution.py:533
  603.4 18.4 collective-permute-done.13
  657.6 62.7 %all-reduce.25.cloned.1.call-done = bf16[512,1536]{1,0:T(8,128)(2,1)} async-done(((bf16[512,1536]{1,0:T(8,128)(2,1)}), bf16[512,1536]{1,0:T(8,128)(2,1)}) %all-reduce.25.cloned.1.call-update) | async-done | bytes 1572880 | tf_op jit(solution)/shard_map/psum | solution.py:107
  751.5 66.3 %all-reduce.27.cloned.1.call-done = bf16[512,1536]{1,0:T(8,128)(2,1)} async-done(((bf16[512,1536]{1,0:T(8,128)(2,1)}), bf16[512,1536]{1,0:T(8,128)(2,1)}) %all-reduce.27.cloned.1.call-update) | async-done | bytes 1572880 | tf_op jit(solution)/shard_map/psum | solution.py:107
  823.1 45.9 %all-gather.37.cloned.1.call-done = bf16[1,1536,2240]{2,1,0:T(8,128)(2,1)} async-done(((bf16[1,192,2240]{2,1,0:T(8,128)(2,1)}), bf16[1,1536,2240]{2,1,0:T(8,128)(2,1)}) %all-gather.37.cloned.1.call-update) | async-done | bytes 6881296 | tf_op jit(solution)/shard_map/all_gather | solution.py:536
  879.2 41.0 %all-gather.39.cloned.1.call-done = bf16[1,2240,1536]{1,2,0:T(8,128)(2,1)} async-done(((bf16[1,2240,192]{1,2,0:T(8,128)(2,1)}), bf16[1,2240,1536]{1,2,0:T(8,128)(2,1)}) %all-gather.39.cloned.1.call-update) | async-done | bytes 6881296 | tf_op jit(solution)/shard_map/all_gather | solution.py:537
  931.7 66.8 %all-reduce.29.cloned.1.call-done = bf16[512,1536]{1,0:T(8,128)(2,1)} async-done(((bf16[512,1536]{1,0:T(8,128)(2,1)}), bf16[512,1536]{1,0:T(8,128)(2,1)}) %all-reduce.29.cloned.1.call-update) | async-done | bytes 1572880 | tf_op jit(solution)/shard_map/psum | solution.py:107
  1023.9 66.8 %all-reduce.31.cloned.1.call-done = bf16[512,1536]{1,0:T(8,128)(2,1)} async-done(((bf16[512,1536]{1,0:T(8,128)(2,1)}), bf16[512,1536]{1,0:T(8,128)(2,1)}) %all-reduce.31.cloned.1.call-update) | async-done | bytes 1572880 | tf_op jit(solution)/shard_map/psum | solution.py:111
  1150.8 48.8 %all-reduce.33.cloned.1.call-done = bf16[512,1536]{1,0:T(8,128)(2,1)} async-done(((bf16[512,1536]{1,0:T(8,128)(2,1)}), bf16[512,1536]{1,0:T(8,128)(2,1)}) %all-reduce.33.cloned.1.call-update) | async-done | bytes 1572880 | tf_op jit(solution)/shard_map/psum | solution.py:111
  1219.8 25.3 %fusion.173 = f32[2048,3,128]{2,0,1:T(8,128)S(1)} fusion(bf16[512,3,128]{2,0,1:T(8,128)(2,1)} %copy-done.332, f32[3,512,2048]{2,1,0:T(8,128)} %fusion.304, f32[3,512,2048]{2,1,0:T(8,128)} %copy-done.36, f32[3,512]{1,0:T(4,128)S(1)} %copy-done.295, pred[2048]{0:T(1024)(128)(4,1)S(1)} %copy-done.285), kind=kOutput, calls=%fused_computation.223 | convolution fusion | flops 839912960 | bytes 28712960 | tf_op jit(solution)/shard_map/hqk,qhd->khd/dot_general | solution.py:189
  1257.2 22.9 fusion.244
  1313.3 67.5 %all-reduce.35.cloned.1.call-done = bf16[512,1536]{1,0:T(8,128)(2,1)} async-done(((bf16[512,1536]{1,0:T(8,128)(2,1)}), bf16[512,1536]{1,0:T(8,128)(2,1)}) %all-reduce.35.cloned.1.call-update) | async-done | bytes 1572880 | tf_op jit(solution)/shard_map/psum | solution.py:111
  1425.0 51.8 %all-reduce.37.cloned.1.call-done = bf16[512,1536]{1,0:T(8,128)(2,1)} async-done(((bf16[512,1536]{1,0:T(8,128)(2,1)}), bf16[512,1536]{1,0:T(8,128)(2,1)}) %all-reduce.37.cloned.1.call-update) | async-done | bytes 1572880 | tf_op jit(solution)/shard_map/psum | solution.py:111
  1538.5 44.4 %all-reduce.39.cloned.1.call-done = bf16[512,1536]{1,0:T(8,128)(2,1)} async-done(((bf16[512,1536]{1,0:T(8,128)(2,1)}), bf16[512,1536]{1,0:T(8,128)(2,1)}) %all-reduce.39.cloned.1.call-update) | async-done | bytes 1572880 | tf_op jit(solution)/shard_map/psum | solution.py:111
  1603.4 26.6 %fusion.170 = f32[2048,3,128]{2,0,1:T(8,128)} fusion(bf16[512,3,128]{2,0,1:T(8,128)(2,1)S(1)} %copy-done.331, f32[3,512,2048]{2,1,0:T(8,128)} %fusion.306, f32[3,512,2048]{2,1,0:T(8,128)} %copy-done.35, f32[3,512]{1,0:T(4,128)S(1)} %copy-done.294, pred[2048]{0:T(1024)(128)(4,1)S(1)} %copy-done.286), kind=kOutput, calls=%fused_computation.222 | convolution fusion | flops 839912960 | bytes 28712960 | tf_op jit(solution)/shard_map/hqk,qhd->khd/dot_general | solution.py:189
  1642.7 21.5 fusion.241
  1929.3 27.3 %all-reduce.2 = (bf16[]{:T(256)}, bf16[2,5,384]{2,1,0:T(8,128)(2,1)}, bf16[2,3,1536]{2,1,0:T(4,128)(2,1)}, bf16[2,384]{1,0:T(2,128)(2,1)}, bf16[2,4,384]{2,1,0:T...) all-reduce(bf16[]{:T(256)} %get-tuple-element.101, ...), channel_id=1, replica_groups=mesh['dp'=8,'tensor'=4] {'dp'}, use_global_device_ids=true, to_apply=%region_39.40 | all-reduce | flops 27521 | bytes 110084 | tf_op jit(solution)/shard_map/psum | solution.py:613
  1990.9 46.1 %reduce-scatter.29.cloned.1.call-done = bf16[192,1152]{1,0:T(8,128)(2,1)} async-done(((bf16[1536,1152]{1,0:T(8,128)(2,1)}), bf16[192,1152]{1,0:T(8,128)(2,1)}) %reduce-scatter.29.cloned.1.call-update) | async-done | bytes 442384
  2042.8 46.5 %reduce-scatter.25.cloned.1.call-done = bf16[192,1152]{1,0:T(8,128)(2,1)} async-done(((bf16[1536,1152]{1,0:T(8,128)(2,1)}), bf16[192,1152]{1,0:T(8,128)(2,1)}) %reduce-scatter.25.cloned.1.call-update) | async-done | bytes 442384
  2095.2 63.6 %reduce-scatter.19.cloned.1.call-done = bf16[192,2240]{1,0:T(8,128)(2,1)} async-done(((bf16[1536,2240]{1,0:T(8,128)(2,1)}), bf16[192,2240]{1,0:T(8,128)(2,1)}) %reduce-scatter.19.cloned.1.call-update) | async-done | bytes 860176 | tf_op jit(solution)/shard_map/reduce_scatter | solution.py:583
  2158.8 69.0 %reduce-scatter.17.cloned.1.call-done = bf16[192,2240]{1,0:T(8,128)(2,1)} async-done(((bf16[1536,2240]{1,0:T(8,128)(2,1)}), bf16[192,2240]{1,0:T(8,128)(2,1)}) %reduce-scatter.17.cloned.1.call-update) | async-done | bytes 860176 | tf_op jit(solution)/shard_map/reduce_scatter | solution.py:583
  2231.3 65.8 %reduce-scatter.23.cloned.1.call-done = bf16[2240,192]{0,1:T(8,128)(2,1)} async-done(((bf16[2240,1536]{0,1:T(8,128)(2,1)}), bf16[2240,192]{0,1:T(8,128)(2,1)}) %reduce-scatter.23.cloned.1.call-update) | async-done | bytes 860176 | tf_op jit(solution)/shard_map/reduce_scatter | solution.py:586
  2297.1 69.0 %reduce-scatter.21.cloned.1.call-done = bf16[2240,192]{0,1:T(8,128)(2,1)} async-done(((bf16[2240,1536]{0,1:T(8,128)(2,1)}), bf16[2240,192]{0,1:T(8,128)(2,1)}) %reduce-scatter.21.cloned.1.call-update) | async-done | bytes 860176 | tf_op jit(solution)/shard_map/reduce_scatter | solution.py:586
  (1184 shorter events, 887.1 us)
Async XLA Ops:
  11.9 148.5 %all-gather.25.cloned.1.call-start = ((), (), s32[]{:S(2)}) async-start(), calls=%async_computation.25 | async-start | bytes 2654208 | tf_op jit(solution)/shard_map/all_gather | solution.py:535
  107.3 125.1 %all-reduce.19.cloned.1.call-start = ((), (), s32[]{:S(2)}) async-start(), calls=%async_computation.8 | async-start | bytes 3145728 | tf_op jit(solution)/shard_map/psum | solution.py:107
  164.0 166.3 %all-reduce.21.cloned.1.call-start = ((), (), s32[]{:S(2)}) async-start(), calls=%async_computation.9 | async-start | bytes 3145728 | tf_op jit(solution)/shard_map/psum | solution.py:107
  169.8 87.7 %collective-permute-start.7 = (bf16[256,3,128]{0,2,1:T(8,128)(2,1)}, bf16[256,3,128]{0,2,1:T(8,128)(2,1)}, u32[]{:S(2)}, u32[]{:S(2)}) collective-permute-start(bf16[256,3,128]{0,2,1:T(8,128)(2,1)} %pad_maximum_fusion.26), channel_id=1, source_target_pairs={{0,8},{8,0},{4,12},{12,4},{16,24},{24,16},{20,28},{28,20},{1,9},{9... | collective-permute-start | bytes 589832 | tf_op jit(solution)/shard_map/ppermute | solution.py:26
  262.7 118.7 %all-gather.27.cloned.1.call-start = ((), (), s32[]{:S(2)}) async-start(), calls=%async_computation.26 | async-start | bytes 7962624 | tf_op jit(solution)/shard_map/all_gather | solution.py:536
  265.5 167.2 %all-gather.29.cloned.1.call-start = ((), (), s32[]{:S(2)}) async-start(), calls=%async_computation.27 | async-start | bytes 7962624 | tf_op jit(solution)/shard_map/all_gather | solution.py:537
  268.4 200.8 %all-gather.33.cloned.1.call-start = ((), (), s32[]{:S(2)}) async-start(), calls=%async_computation.29 | async-start | bytes 3981312 | tf_op jit(solution)/shard_map/all_gather | solution.py:534
  269.1 271.3 %all-reduce.23.cloned.1.call-start = ((), (), s32[]{:S(2)}) async-start(), calls=%async_computation.10 | async-start | bytes 3145728 | tf_op jit(solution)/shard_map/psum | solution.py:107
  442.6 133.5 %all-gather.31.cloned.1.call-start = ((), (), s32[]{:S(2)}) async-start(), calls=%async_computation.28 | async-start | bytes 3981312 | tf_op jit(solution)/shard_map/all_gather | solution.py:533
  443.2 204.9 %all-gather.35.cloned.1.call-start = ((), (), s32[]{:S(2)}) async-start(), calls=%async_computation.30 | async-start | bytes 2654208 | tf_op jit(solution)/shard_map/all_gather | solution.py:535
  599.4 120.8 %all-reduce.25.cloned.1.call-start = ((), (), s32[]{:S(2)}) async-start(), calls=%async_computation.11 | async-start | bytes 3145728 | tf_op jit(solution)/shard_map/psum | solution.py:107
  651.7 166.1 %all-reduce.27.cloned.1.call-start = ((), (), s32[]{:S(2)}) async-start(), calls=%async_computation.12 | async-start | bytes 3145728 | tf_op jit(solution)/shard_map/psum | solution.py:107
  654.8 90.3 %collective-permute-start.15 = (bf16[256,3,128]{0,2,1:T(8,128)(2,1)}, bf16[256,3,128]{0,2,1:T(8,128)(2,1)}, u32[]{:S(2)}, u32[]{:S(2)}) collective-permute-start(bf16[256,3,128]{0,2,1:T(8,128)(2,1)} %pad_maximum_fusion.28), channel_id=1, source_target_pairs={{0,8},{8,0},{4,12},{12,4},{16,24},{24,16},{20,28},{28,20},{1,9},{9... | collective-permute-start | bytes 589832 | tf_op jit(solution)/shard_map/ppermute | solution.py:26
  657.0 85.1 %collective-permute-start.17 = (bf16[256,3,128]{2,0,1:T(8,128)(2,1)}, bf16[256,3,128]{2,0,1:T(8,128)(2,1)}, u32[]{:S(2)}, u32[]{:S(2)}) collective-permute-start(bf16[256,3,128]{2,0,1:T(8,128)(2,1)} %pad_maximum_fusion.29), channel_id=1, source_target_pairs={{0,8},{8,0},{4,12},{12,4},{16,24},{24,16},{20,28},{28,20},{1,9},{9... | collective-permute-start | bytes 589832 | tf_op jit(solution)/shard_map/ppermute | solution.py:26
  750.3 118.6 %all-gather.37.cloned.1.call-start = ((), (), s32[]{:S(2)}) async-start(), calls=%async_computation.31 | async-start | bytes 7962624 | tf_op jit(solution)/shard_map/all_gather | solution.py:536
  750.9 169.2 %all-gather.39.cloned.1.call-start = ((), (), s32[]{:S(2)}) async-start(), calls=%async_computation.32 | async-start | bytes 7962624 | tf_op jit(solution)/shard_map/all_gather | solution.py:537
  751.5 247.0 %all-reduce.29.cloned.1.call-start = ((), (), s32[]{:S(2)}) async-start(), calls=%async_computation.13 | async-start | bytes 3145728 | tf_op jit(solution)/shard_map/psum | solution.py:107
  930.0 160.6 %all-reduce.31.cloned.1.call-start = ((), (), s32[]{:S(2)}) async-start(), calls=%async_computation.14 | async-start | bytes 3145728 | tf_op jit(solution)/shard_map/psum | solution.py:111
  1022.3 177.3 %all-reduce.33.cloned.1.call-start = ((), (), s32[]{:S(2)}) async-start(), calls=%async_computation.15 | async-start | bytes 3145728 | tf_op jit(solution)/shard_map/psum | solution.py:111
  1132.1 248.7 %all-reduce.35.cloned.1.call-start = ((), (), s32[]{:S(2)}) async-start(), calls=%async_computation.16 | async-start | bytes 3145728 | tf_op jit(solution)/shard_map/psum | solution.py:111
  1313.2 163.6 %all-reduce.37.cloned.1.call-start = ((), (), s32[]{:S(2)}) async-start(), calls=%async_computation.17 | async-start | bytes 3145728 | tf_op jit(solution)/shard_map/psum | solution.py:111
  1408.5 174.4 %all-reduce.39.cloned.1.call-start = ((), (), s32[]{:S(2)}) async-start(), calls=%async_computation.18 | async-start | bytes 3145728 | tf_op jit(solution)/shard_map/psum | solution.py:111
  1515.4 272.2 %all-reduce.43.cloned.1.call-start = ((), (), s32[]{:S(2)}) async-start(), calls=%async_computation.38 | async-start | bytes 3932160 | tf_op jit(solution)/shard_map/psum | solution.py:111
  1707.1 204.9 %reduce-scatter.27.cloned.1.call-start = ((), (), s32[]{:S(2)}) async-start(), calls=%async_computation.34 | async-start | bytes 3981312
  1726.1 190.3 %reduce-scatter.31.cloned.1.call-start = ((), (), s32[]{:S(2)}) async-start(), calls=%async_computation.36 | async-start | bytes 3981312
  1748.9 236.2 %all-reduce.41.cloned.1.call-start = ((), (), s32[]{:S(2)}) async-start(), calls=%async_computation.37 | async-start | bytes 9584640 | tf_op jit(solution)/shard_map/psum | solution.py:612
  1797.1 239.8 %reduce-scatter.29.cloned.1.call-start = ((), (), s32[]{:S(2)}) async-start(), calls=%async_computation.35 | async-start | bytes 3981312
  1818.8 270.5 %reduce-scatter.25.cloned.1.call-start = ((), (), s32[]{:S(2)}) async-start(), calls=%async_computation.33 | async-start | bytes 3981312
  1837.1 321.7 %reduce-scatter.19.cloned.1.call-start = ((), (), s32[]{:S(2)}) async-start(), calls=%async_computation.20 | async-start | bytes 7962624 | tf_op jit(solution)/shard_map/reduce_scatter | solution.py:583
  1847.5 380.3 %reduce-scatter.17.cloned.1.call-start = ((), (), s32[]{:S(2)}) async-start(), calls=%async_computation.19 | async-start | bytes 7962624 | tf_op jit(solution)/shard_map/reduce_scatter | solution.py:583
  1858.4 438.7 %reduce-scatter.23.cloned.1.call-start = ((), (), s32[]{:S(2)}) async-start(), calls=%async_computation.22 | async-start | bytes 7962624 | tf_op jit(solution)/shard_map/reduce_scatter | solution.py:586
  1869.0 497.2 %reduce-scatter.21.cloned.1.call-start = ((), (), s32[]{:S(2)}) async-start(), calls=%async_computation.21 | async-start | bytes 7962624 | tf_op jit(solution)/shard_map/reduce_scatter | solution.py:586
  (375 other events, 6114.2 us)
Sparse Core Ops, SparseCore 0:
  10.6 35.1 all-gather.22
  48.2 33.9 all-gather.20
  107.4 34.3 all-gather.24
  164.1 68.2 all-reduce.18
  262.8 67.3 all-reduce.20
  332.6 48.7 all-gather.26
  383.8 48.8 all-gather.28
  435.2 33.9 all-gather.32
  472.1 68.2 all-reduce.22
  542.2 33.8 all-gather.30
  599.5 38.4 all-gather.34
  651.8 68.3 all-reduce.24
  750.5 67.3 all-reduce.26
  820.2 48.7 all-gather.36
  871.3 48.8 all-gather.38
  930.1 68.2 all-reduce.28
  1022.4 68.1 all-reduce.30
  1132.2 67.3 all-reduce.32
  1313.3 67.4 all-reduce.34
  1408.6 68.1 all-reduce.36
  1515.5 67.3 all-reduce.38
  1707.2 80.2 all-reduce.42
  1791.6 48.2 reduce-scatter.26
  1843.3 48.0 reduce-scatter.30
  1895.6 89.3 all-reduce.40
  1988.8 48.0 reduce-scatter.28
  2041.2 48.0 reduce-scatter.24
  2093.3 65.4 reduce-scatter.18
  2162.3 65.4 reduce-scatter.16
  2231.6 65.4 reduce-scatter.22
  2300.7 65.4 reduce-scatter.20
where the time goes:
time: 2390 us; the launch traced here: 2380 us
  waiting for transfers between devices  1410 us (59%)
  matrix products  388 us (16%)
  local copies, waits for them, and re-layouts  225 us (9%)
  other arithmetic  205 us (9%)
  blocking collectives  106 us (4%)
  starting transfers between devices  26 us (1%)
    psum x6, waiting for transfers between devices, head_total(): lax.psum(partial_rows.astype(jnp.bfloat16), 'tensor').astype(jnp.float32)  382 us
    psum x6, waiting for transfers between devices, input_total(): lax.psum(partial_rows.astype(jnp.bfloat16), 'tensor').astype(jnp.float32)  280 us
    reduce_scatter x2, waiting for transfers between devices, per_device(): lax.psum_scatter(matrix_grads[4].astype(jnp.bfloat16), 'dp', scatter_dime...  135 us
    reduce_scatter x2, waiting for transfers between devices, per_device(): lax.psum_scatter(matrix_grads[3].astype(jnp.bfloat16), 'dp', scatter_dime...  133 us
    unnamed x711, local copies, waits for them, and re-layouts  126 us
    unnamed x35, waiting for transfers between devices  95.3 us
    all_gather x2, waiting for transfers between devices, per_device(): lax.all_gather(ffn_up[layer_index], 'dp', axis=0, tiled=True)  91.8 us
    all_gather x2, waiting for transfers between devices, per_device(): lax.all_gather(ffn_down[layer_index], 'dp', axis=1, tiled=True)  82 us
  transfers between devices with their start and end apart: 65, of which 39 were waited for; matrix products, arithmetic and copies ran while one was open for 22% of the time, Pallas kernels for 0%

commit v1 on v0

v1 whole, which is shorter than its diff:
```python
import functools
import math

import jax
import jax.numpy as jnp
import numpy as np
from jax import lax
from jax.experimental import pallas as pl
from jax.experimental.pallas import tpu as pltpu
from jax.sharding import PartitionSpec as P

MESH = pl.DeviceIdType.MESH
F32, BF16 = jnp.float32, jnp.bfloat16
NN = (((1,), (0,)), ((), ()))
NT = (((1,), (1,)), ((), ()))
TN = (((0,), (0,)), ((), ()))
HEAD_DIM = 128
HOLD = 4
LAYERS = 2
CHAIN = 4
CHUNK = 32
EPS = 1e-06
LOG2E = math.log2(math.e)
SCALE = 1.0 / math.sqrt(HEAD_DIM)
VMEM_BYTES = 60 * 2**20


def dot(left, right, dims=NN, exact=False):
    precision = lax.Precision.HIGHEST if exact else None
    return lax.dot_general(left, right, dims, precision=precision, preferred_element_type=F32)


def rope_table(head_size):
    third = head_size // 6
    spans = [head_size - 4 * third, 2 * third, 2 * third]
    table = np.zeros((3, head_size), np.float32)
    start_col = 0
    for component in range(3):
        for pair_index in range(spans[component] // 2):
            freq_value = 10000.0 ** (-(2.0 * pair_index) / spans[component])
            table[component, start_col + 2 * pair_index] = freq_value
            table[component, start_col + 2 * pair_index + 1] = freq_value
        start_col += spans[component]
    return table


def rope_angles(positions, head_size):
    table = rope_table(head_size)
    places = positions.astype(F32)
    angles = (
        places[0][:, None] * table[0][None, :]
        + places[1][:, None] * table[1][None, :]
        + places[2][:, None] * table[2][None, :]
    )
    return (jnp.cos(angles), jnp.sin(angles))


def signal(**device):
    pl.semaphore_signal(
        pltpu.get_barrier_semaphore(), inc=1, device_id=device, device_id_type=MESH
    )


def bits_of_dp():
    return max(lax.axis_size("dp").bit_length() - 1, 1)


def flip(index, mask):
    result, bit = index, 0
    while mask >> bit:
        if mask >> bit & 1:
            half = 1 << bit
            result = result + half - 2 * half * lax.rem(index // half, 2)
        bit += 1
    return result


def greet(tensor, masks):
    place, me = lax.axis_index("tensor"), lax.axis_index("dp")
    if tensor:
        for step in range(1, CHAIN):
            signal(tensor=lax.rem(place + step, CHAIN))
    for mask in masks:
        signal(dp=flip(me, mask))
    pl.semaphore_wait(
        pltpu.get_barrier_semaphore(), (CHAIN - 1 if tensor else 0) + len(masks)
    )


def holders():
    me = lax.axis_index("dp")
    return flip(me, 1), flip(me, 2)


def send(src, dst, send_sem, recv_sem, **device):
    return pltpu.make_async_remote_copy(
        src_ref=src,
        dst_ref=dst,
        send_sem=send_sem,
        recv_sem=recv_sem,
        device_id=device,
        device_id_type=MESH,
    )


def masks_over(bits):
    masks = [0]
    for bit in bits:
        masks += [mask | 1 << bit for mask in masks]
    return masks


def halves_of(size):
    cut = (size // 2 + 15) // 16 * 16
    return ((0, cut), (cut, size - cut))


def half_orders(bits):
    rising = list(range(1, bits))
    return (rising, rising[::-1])


class Gather:
    def __init__(self, source, layer):
        self.layer = layer
        self.operands = [source]
        shape = source.shape[1:]
        self.lead = shape[:-2]
        self.size = shape[-2]
        devices = lax.axis_size("dp")
        self.outs = [(self.lead + (self.size * devices, shape[-1]), source.dtype)]
        self.spaces = [pl.ANY]
        self.bits = bits_of_dp()
        plan = []
        for half, order in enumerate(half_orders(self.bits)):
            for phase, bit in enumerate(order):
                for mask in masks_over(order[:phase]):
                    plan.append((phase, half, bit, mask))
        for mask in masks_over(range(1, self.bits)):
            plan.append((self.bits - 1, None, 0, mask))
        self.plan = plan
        count = len(plan)
        self.scratch = [
            pltpu.SemaphoreType.DMA((count,)),
            pltpu.SemaphoreType.DMA((count,)),
            pltpu.SemaphoreType.DMA,
        ]

    def key(self):
        return ("gather", self.layer, self.outs[0][0])

    def bind(self, sources, outs, scratch):
        self.source = sources[0].at[self.layer]
        self.out = outs[0]
        self.send_sems, self.recv_sems, self.own_sem = scratch

    def block(self, ref, index, half):
        low, size = (0, self.size) if half is None else halves_of(self.size)[half]
        start = low if index is None else index * self.size + low
        rows = pl.ds(pl.multiple_of(start, 16), size)
        return ref.at[:, rows] if self.lead else ref.at[rows]

    def copies(self, phase, own=None):
        me = lax.axis_index("dp")
        for number, (step, half, bit, mask) in enumerate(self.plan):
            if step == phase and own in (None, mask == 0):
                index = flip(me, mask)
                source = (
                    self.block(self.source, None, half)
                    if mask == 0
                    else self.block(self.out, index, half)
                )
                yield send(
                    source,
                    self.block(self.out, index, half),
                    self.send_sems.at[number],
                    self.recv_sems.at[number],
                    dp=flip(me, 1 << bit),
                )

    def own_copy(self):
        me = lax.axis_index("dp")
        return pltpu.make_async_copy(
            self.source, self.block(self.out, me, None), self.own_sem
        )

    def start(self):
        for phase in range(self.bits):
            for copy in self.copies(phase, True):
                copy.start()
        self.own_copy().start()

    def advance(self, phase):
        for copy in self.copies(phase - 1):
            copy.wait_recv()
        for copy in self.copies(phase, False):
            copy.start()

    def finish(self):
        for copy in self.copies(self.bits - 1):
            copy.wait_recv()
        for phase in range(self.bits):
            for copy in self.copies(phase):
                copy.wait_send()
        self.own_copy().wait()


class Scatter:
    def __init__(self, source):
        self.operands = [source]
        self.bits = bits_of_dp()
        self.size = source.shape[0] // lax.axis_size("dp")
        self.width = source.shape[1]
        self.outs = [((self.size, self.width), F32)]
        self.spaces = [pltpu.VMEM]
        self.slots = 1 << self.bits - 1
        orders = [order[::-1] for order in half_orders(self.bits)]
        plan = [(0, None, 0, mask, mask >> 1) for mask in masks_over(range(1, self.bits))]
        for half, order in enumerate(orders):
            for phase, bit in enumerate(order):
                kept = masks_over(order[phase + 1 :])
                for place, mask in enumerate(kept):
                    plan.append((phase + 1, half, bit, mask, place))
        self.plan = plan
        count = len(plan)
        buffers = [pltpu.VMEM((self.slots, self.size, self.width), BF16)] * 2
        for phase in range(1, self.bits):
            places = 1 << self.bits - 1 - phase
            buffers += [
                pltpu.VMEM((places, size, self.width), BF16)
                for _, size in halves_of(self.size)
            ]
        self.scratch = buffers + [
            pltpu.SemaphoreType.DMA((count,)),
            pltpu.SemaphoreType.DMA((count,)),
            pltpu.SemaphoreType.DMA((self.slots,)),
        ]

    def key(self):
        return ("scatter", self.width)

    def bind(self, sources, outs, scratch):
        self.source, self.out = sources[0], outs[0]
        self.held, self.landed = scratch[:2]
        self.parts = scratch[2:-3]
        self.send_sems, self.recv_sems, self.own_sems = scratch[-3:]

    def rows(self, index):
        return pl.ds(pl.multiple_of(index * self.size, 16), self.size)

    def copies(self, phase):
        me = lax.axis_index("dp")
        for number, (step, half, bit, mask, place) in enumerate(self.plan):
            if step != phase:
                continue
            if phase == 0:
                source = self.source.at[self.rows(flip(me, mask | 1))]
                target = self.landed.at[mask >> 1]
            else:
                low, size = halves_of(self.size)[half]
                source = self.held.at[(mask | 1 << bit) >> 1, pl.ds(low, size)]
                target = self.parts[2 * (phase - 1) + half].at[place]
            yield send(
                source,
                target,
                self.send_sems.at[number],
                self.recv_sems.at[number],
                dp=flip(me, 1 << bit),
            )

    def own_copies(self):
        me = lax.axis_index("dp")
        for slot in range(self.slots):
            yield pltpu.make_async_copy(
                self.source.at[self.rows(flip(me, slot << 1))],
                self.held.at[slot],
                self.own_sems.at[slot],
            )

    def start(self):
        for copy in self.copies(0):
            copy.start()
        for copy in self.own_copies():
            copy.start()

    def add(self, phase):
        for copy in self.copies(phase):
            copy.wait_recv()
        if phase == 0:
            for copy in self.own_copies():
                copy.wait()
            for slot in range(self.slots):

                def step(rows, index, slot=slot):
                    self.held[slot, rows] = self.held[slot, rows] + self.landed[slot, rows]

                loop_rows(self.size, 16, step)
            return
        for number, (step, half, bit, mask, place) in enumerate(self.plan):
            if step == phase:
                low, size = halves_of(self.size)[half]
                part = self.parts[2 * (phase - 1) + half]

                def step(index, carry, mask=mask, place=place, low=low, part=part):
                    near = pl.ds(pl.multiple_of(index * 16, 16), 16)
                    rows = pl.ds(pl.multiple_of(low + index * 16, 16), 16)
                    if phase == self.bits - 1:
                        self.out[rows] = self.held[0, rows].astype(F32) + part[place, near].astype(
                            F32
                        )
                    else:
                        self.held[mask >> 1, rows] = (
                            self.held[mask >> 1, rows] + part[place, near]
                        )
                    return carry

                lax.fori_loop(0, size // 16, step, 0)

    def advance(self, phase):
        self.add(phase - 1)
        for copy in self.copies(phase):
            copy.start()

    def finish(self):
        self.add(self.bits - 1)
        for phase in range(self.bits):
            for copy in self.copies(phase):
                copy.wait_send()


class Side:
    def __init__(self, jobs):
        self.jobs = jobs
        self.masks = [1 << bit for bit in range(bits_of_dp())] if jobs else []

    def start(self):
        for job in self.jobs:
            job.start()

    def early(self):
        for phase in range(1, bits_of_dp() - 1):
            for job in self.jobs:
                job.advance(phase)

    def early_first(self):
        if bits_of_dp() > 2:
            for job in self.jobs:
                job.advance(1)

    def early_rest(self):
        for phase in range(2, bits_of_dp() - 1):
            for job in self.jobs:
                job.advance(phase)

    def late(self):
        for job in self.jobs:
            job.advance(bits_of_dp() - 1)

    def finish(self):
        for job in self.jobs:
            job.finish()


class Exchange:
    def __init__(self, slots, send_sems, recv_sems):
        self.slots = slots
        place = lax.axis_index("tensor")
        self.place = place
        self.copies = [
            send(
                slots.at[place],
                slots.at[place],
                send_sems.at[step - 1],
                recv_sems.at[step - 1],
                tensor=lax.rem(place + step, CHAIN),
            )
            for step in range(1, CHAIN)
        ]

    def start(self, rows):
        self.slots[self.place] = rows
        for copy in self.copies:
            copy.start()

    def finish(self):
        for copy in self.copies:
            copy.wait()


def stat_rows(squares, row):
    count, width = squares.shape
    ones = jnp.ones((8, width), F32)
    sums = dot(ones, squares, NT, exact=True)
    index = lax.broadcasted_iota(jnp.int32, sums.shape, 0)
    return jnp.where(index == row, sums, 0.0)


def stat_column(slots, row, lanes):
    gathered = jnp.concatenate([slots[place] for place in range(CHAIN)], axis=0)
    index = lax.broadcasted_iota(jnp.int32, (8 * CHAIN, lanes), 0)
    pick = jnp.where(lax.rem(index, 8) == row, 1.0, 0.0)
    return dot(gathered, pick, TN, exact=True)


class Chain:
    def __init__(self, part, total, buffers, sems):
        self.part, self.total = part, total
        self.came, self.pair, self.peers = buffers
        self.sems = sems
        place = lax.axis_index("tensor")
        self.is_end = (place == 0) | (place == 3)
        self.is_mid = jnp.logical_not(self.is_end)
        self.inner = jnp.where(place == 0, 1, 2)
        self.outer = jnp.where(place == 1, 0, 3)
        self.peer = 3 - place
        self.chunks = part.shape[0] // CHUNK

    @staticmethod
    def scratch(rows, width):
        chunks = rows // CHUNK
        return [pltpu.VMEM((rows, width), BF16)] * 4 + [pltpu.SemaphoreType.DMA((6, chunks))]

    def rows(self, k):
        return pl.ds(pl.multiple_of(k * CHUNK, CHUNK), CHUNK)

    def copy(self, src, dst, kind, k, device):
        return send(
            src.at[self.rows(k)],
            dst.at[self.rows(k)],
            self.sems.at[2 * kind, k],
            self.sems.at[2 * kind + 1, k],
            tensor=device,
        )

    def inward(self, k, device):
        return self.copy(self.part, self.came, 0, k, device)

    def across(self, k):
        return self.copy(self.pair, self.peers, 1, k, self.peer)

    def outward(self, k, device):
        return self.copy(self.total, self.total, 2, k, device)

    def begin(self, low, count):
        @pl.when(self.is_end)
        def _():
            def step(k, carry):
                self.inward(low + k, self.inner).start()
                return carry

            lax.fori_loop(0, count, step, 0)

    def first(self, k):
        self.inward(k, self.outer).wait_recv()
        rows = self.rows(k)
        self.pair[rows] = (self.part[rows].astype(F32) + self.came[rows].astype(F32)).astype(BF16)
        self.across(k).start()

    def second(self, k):
        self.across(k).wait_recv()
        rows = self.rows(k)
        self.total[rows] = (self.pair[rows].astype(F32) + self.peers[rows].astype(F32)).astype(
            BF16
        )
        self.outward(k, self.outer).start()

    def serve(self, k):
        @pl.when(self.is_mid)
        def _():
            self.first(k)

            @pl.when(k > 0)
            def _():
                self.second(jnp.maximum(k - 1, 0))

    def segment(self, low, high, closed, upto):
        @pl.when(self.is_mid)
        def _():
            def both(k, carry):
                self.first(k)

                @pl.when(k > 0)
                def _():
                    self.second(jnp.maximum(k - 1, 0))

                return carry

            lax.fori_loop(low, high, both, 0)
            if high == self.chunks:
                self.second(self.chunks - 1)

        @pl.when(self.is_end)
        def _():
            def close(k, carry):
                self.inward(k, self.inner).wait_send()
                self.outward(k, self.inner).wait_recv()
                return carry

            lax.fori_loop(closed, upto, close, 0)

    def drain(self, low, early=None, late=None):
        done, last = 0, self.chunks
        if early is not None:
            cut = low + (last - low) // 4
            self.segment(low, cut, done, cut - 1)
            low, done = cut, cut - 1
            early()
        if late is not None:
            cut = low + (last - low) * 5 // 8
            self.segment(low, cut, done, cut - 1)
            low, done = cut, cut - 1
            late()
        self.segment(low, last, done, last)

        @pl.when(self.is_mid)
        def _():
            def close(k, carry):
                self.across(k).wait_send()
                self.outward(k, self.outer).wait_send()
                return carry

            lax.fori_loop(0, self.chunks, close, 0)


COLLECTIVES = {}


def collective_of(key):
    return COLLECTIVES.setdefault(key, 1 + len(COLLECTIVES))


def run(name, kernel, ins, outs, scratch=(), remote=True, jobs=(), scalars=0, micros=0):
    whole = pl.BlockSpec(memory_space=pltpu.VMEM)
    far = pl.BlockSpec(memory_space=pl.ANY)
    job_ins = [item for job in jobs for item in job.operands]
    job_outs = [item for job in jobs for item in job.outs]
    job_spaces = [pl.BlockSpec(memory_space=space) for job in jobs for space in job.spaces]
    job_scratch = [item for job in jobs for item in job.scratch]
    side = Side(jobs)

    def body(*refs):
        refs = list(refs)

        def take(count):
            taken = refs[:count]
            del refs[:count]
            return taken

        own_in, side_in = take(len(ins)), take(len(job_ins))
        own_out, side_out = take(len(outs)), take(len(job_outs))
        own_scratch = take(len(scratch))
        for job in jobs:
            job.bind(
                [side_in.pop(0) for _ in job.operands],
                [side_out.pop(0) for _ in job.outs],
                take(len(job.scratch)),
            )
        kernel(side, *own_in, *own_out, *own_scratch)

    key = (name,) + tuple(job.key() for job in jobs)
    results = pl.pallas_call(
        body,
        out_shape=tuple(jax.ShapeDtypeStruct(shape, kind) for shape, kind in outs + tuple(job_outs)),
        in_specs=[pl.BlockSpec(memory_space=pltpu.SMEM)] * scalars
        + [whole] * (len(ins) - scalars)
        + [far] * len(job_ins),
        out_specs=tuple([whole] * len(outs) + job_spaces),
        scratch_shapes=list(scratch) + job_scratch,
        cost_estimate=pl.CostEstimate(
            flops=0, bytes_accessed=micros * 3000000, transcendentals=0
        ),
        compiler_params=pltpu.CompilerParams(
            collective_id=collective_of(key) if remote else None,
            has_side_effects=remote,
            vmem_limit_bytes=VMEM_BYTES,
        ),
    )(*ins, *job_ins)
    return results[: len(outs)], results[len(outs) :]


def normed(hidden):
    center = hidden - jnp.mean(hidden, axis=-1, keepdims=True)
    inverse = lax.rsqrt(jnp.mean(center * center, axis=-1, keepdims=True) + EPS)
    return center * inverse, inverse


def norm_back(hidden, scale_row, grad):
    hat, inverse = normed(hidden)
    inner = grad * scale_row
    back = inverse * (
        inner
        - jnp.mean(inner, axis=-1, keepdims=True)
        - hat * jnp.mean(inner * hat, axis=-1, keepdims=True)
    )
    return back, hat


def loop_rows(total, size, body):
    def step(index, carry):
        body(pl.ds(pl.multiple_of(index * size, size), size), index)
        return carry

    lax.fori_loop(0, total // size, step, 0)


def add_sum(ref, row, block):
    ref[row : row + 1] += jnp.sum(block, axis=0, keepdims=True)


def turned(rows):
    lane = lax.broadcasted_iota(jnp.int32, rows.shape, 1)
    width = rows.shape[1]
    return jnp.where(
        lax.rem(lane, 2) == 0, -pltpu.roll(rows, width - 1, 1), pltpu.roll(rows, 1, 1)
    )


def head_cols(head):
    return slice(head * HEAD_DIM, (head + 1) * HEAD_DIM)


def inverse_rms(sums, features):
    return lax.rsqrt(sums / features + EPS)


MODS, OUT_BIAS, CROSS_GAIN, CROSS_SHIFT = 0, 6, 9, 10
KEY_BIAS, GAINS = 5, 6


def row_of(ref, index):
    return ref[index : index + 1]


def entry_kernel(
    side,
    lengths,
    block_order,
    time_embed,
    modulation,
    out_bias,
    cross_gain,
    cross_shift,
    proj_bias,
    key_bias,
    norm_gains,
    ffn_bias,
    counts,
    *rest,
):
    packs, (send_sems, recv_sems) = rest[:-2], rest[-2:]
    greet(False, side.masks)
    near, far = holders()
    tokens = counts.shape[2]
    clip = lax.axis_index("dp") // HOLD
    mine = (lengths[clip] - block_order[0] * tokens).astype(F32)
    counts[0] = jnp.full(counts.shape[1:], mine, F32)

    def copy(number, source, target, device):
        return send(
            counts.at[source],
            counts.at[target],
            send_sems.at[number],
            recv_sems.at[number],
            dp=device,
        )

    to_near, to_far, onward = copy(0, 0, 1, near), copy(1, 0, 2, far), copy(2, 2, 3, near)
    side.start()
    to_near.start()
    to_far.start()
    for layer in range(LAYERS):
        rows_d, rows_w, rows_f = packs[3 * layer : 3 * layer + 3]
        rows_d[...] = jnp.zeros(rows_d.shape, F32)
        rows_w[...] = jnp.zeros(rows_w.shape, F32)
        rows_d[MODS : MODS + 6] = modulation[layer] + time_embed[clip]
        rows_d[OUT_BIAS : OUT_BIAS + 3] = out_bias[layer]
        rows_d[CROSS_GAIN : CROSS_GAIN + 1] = row_of(cross_gain, layer)
        rows_d[CROSS_SHIFT : CROSS_SHIFT + 1] = row_of(cross_shift, layer)
        rows_w[0:5] = proj_bias[layer]
        rows_w[KEY_BIAS : KEY_BIAS + 1] = row_of(key_bias, layer)
        rows_w[GAINS : GAINS + 4] = norm_gains[layer]
        rows_f[...] = row_of(ffn_bias, layer)
    to_far.wait_recv()
    onward.start()
    side.early()
    side.late()
    to_near.wait_recv()
    onward.wait_recv()
    for copy in (to_near, to_far, onward):
        copy.wait_send()
    side.finish()


def add_branch(base, tot, bias_row, gate_row):
    return base + (tot.astype(F32) + bias_row) * gate_row


def qkv_kernel(
    first,
    side,
    base,
    tot,
    rows_before,
    rows_d,
    rows_w,
    weight,
    cosine,
    sine,
    hidden,
    normal,
    query,
    key,
    query_rot,
    key_value,
    slots,
    send_sems,
    recv_sems,
):
    greet(True, side.masks)
    side.start()
    tokens, width = query.shape
    features = hidden.shape[1]
    heads = width // HEAD_DIM
    scale_row = 1.0 + row_of(rows_d, MODS + 1)
    shift_row = row_of(rows_d, MODS)

    def project(rows, index):
        if first:
            block = base[rows].astype(F32)
        else:
            block = add_branch(
                base[rows], tot[rows], row_of(rows_before, OUT_BIAS + 2), row_of(rows_before, MODS + 5)
            )
        hidden[rows] = block
        block = (normed(block)[0] * scale_row + shift_row).astype(BF16)
        normal[rows] = block
        query[rows] = dot(block, weight[0]) + row_of(rows_w, 0)
        key[rows] = dot(block, weight[1]) + row_of(rows_w, KEY_BIAS)
        value = (dot(block, weight[2]) + row_of(rows_w, 1)).astype(BF16)
        for head in range(heads):
            key_value[head, 1, rows] = value[:, head_cols(head)]

    loop_rows(tokens, 256, project)
    exchange = Exchange(slots, send_sems, recv_sems)
    exchange.start(
        stat_rows(query[...] * query[...], 0) + stat_rows(key[...] * key[...], 1)
    )
    side.early()
    exchange.finish()
    query_inv = inverse_rms(stat_column(slots, 0, HEAD_DIM), features)
    key_inv = inverse_rms(stat_column(slots, 1, HEAD_DIM), features)
    for head in range(heads):
        cols = head_cols(head)
        rows = query[:, cols] * query_inv * rows_w[GAINS : GAINS + 1, cols]
        query_rot[:, cols] = (rows * cosine[...] + turned(rows) * sine[...]).astype(BF16)
        rows = key[:, cols] * key_inv * rows_w[GAINS + 1 : GAINS + 2, cols]
        key_value[head, 0] = (rows * cosine[...] + turned(rows) * sine[...]).astype(BF16)
    side.late()
    side.finish()


def below(counts, slot, shape):
    index = lax.broadcasted_iota(jnp.int32, shape, 0).astype(F32)
    return index < counts[slot, 0:1]


def softmax_back(scores, lse_row, mask):
    probs = jnp.exp2(scores * (SCALE * LOG2E) - lse_row)
    return probs if mask is None else jnp.where(mask, probs, 0.0)


def attend_kernel(with_context, side, counts, query, key_value, *refs):
    refs = list(refs)
    context = refs.pop(0) if with_context else None
    others, result, lse = refs[:3]
    clip_context = refs[3] if with_context else None
    scores, send_sems, recv_sems = refs[-3:]
    greet(False, [1, 2])
    near, far = holders()
    tokens, width = query.shape
    heads = width // HEAD_DIM

    def copy(source, target, number, device):
        return send(source, target, send_sems.at[number], recv_sems.at[number], dp=device)

    to_near = copy(key_value, others.at[0], 0, near)
    to_far = [
        copy(key_value.at[head], others.at[1, head], 1 + head, far) for head in range(heads)
    ]
    onward = [
        copy(others.at[1, head], others.at[2, head], 1 + heads + head, near)
        for head in range(heads)
    ]
    for item in to_far:
        item.start()
    to_near.start()
    text = []
    if with_context:
        place = lax.rem(lax.axis_index("dp"), HOLD)
        size = context.shape[0]

        def block(index):
            return clip_context.at[pl.ds(pl.multiple_of(index * size, 16), size)]

        low = 1 + 2 * heads
        clip_context[pl.ds(pl.multiple_of(place * size, 16), size)] = context[...]
        text = [
            copy(block(place), block(place), low, near),
            copy(block(place), block(place), low + 1, far),
            copy(block(flip(place, 2)), block(flip(place, 2)), low + 2, near),
        ]
        text[0].start()
        text[1].start()

    def score(head, slot, keys):
        block = dot(keys, query[:, head_cols(head)], NT) * (SCALE * LOG2E)
        scores[head, slot] = jnp.where(below(counts, slot, block.shape), block, -1e30)

    for head in range(heads):
        score(head, 0, key_value[head, 0])
    to_near.wait_recv()
    for head in range(heads):
        score(head, 1, others[0, head, 0])
    lse[...] = jnp.zeros(lse.shape, F32)
    for head in range(heads):
        to_far[head].wait_recv()
        onward[head].start()
        score(head, 2, others[1, head, 0])
        onward[head].wait_recv()
        score(head, 3, others[2, head, 0])
        top = jnp.max(scores[head, 0], axis=0, keepdims=True)
        for slot in range(1, HOLD):
            top = jnp.maximum(top, jnp.max(scores[head, slot], axis=0, keepdims=True))
        total = jnp.zeros_like(top)
        summed = jnp.zeros((HEAD_DIM, tokens), F32)
        for slot in range(HOLD):
            values = key_value[head, 1] if slot == 0 else others[slot - 1, head, 1]
            probs = jnp.exp2(scores[head, slot] - top)
            total = total + jnp.sum(probs, axis=0, keepdims=True)
            summed = summed + dot(values, probs.astype(BF16), TN)
        result[:, head_cols(head)] = (summed / total).T.astype(BF16)
        lse[head : head + 1] = top + jnp.log2(total)
    if with_context:
        text[1].wait_recv()
        text[2].start()
        text[0].wait_recv()
        text[2].wait_recv()
    for item in [to_near] + to_far + onward + text:
        item.wait_send()


def out_sum_kernel(
    side,
    rows_in,
    weight,
    context,
    text_weight,
    rows_w,
    total,
    text_key,
    text_kb,
    text_vb,
    slots,
    send_sems,
    recv_sems,
    part,
    came,
    pair,
    peers,
    sems,
):
    greet(True, side.masks)
    side.start()
    chain = Chain(part, total, (came, pair, peers), sems)
    tokens, features = total.shape
    per_block = 128 // CHUNK

    def project(rows, index):
        part[rows] = dot(rows_in[rows], weight[0], NT).astype(BF16)
        chain.begin(index * per_block, per_block)

    loop_rows(tokens, 128, project)
    text_count, width = text_key.shape
    blocks = text_count // 128

    def text(rows, index):
        block = context[rows]
        text_key[rows] = dot(block, text_weight[1]) + row_of(rows_w, 3)
        chain.serve(2 * index)
        text_vb[rows] = (dot(block, text_weight[2]) + row_of(rows_w, 4)).astype(BF16)
        chain.serve(2 * index + 1)

    loop_rows(text_count, 128, text)
    exchange = Exchange(slots, send_sems, recv_sems)

    def early():
        side.early()
        exchange.start(stat_rows(text_key[...] * text_key[...], 0))

    def late():
        exchange.finish()
        text_inv = inverse_rms(stat_column(slots, 0, HEAD_DIM), features)
        for head in range(width // HEAD_DIM):
            cols = head_cols(head)
            text_kb[:, cols] = (
                text_key[:, cols] * text_inv * rows_w[GAINS + 3 : GAINS + 4, cols]
            ).astype(BF16)
        side.late()

    chain.drain(2 * blocks, early, late)
    side.finish()


def cross_kernel(
    side,
    base,
    tot,
    rows_d,
    rows_w,
    weight,
    text_kb,
    text_vb,
    out_weight,
    hidden,
    normal,
    query,
    query_b,
    result,
    lse,
    slots,
    total,
    send_sems,
    recv_sems,
    part,
    came,
    pair,
    peers,
    sems,
):
    greet(True, side.masks)
    side.start()
    chain = Chain(part, total, (came, pair, peers), sems)
    tokens, width = query.shape
    features = hidden.shape[1]
    heads = width // HEAD_DIM

    def project(rows, index):
        block = add_branch(
            base[rows], tot[rows], row_of(rows_d, OUT_BIAS), row_of(rows_d, MODS + 2)
        )
        hidden[rows] = block
        block = normed(block)[0] * row_of(rows_d, CROSS_GAIN) + row_of(rows_d, CROSS_SHIFT)
        block = block.astype(BF16)
        normal[rows] = block
        query[rows] = dot(block, weight[0]) + row_of(rows_w, 2)

    loop_rows(tokens, 256, project)
    exchange = Exchange(slots, send_sems, recv_sems)
    exchange.start(stat_rows(query[...] * query[...], 0))
    exchange.finish()
    query_inv = inverse_rms(stat_column(slots, 0, HEAD_DIM), features)
    lse[...] = jnp.zeros(lse.shape, F32)
    for head in range(heads):
        cols = head_cols(head)
        query_b[:, cols] = (
            query[:, cols] * query_inv * rows_w[GAINS + 2 : GAINS + 3, cols]
        ).astype(BF16)
        scores = dot(text_kb[:, cols], query_b[:, cols], NT) * (SCALE * LOG2E)
        top = jnp.max(scores, axis=0, keepdims=True)
        probs = jnp.exp2(scores - top)
        amount = jnp.sum(probs, axis=0, keepdims=True)
        summed = dot(text_vb[:, cols], probs.astype(BF16), TN)
        result[:, cols] = (summed / amount).T.astype(BF16)
        lse[head : head + 1] = top + jnp.log2(amount)
    per_block = 128 // CHUNK

    def project_out(rows, index):
        part[rows] = dot(result[rows], out_weight[1], NT).astype(BF16)
        chain.begin(index * per_block, per_block)

    loop_rows(tokens, 128, project_out)
    chain.drain(0, side.early, side.late)
    side.finish()


def column_cuts(width):
    cuts, low = [], 0
    while low < width:
        high = low + 512 if width - low >= 1024 else width
        cuts.append((low, high))
        low = high
    return cuts


GELU_A = 0.7978845608028654
GELU_B = 0.044715


def mlp_loop(side, tokens, rows_of, inner, second, chain, middle):
    size = 128
    per_block = size // CHUNK
    features, hidden_width = second.shape
    cuts = column_cuts(hidden_width)
    half = features // 2
    blocks = tokens // size

    def step(index, carry):
        rows = pl.ds(pl.multiple_of(index * size, size), size)
        block = rows_of(rows)

        def serve(offset):
            @pl.when(index > 0)
            def _():
                chain.serve(jnp.maximum(index - 1, 0) * per_block + offset)

        served = 0
        for place, (low, high) in enumerate(cuts):
            inner(rows, block, low, high)
            if place % 2 == 1 and served < 2:
                serve(served)
                served += 1
        while served < 2:
            serve(served)
            served += 1
        for part_index in range(2):
            cols = slice(part_index * half, (part_index + 1) * half)
            chain.part[rows, cols] = dot(middle[rows], second[cols], NT).astype(BF16)
            if part_index == 0:
                serve(2)
        chain.begin(index * per_block, per_block)
        serve(3)
        if side.jobs:

            @pl.when(index == 1)
            def _():
                side.early()

            @pl.when(index == blocks - 1)
            def _():
                side.late()

        return carry

    lax.fori_loop(0, blocks, step, 0)
    chain.drain((blocks - 1) * per_block)
    side.finish()


def ffn_kernel(
    side,
    base,
    tot,
    rows_d,
    up,
    rows_f,
    down,
    hidden,
    normal,
    gelu_b,
    slope,
    total,
    part,
    came,
    pair,
    peers,
    sems,
):
    greet(True, side.masks)
    side.start()
    chain = Chain(part, total, (came, pair, peers), sems)
    tokens = hidden.shape[0]
    scale_row = 1.0 + row_of(rows_d, MODS + 4)
    shift_row = row_of(rows_d, MODS + 3)

    def rows_of(rows):
        block = add_branch(base[rows], tot[rows], row_of(rows_d, OUT_BIAS + 1), 1.0)
        hidden[rows] = block
        block = (normed(block)[0] * scale_row + shift_row).astype(BF16)
        normal[rows] = block
        return block

    def inner(rows, block, low, high):
        z = dot(block, up[:, low:high]) + rows_f[:, low:high]
        square = z * z
        tanh = jnp.tanh(GELU_A * z * (1.0 + GELU_B * square))
        side_value = 0.5 * (1.0 + tanh)
        gelu_b[rows, low:high] = (z * side_value).astype(BF16)
        slope[rows, low:high] = (
            side_value
            + 0.5 * z * (1.0 - tanh * tanh) * (GELU_A * (1.0 + 3.0 * GELU_B * square))
        ).astype(BF16)

    mlp_loop(side, tokens, rows_of, inner, down, chain, gelu_b)


def ffn_back_kernel(
    side,
    grad,
    tot,
    rows_d,
    down,
    up,
    slope,
    down_in,
    inner_b,
    total,
    sums,
    bias_sum,
    part,
    came,
    pair,
    peers,
    sems,
):
    greet(True, side.masks)
    side.start()
    chain = Chain(part, total, (came, pair, peers), sems)
    tokens = grad.shape[0]
    sums[...] = jnp.zeros(sums.shape, F32)
    bias_sum[...] = jnp.zeros(bias_sum.shape, F32)

    def rows_of(rows):
        block = grad[rows]
        add_sum(sums, 0, block * (tot[rows].astype(F32) + row_of(rows_d, OUT_BIAS + 2)))
        block = (block * row_of(rows_d, MODS + 5)).astype(BF16)
        down_in[rows] = block
        add_sum(sums, 1, block.astype(F32))
        return block

    def inner(rows, block, low, high):
        cols = (dot(block, down[:, low:high]) * slope[rows, low:high].astype(F32)).astype(BF16)
        inner_b[rows, low:high] = cols
        bias_sum[0:1, low:high] += jnp.sum(cols.astype(F32), axis=0, keepdims=True)

    mlp_loop(side, tokens, rows_of, inner, up, chain, inner_b)


def cross_back_kernel(
    side,
    grad,
    branch,
    hidden,
    rows_d,
    rows_w,
    out_weight,
    query,
    query_b,
    lse,
    slots_q,
    text_kb,
    text_vb,
    weight,
    new_grad,
    out_in,
    text_grad,
    query_grad_b,
    sums,
    width_sums,
    total,
    out_grad,
    query_n,
    slots,
    send_sems,
    recv_sems,
    part,
    came,
    pair,
    peers,
    sems,
):
    greet(True, side.masks)
    side.start()
    chain = Chain(part, total, (came, pair, peers), sems)
    tokens, width = query.shape
    features = grad.shape[1]
    heads = width // HEAD_DIM
    gain = rows_w[GAINS + 2 : GAINS + 3]
    sums[...] = jnp.zeros(sums.shape, F32)
    width_sums[...] = jnp.zeros(width_sums.shape, F32)
    scale_row = 1.0 + row_of(rows_d, MODS + 4)

    def enter(rows, index):
        step = branch[rows].astype(F32)
        back, hat = norm_back(hidden[rows], scale_row, step)
        add_sum(sums, 0, step)
        add_sum(sums, 1, step * hat)
        block = grad[rows] + back
        new_grad[rows] = block
        block = block.astype(BF16)
        out_in[rows] = block
        add_sum(sums, 2, block.astype(F32))
        out_grad[rows] = dot(block, out_weight[1]).astype(BF16)

    loop_rows(tokens, 256, enter)
    side.early_first()
    for head in range(heads):
        cols = head_cols(head)
        query_h, out_grad_h = query_b[:, cols], out_grad[:, cols]
        text_k, text_v = text_kb[:, cols], text_vb[:, cols]
        probs = softmax_back(dot(text_k, query_h, NT), lse[head : head + 1], None)
        prob_grad = dot(text_v, out_grad_h, NT)
        inner = jnp.sum(probs * prob_grad, axis=0, keepdims=True)
        score_b = (probs * (prob_grad - inner) * SCALE).astype(BF16)
        query_n[:, cols] = dot(text_k, score_b, TN).T
        text_grad[0, :, cols] = dot(score_b, query_h)
        text_grad[1, :, cols] = dot(probs.astype(BF16), out_grad_h)
    exchange = Exchange(slots, send_sems, recv_sems)
    exchange.start(stat_rows(query[...] * query_n[...] * gain, 0))
    inverse = inverse_rms(stat_column(slots_q, 0, HEAD_DIM), features)
    exchange.finish()
    term = stat_column(slots, 0, HEAD_DIM) * inverse * inverse * inverse / features
    for head in range(heads):
        cols = head_cols(head)
        width_sums[0:1, cols] = jnp.sum(
            query[:, cols] * query_n[:, cols] * inverse, axis=0, keepdims=True
        )
        block = inverse * gain[:, cols] * query_n[:, cols] - query[:, cols] * term
        block = block.astype(BF16)
        query_grad_b[:, cols] = block
        width_sums[1:2, cols] = jnp.sum(block.astype(F32), axis=0, keepdims=True)
    per_block = 128 // CHUNK

    def leave(rows, index):
        part[rows] = dot(query_grad_b[rows], weight[0], NT).astype(BF16)
        chain.begin(index * per_block, per_block)

    loop_rows(tokens, 128, leave)
    chain.drain(0, side.early_rest, side.late)
    side.finish()


def attend_back_kernel(
    side,
    counts,
    grad,
    branch,
    hidden,
    rows_d,
    tot,
    out_weight,
    query,
    key_value,
    others,
    lse,
    text_grad,
    new_grad,
    out_in,
    sums,
    query_grad,
    key_value_grad,
    text_sum,
    out_grad,
    probs,
    prob_grads,
    away,
    landed,
    text_away,
    text_landed,
    send_sems,
    recv_sems,
):
    greet(False, [1, 2])
    near, far = holders()
    tokens, width = query.shape
    heads = width // HEAD_DIM
    text_rows = text_sum.shape[1]
    sums[...] = jnp.zeros(sums.shape, F32)

    def copy(kind, head):
        return send(
            away.at[kind, head],
            landed.at[kind, head],
            send_sems.at[kind, head],
            recv_sems.at[kind, head],
            dp=far if kind == 1 else near,
        )

    def text_copy(kind):
        return send(
            text_away.at[kind],
            text_landed.at[kind],
            send_sems.at[kind, heads],
            recv_sems.at[kind, heads],
            dp=far if kind == 1 else near,
        )

    place = lax.rem(lax.axis_index("dp"), HOLD)

    def text_part(slot):
        start = pl.multiple_of(flip(place, slot) * text_rows, text_rows)
        return text_grad[:, pl.ds(start, text_rows)]

    text_away[2] = text_part(3).astype(BF16)
    text_copy(2).start()
    text_away[0] = text_part(1).astype(BF16)
    text_copy(0).start()

    def enter(rows, index):
        step = branch[rows].astype(F32)
        back, hat = norm_back(hidden[rows], row_of(rows_d, CROSS_GAIN), step)
        add_sum(sums, 0, step * hat)
        add_sum(sums, 1, step)
        block = grad[rows] + back
        new_grad[rows] = block
        add_sum(sums, 2, block * (tot[rows].astype(F32) + row_of(rows_d, OUT_BIAS)))
        block = (block * row_of(rows_d, MODS + 2)).astype(BF16)
        out_in[rows] = block
        add_sum(sums, 3, block.astype(F32))
        out_grad[rows] = dot(block, out_weight[0]).astype(BF16)

    loop_rows(tokens, 256, enter)
    text_copy(2).wait_recv()
    text_away[1] = (text_part(2) + text_landed[2].astype(F32)).astype(BF16)
    text_copy(1).start()

    for head in range(heads):
        cols = head_cols(head)
        query_h, out_grad_h = query[:, cols], out_grad[:, cols]

        def pair_of(slot, head=head):
            if slot == 0:
                return key_value[head, 0], key_value[head, 1]
            return others[slot - 1, head, 0], others[slot - 1, head, 1]

        inner = jnp.zeros((1, tokens), F32)
        for slot in range(HOLD):
            keys, values = pair_of(slot)
            block = softmax_back(
                dot(keys, query_h, NT),
                lse[head : head + 1],
                below(counts, slot, (tokens, tokens)),
            )
            probs[slot] = block
            block_grad = dot(values, out_grad_h, NT)
            prob_grads[slot] = block_grad
            inner = inner + jnp.sum(block * block_grad, axis=0, keepdims=True)
        query_n = jnp.zeros((HEAD_DIM, tokens), F32)
        for slot in (3, 2, 1, 0):
            keys, values = pair_of(slot)
            block = probs[slot]
            score_b = (block * (prob_grads[slot] - inner) * SCALE).astype(BF16)
            query_n = query_n + dot(keys, score_b, TN)
            key_g = dot(score_b, query_h)
            value_g = dot(block.astype(BF16), out_grad_h)
            if slot == 0:
                key_value_grad[0, :, cols] = key_g
                key_value_grad[1, :, cols] = value_g
            elif slot == 2:
                copy(2, head).wait_recv()
                away[1, head, 0] = (key_g + landed[2, head, 0].astype(F32)).astype(BF16)
                away[1, head, 1] = (value_g + landed[2, head, 1].astype(F32)).astype(BF16)
                copy(1, head).start()
            else:
                away[slot - 1, head, 0] = key_g.astype(BF16)
                away[slot - 1, head, 1] = value_g.astype(BF16)
                copy(slot - 1, head).start()
        query_grad[:, cols] = query_n.T
    text_copy(0).wait_recv()
    text_copy(1).wait_recv()
    text_sum[...] = text_part(0) + text_landed[0].astype(F32) + text_landed[1].astype(F32)
    for head in range(heads):
        cols = head_cols(head)
        copy(0, head).wait_recv()
        copy(1, head).wait_recv()
        for member in range(2):
            key_value_grad[member, :, cols] += landed[0, head, member].astype(F32) + landed[
                1, head, member
            ].astype(F32)
    for kind in range(3):
        text_copy(kind).wait_send()
        for head in range(heads):
            copy(kind, head).wait_send()


def qkv_back_kernel(
    side,
    query_grad,
    key_value_grad,
    text_grad,
    query,
    key,
    text_key,
    slots_in,
    text_slots,
    rows_w,
    cosine,
    sine,
    weight,
    grads_b,
    text_b,
    width_sums,
    total,
    query_n,
    key_n,
    slots,
    send_sems,
    recv_sems,
    part,
    came,
    pair,
    peers,
    sems,
):
    greet(True, side.masks)
    side.start()
    chain = Chain(part, total, (came, pair, peers), sems)
    tokens, width = query.shape
    features = total.shape[1]
    heads = width // HEAD_DIM
    text_rows = text_grad.shape[1]
    place = lax.rem(lax.axis_index("dp"), HOLD)
    mine = pl.ds(pl.multiple_of(place * text_rows, text_rows), text_rows)
    text_k = text_key[mine]
    width_sums[...] = jnp.zeros(width_sums.shape, F32)
    for head in range(heads):
        cols = head_cols(head)
        rows = query_grad[:, cols]
        query_n[:, cols] = rows * cosine[...] - turned(rows * sine[...])
        rows = key_value_grad[0, :, cols]
        key_n[:, cols] = rows * cosine[...] - turned(rows * sine[...])

    def gain(member):
        return rows_w[GAINS + member : GAINS + member + 1]

    exchange = Exchange(slots, send_sems, recv_sems)
    text_terms = stat_rows(text_k * gain(3) * text_grad[0], 2)
    exchange.start(
        stat_rows(query[...] * gain(0) * query_n[...], 0)
        + stat_rows(key[...] * gain(1) * key_n[...], 1)
        + jnp.concatenate([text_terms, jnp.zeros((8, tokens - text_rows), F32)], axis=1)
    )
    query_inv = inverse_rms(stat_column(slots_in, 0, HEAD_DIM), features)
    key_inv = inverse_rms(stat_column(slots_in, 1, HEAD_DIM), features)
    text_inv = inverse_rms(stat_column(text_slots.at[:, :, mine], 0, HEAD_DIM), features)
    side.early_first()
    exchange.finish()

    def cubed(inverse, term):
        return term * inverse * inverse * inverse / features

    query_t = cubed(query_inv, stat_column(slots, 0, HEAD_DIM))
    key_t = cubed(key_inv, stat_column(slots, 1, HEAD_DIM))
    text_t = cubed(text_inv, stat_column(slots.at[:, :, pl.ds(0, text_rows)], 2, HEAD_DIM))

    def back(member, cols, values, inverse, term, grads):
        width_sums[member : member + 1, cols] = jnp.sum(
            values * inverse * grads, axis=0, keepdims=True
        )
        block = inverse * gain(member)[:, cols] * grads - values * term
        block = block.astype(BF16)
        width_sums[4 + member : 5 + member, cols] = jnp.sum(
            block.astype(F32), axis=0, keepdims=True
        )
        return block

    def shifted(cols, member):
        return slice(cols.start + member * width, cols.stop + member * width)

    for head in range(heads):
        cols = head_cols(head)
        grads_b[:, cols] = back(0, cols, query[:, cols], query_inv, query_t, query_n[:, cols])
        grads_b[:, shifted(cols, 1)] = back(
            1, cols, key[:, cols], key_inv, key_t, key_n[:, cols]
        )
        text_b[:, cols] = back(
            3, cols, text_k[:, cols], text_inv, text_t, text_grad[0, :, cols]
        )
    block = key_value_grad[1].astype(BF16)
    grads_b[:, 2 * width :] = block
    width_sums[6:7] = jnp.sum(block.astype(F32), axis=0, keepdims=True)
    block = text_grad[1].astype(BF16)
    text_b[:, width:] = block
    width_sums[8:9] = jnp.sum(block.astype(F32), axis=0, keepdims=True)
    per_block = 128 // CHUNK

    def leave(rows, index):
        part[rows] = (
            dot(grads_b[rows, :width], weight[0], NT)
            + dot(grads_b[rows, width : 2 * width], weight[1], NT)
            + dot(grads_b[rows, 2 * width :], weight[2], NT)
        ).astype(BF16)
        chain.begin(index * per_block, per_block)

    loop_rows(tokens, 128, leave)
    chain.drain(0, side.early_rest, side.late)
    side.finish()


def norm_back_kernel(side, grad, branch, hidden, rows_d, new_grad, sums):
    sums[...] = jnp.zeros(sums.shape, F32)
    scale_row = 1.0 + row_of(rows_d, MODS + 1)

    def enter(rows, index):
        step = branch[rows].astype(F32)
        back, hat = norm_back(hidden[rows], scale_row, step)
        add_sum(sums, 0, step)
        add_sum(sums, 1, step * hat)
        new_grad[rows] = grad[rows] + back

    loop_rows(grad.shape[0], 128, enter)


def scatter_kernel(side):
    greet(False, side.masks)
    side.start()
    side.early()
    side.late()
    side.finish()


def weight_grad(left, right):
    return dot(left, right, TN).astype(BF16)


def per_device(
    latents,
    context,
    time_embed,
    teacher,
    lengths,
    block_order,
    positions,
    self_proj,
    cross_proj,
    out_proj,
    ffn_up,
    ffn_down,
    proj_bias,
    key_bias,
    norm_gains,
    ffn_bias,
    out_bias,
    cross_gain,
    cross_shift,
    modulation,
):
    tokens, features = latents.shape
    width = norm_gains.shape[-1]
    heads = width // HEAD_DIM
    hidden_width = ffn_bias.shape[-1]
    clip_count = time_embed.shape[0]
    text_rows = context.shape[0]
    text_all = text_rows * HOLD
    clip = lax.axis_index("dp") // HOLD
    out_t = jnp.swapaxes(out_proj, 2, 3)
    down_t = jnp.swapaxes(ffn_down, 1, 2)

    rows_d = (tokens, features)
    rows_w = (tokens, width)
    rows_f = (tokens, hidden_width)
    stats = (CHAIN, 8, tokens)
    three = pltpu.SemaphoreType.DMA((CHAIN - 1,))
    chain_scratch = Chain.scratch(tokens, features)
    kv_shape = (heads, 2, tokens, HEAD_DIM)

    pack = (((16, features), F32), ((16, width), F32), ((1, hidden_width), F32))
    results, (self_w,) = run(
        "entry",
        entry_kernel,
        (
            lengths,
            block_order,
            time_embed,
            modulation,
            out_bias,
            cross_gain,
            cross_shift,
            proj_bias,
            key_bias,
            norm_gains,
            ffn_bias,
        ),
        (((HOLD, 8, tokens), F32),) + pack * LAYERS,
        [three, three],
        jobs=[Gather(self_proj, 0)],
        scalars=2,
        micros=25,
    )
    counts = results[0]
    packs = [results[1 + 3 * layer : 4 + 3 * layer] for layer in range(LAYERS)]
    cosine, sine = rope_angles(positions, HEAD_DIM)

    saved = []
    weights = {"self": [self_w], "cross": [], "out": [], "up": [], "down": []}
    sources = {
        "self": self_proj,
        "cross": cross_proj,
        "out": out_t,
        "up": ffn_up,
        "down": down_t,
    }

    def gathers(layer, *names):
        return [Gather(sources[name], layer) for name in names if layer < LAYERS]

    def keep(found, *names):
        for name, item in zip(names, found):
            weights[name].append(item)

    base, tot, before = latents, latents, packs[0][0]
    for layer in range(LAYERS):
        pack_d, pack_w, pack_f = packs[layer]
        names = ("cross", "out") if layer == 0 else ()
        (hidden, a1, sq, sk, q_rot, kv, stat1), found = run(
            "qkv" + str(layer > 0),
            functools.partial(qkv_kernel, layer == 0),
            (base, tot, before, pack_d, pack_w, weights["self"][layer], cosine, sine),
            (
                (rows_d, F32),
                (rows_d, BF16),
                (rows_w, F32),
                (rows_w, F32),
                (rows_w, BF16),
                (kv_shape, BF16),
                (stats, F32),
            ),
            [three, three],
            jobs=gathers(layer, *names),
            micros=15,
        )
        keep(found, *names)
        attended, unused = run(
            "attend" + str(layer > 0),
            functools.partial(attend_kernel, layer == 0),
            (counts, q_rot, kv) + ((context,) if layer == 0 else ()),
            (((HOLD - 1,) + kv_shape, BF16), (rows_w, BF16), ((8, tokens), F32))
            + ((((text_all, features), BF16),) if layer == 0 else ()),
            [
                pltpu.VMEM((heads, HOLD, tokens, tokens), F32),
                pltpu.SemaphoreType.DMA((4 + 2 * heads,)),
                pltpu.SemaphoreType.DMA((4 + 2 * heads,)),
            ],
            micros=30,
        )
        others, o1, lse1 = attended[:3]
        if layer == 0:
            clip_context = attended[3]
        (tot1, ck, ckb, cvb, stat_t), found = run(
            "out_sum",
            out_sum_kernel,
            (o1, weights["out"][layer], clip_context, weights["cross"][layer], pack_w),
            (
                (rows_d, BF16),
                ((text_all, width), F32),
                ((text_all, width), BF16),
                ((text_all, width), BF16),
                ((CHAIN, 8, text_all), F32),
            ),
            [three, three] + chain_scratch,
            jobs=gathers(layer, "up"),
            micros=45,
        )
        keep(found, "up")
        names = ("down",) if layer == LAYERS - 1 else ("down", "self")
        (h1, a3, cq, cqb, o2, lse2, stat2, tot2), found = run(
            "cross",
            cross_kernel,
            (hidden, tot1, pack_d, pack_w, weights["cross"][layer], ckb, cvb)
            + (weights["out"][layer],),
            (
                (rows_d, F32),
                (rows_d, BF16),
                (rows_w, F32),
                (rows_w, BF16),
                (rows_w, BF16),
                ((8, tokens), F32),
                (stats, F32),
                (rows_d, BF16),
            ),
            [three, three] + chain_scratch,
            jobs=gathers(layer, "down") + (gathers(layer + 1, "self")),
            micros=50,
        )
        keep(found, *names)
        (h2, a2, gelu_b, slope, tot3), found = run(
            "ffn",
            ffn_kernel,
            (h1, tot2, pack_d, weights["up"][layer], pack_f, weights["down"][layer]),
            (
                (rows_d, F32),
                (rows_d, BF16),
                (rows_f, BF16),
                (rows_f, BF16),
                (rows_d, BF16),
            ),
            chain_scratch,
            jobs=gathers(layer + 1, "cross", "out"),
            micros=55,
        )
        keep(found, "cross", "out")
        saved.append(
            (hidden, a1, sq, sk, q_rot, kv, stat1, others, o1, lse1, tot1, ck, ckb, cvb, stat_t)
            + (h1, a3, cq, cqb, o2, lse2, stat2, h2, a2, gelu_b, slope, tot3)
        )
        base, tot, before = h2, tot3, pack_d
    output = add_branch(base, tot, before[OUT_BIAS + 2], before[MODS + 5])
    valid = jnp.arange(tokens, dtype=jnp.int32).astype(F32) < counts[0, 0, 0]
    error = jnp.where(valid[:, None], output - teacher.astype(F32), 0.0)
    sse = jnp.sum(error * error)
    grad = error

    pending = []
    reduced = {}

    def scatter_some(names):
        chosen = [item for item in pending if item[0] in names]
        for item in chosen:
            pending.remove(item)
        return [item[0] for item in chosen], [Scatter(item[1]) for item in chosen]

    def keep_sums(names, found):
        for name, item in zip(names, found):
            reduced[name] = item

    sums_d, sums_w, sums_f = [], [], []
    context_part = jnp.zeros(context.shape, F32)
    for layer in reversed(range(LAYERS)):
        (hidden, a1, sq, sk, q_rot, kv, stat1, others, o1, lse1, tot1, ck, ckb, cvb, stat_t) = saved[
            layer
        ][:15]
        (h1, a3, cq, cqb, o2, lse2, stat2, h2, a2, gelu_b, slope, tot3) = saved[layer][15:]
        pack_d, pack_w, pack_f = packs[layer]
        w_self, w_cross, w_out, w_up, w_down = [
            weights[name][layer] for name in ("self", "cross", "out", "up", "down")
        ]
        names, jobs = scatter_some([("self", layer + 1), ("text", layer + 1), ("out0", layer + 1)])
        (dy3, dz, da2, sums3, dz_sum), found = run(
            "ffn_back",
            ffn_back_kernel,
            (grad, tot3, pack_d, w_down, w_up, slope),
            (
                (rows_d, BF16),
                (rows_f, BF16),
                (rows_d, BF16),
                ((8, features), F32),
                ((8, hidden_width), F32),
            ),
            chain_scratch,
            jobs=jobs,
            micros=55,
        )
        keep_sums(names, found)
        pending.append((("up", layer), weight_grad(a2, dz)))
        pending.append((("down", layer), weight_grad(dy3, gelu_b)))
        names, jobs = scatter_some([("up", layer), ("down", layer)])
        (grad, dy2, dct, dcq, sums2, wsums2, da3), found = run(
            "cross_back",
            cross_back_kernel,
            (grad, da2, h2, pack_d, pack_w, w_out, cq, cqb, lse2, stat2, ckb, cvb, w_cross),
            (
                (rows_d, F32),
                (rows_d, BF16),
                ((2, text_all, width), F32),
                (rows_w, BF16),
                ((8, features), F32),
                ((8, width), F32),
                (rows_d, BF16),
            ),
            [
                pltpu.VMEM(rows_w, BF16),
                pltpu.VMEM(rows_w, F32),
                pltpu.VMEM(stats, F32),
                three,
                three,
            ]
            + chain_scratch,
            jobs=jobs,
            micros=60,
        )
        keep_sums(names, found)
        (grad, dy1, sums1, dq_rot, dkv, dtext), unused = run(
            "attend_back",
            attend_back_kernel,
            (counts, grad, da3, h1, pack_d, tot1, w_out, q_rot, kv, others, lse1, dct),
            (
                (rows_d, F32),
                (rows_d, BF16),
                ((8, features), F32),
                (rows_w, F32),
                ((2,) + rows_w, F32),
                ((2, text_rows, width), F32),
            ),
            [
                pltpu.VMEM(rows_w, BF16),
                pltpu.VMEM((HOLD, tokens, tokens), F32),
                pltpu.VMEM((HOLD, tokens, tokens), F32),
                pltpu.VMEM((3,) + kv_shape, BF16),
                pltpu.VMEM((3,) + kv_shape, BF16),
                pltpu.VMEM((3, 2, text_rows, width), BF16),
                pltpu.VMEM((3, 2, text_rows, width), BF16),
                pltpu.SemaphoreType.DMA((3, heads + 1)),
                pltpu.SemaphoreType.DMA((3, heads + 1)),
            ],
            micros=35,
        )
        pending.append((("crossq", layer), weight_grad(a3, dcq)))
        pending.append((("out1", layer), weight_grad(dy2, o2)))
        pending.append((("out0", layer), weight_grad(dy1, o1)))
        names, jobs = scatter_some([("crossq", layer), ("out1", layer)] + [("out0", 0)])
        (ds, dt, wsums1, da1), found = run(
            "qkv_back",
            qkv_back_kernel,
            (dq_rot, dkv, dtext, sq, sk, ck, stat1, stat_t, pack_w, cosine, sine, w_self),
            (
                ((tokens, 3 * width), BF16),
                ((text_rows, 2 * width), BF16),
                ((16, width), F32),
                (rows_d, BF16),
            ),
            [
                pltpu.VMEM(rows_w, F32),
                pltpu.VMEM(rows_w, F32),
                pltpu.VMEM(stats, F32),
                three,
                three,
            ]
            + chain_scratch,
            jobs=jobs,
            micros=50,
        )
        keep_sums(names, found)
        pending.append((("self", layer), weight_grad(a1, ds)))
        pending.append((("text", layer), weight_grad(context, dt)))
        context_part = (
            context_part
            + dot(dt[:, :width], w_cross[1], NT)
            + dot(dt[:, width:], w_cross[2], NT)
        )
        (grad, sums0), unused = run(
            "norm_back",
            norm_back_kernel,
            (grad, da1, hidden, pack_d),
            ((rows_d, F32), ((8, features), F32)),
            remote=False,
            micros=6,
        )
        sums_d = [sums0, sums1, sums2, sums3] + sums_d
        sums_w = [wsums1, wsums2] + sums_w
        sums_f = [dz_sum] + sums_f
    names, jobs = scatter_some([("self", 0), ("text", 0), ("out0", 0)])
    unused, found = run("scatter", scatter_kernel, (), (), jobs=jobs, micros=40)
    keep_sums(names, found)

    sums_d = jnp.stack(sums_d).reshape(LAYERS, 4, 8, features)
    onehot = (jnp.arange(clip_count, dtype=jnp.int32) == clip).astype(F32)
    mod_sums = jnp.stack(
        [
            sums_d[:, 0, 0],
            sums_d[:, 0, 1],
            sums_d[:, 1, 2],
            sums_d[:, 2, 0],
            sums_d[:, 2, 1],
            sums_d[:, 3, 0],
        ],
        axis=1,
    )
    time_sums = onehot[:, None, None] * jnp.sum(mod_sums, axis=0)[None]
    packed_d = jnp.concatenate(
        [
            mod_sums.reshape(-1, features),
            time_sums.reshape(-1, features),
            jnp.stack([sums_d[:, 1, 3], sums_d[:, 2, 2], sums_d[:, 3, 1]], axis=1).reshape(
                -1, features
            ),
            sums_d[:, 1, 0],
            sums_d[:, 1, 1],
            jnp.full((1, features), sse / features, F32),
        ]
    )
    packed_w = jnp.concatenate(sums_w)
    packed_f = jnp.concatenate([item[0:1] for item in sums_f])
    packed_d, packed_w, packed_f = lax.psum(
        (packed_d.astype(BF16), packed_w.astype(BF16), packed_f.astype(BF16)), "dp"
    )
    packed_d, packed_w, packed_f = (
        packed_d.astype(F32),
        packed_w.astype(F32).reshape(LAYERS, 24, width),
        packed_f.astype(F32),
    )
    context_grad = lax.psum(context_part.astype(BF16), "tensor").astype(F32)
    low = 6 * LAYERS
    modulation_grad = packed_d[:low].reshape(LAYERS, 6, features)
    time_grad = packed_d[low : low + 6 * clip_count].reshape(clip_count, 6, features)
    low += 6 * clip_count
    out_bias_grad = packed_d[low : low + 3 * LAYERS].reshape(LAYERS, 3, features)
    low += 3 * LAYERS
    cross_gain_grad = packed_d[low : low + LAYERS]
    cross_shift_grad = packed_d[low + LAYERS : low + 2 * LAYERS]
    loss = jnp.sum(packed_d[low + 2 * LAYERS]) / (jnp.sum(lengths).astype(F32) * features)
    proj_bias_grad = jnp.stack([packed_w[:, row] for row in (4, 6, 17, 7, 8)], axis=1)
    gains_grad = jnp.stack([packed_w[:, row] for row in (0, 1, 16, 3)], axis=1)

    def split(block):
        return jnp.swapaxes(block.reshape(block.shape[0], -1, width), 0, 1)

    self_grad = jnp.stack([split(reduced["self", layer]) for layer in range(LAYERS)])
    cross_grad = jnp.stack(
        [
            jnp.concatenate([reduced["crossq", layer][None], split(reduced["text", layer])])
            for layer in range(LAYERS)
        ]
    )
    out_grad = jnp.stack(
        [
            jnp.stack([reduced["out0", layer].T, reduced["out1", layer].T])
            for layer in range(LAYERS)
        ]
    )
    up_grad = jnp.stack([reduced["up", layer] for layer in range(LAYERS)])
    down_grad = jnp.stack([reduced["down", layer].T for layer in range(LAYERS)])
    return (
        output,
        loss,
        grad,
        context_grad,
        time_grad,
        self_grad,
        cross_grad,
        out_grad,
        up_grad,
        down_grad,
        proj_bias_grad,
        packed_w[:, 5],
        gains_grad,
        packed_f,
        out_bias_grad,
        cross_gain_grad,
        cross_shift_grad,
        modulation_grad,
    )


def solution(mesh):
    COLLECTIVES.clear()
    rows = P("dp", None)
    col_in = P(None, None, "dp", "tensor")
    col_out = P(None, None, "tensor", "dp")
    up, down = P(None, "dp", "tensor"), P(None, "tensor", "dp")
    vec, mat = P(None, "tensor"), P(None, None, "tensor")
    return jax.shard_map(
        per_device,
        mesh=mesh,
        in_specs=(rows, rows, P(), rows, P(), P("dp"), P(None, "dp"))
        + (col_in, col_in, col_out, up, down)
        + (mat, vec, mat, vec, P(), P(), P(), P()),
        out_specs=(rows, P(), rows, rows, P())
        + (col_in, col_in, col_out, up, down)
        + (mat, vec, mat, vec, P(), P(), P(), P()),
        check_vma=False,
    )
```

time: 2390 us -> 1300 us (0.54)
  waiting for transfers between devices: 1410 us -> 0.04 us
  Pallas kernels: 0 us -> 1070 us
  matrix products: 388 us -> 64.2 us
  other arithmetic: 205 us -> 25.9 us
  local copies, waits for them, and re-layouts: 225 us -> 82.2 us
  blocking collectives: 106 us -> 23.1 us
  starting transfers between devices: 26 us -> 0.08 us
    pallas_call x0 -> x22, Pallas kernels: none -> 1070 us  [run(): pl.pallas_call(body, out_shape=tuple((jax.ShapeDtypeStruct(shape, kind) f...]
    psum x13 -> x2, waiting for transfers between devices: 674 us -> 0.01 us  [the longest x1 0.01 us: per_device(): lax.psum((packed_d.astype(BF16), packed_w.astype(BF16), packed_f.astype(B...]
    dot_general x74 -> x18, matrix products: 388 us -> 64.2 us  [dot(): lax.dot_general(left, right, dims, precision=precision, preferred_element...]
    all_gather x10 -> x0, waiting for transfers between devices: 290 us -> none  [the longest x2 91.8 us: per_device(): lax.all_gather(ffn_up[layer_index], 'dp', axis=0, tiled=True)]
    reduce_scatter x4 -> x0, waiting for transfers between devices: 267 us -> none  [the longest x2 135 us: per_device(): lax.psum_scatter(matrix_grads[4].astype(jnp.bfloat16), 'dp', scatter_dime...]
    unnamed x711 -> x117, local copies, waits for them, and re-layouts: 126 us -> 15 us
    unnamed x35 -> x2, waiting for transfers between devices: 95.3 us -> 0.03 us
    reduce_sum x54 -> x4, other arithmetic: 105 us -> 9.58 us  [the longest x1 6.73 us: per_device(): sse = jnp.sum(error * error)]
  transfers between devices with their start and end apart: 65 -> 2, of which waited for: 39 -> 0; matrix products, arithmetic and copies ran while one was open for 22% -> 3% of each run, Pallas kernels for 0% -> 3%
where the time goes in v1:
time: 1300 us; the launch traced here: 1290 us
  Pallas kernels  1070 us (82%)
  local copies, waits for them, and re-layouts  82.2 us (6%)
  matrix products  64.2 us (5%)
  other arithmetic  25.9 us (2%)
  blocking collectives  23.1 us (2%)
  between operations  18.9 us (1%)
    pallas_call x22, Pallas kernels, run(): pl.pallas_call(body, out_shape=tuple((jax.ShapeDtypeStruct(shape, kind) f...  1070 us
    dot_general x18, matrix products, dot(): lax.dot_general(left, right, dims, precision=precision, preferred_element...  64.2 us
    convert_element_type x4, local copies, waits for them, and re-layouts, weight_grad(): return dot(left, right, TN).astype(BF16)  40 us
  transfers between devices with their start and end apart: 2, of which 0 were waited for; matrix products, arithmetic and copies ran while one was open for 3% of the time, Pallas kernels for 3%

profile of v1, /device:TPU:8, one launch (start us, length us, event | category | flops | bytes accessed | tf_op | source)
XLA Modules:
  0.0 1288.6 jit_solution(14904218417376055341)
XLA Ops:
  14.5 24.9 %shard_map.358 = (f32[4,8,512]{2,1,0:T(8,128)}, f32[16,1536]{1,0:T(8,128)}, f32[16,384]{1,0:T(8,128)}, f32[1,2240]{1,0:T(1,128)}, f32[16,1536]{1,0:T(8,128)}, /*...) custom-call(s32[2]{0:T(128)} %refs_0_.2, s32[1]{0:T(128)S(6)} %copy.137.refs_1_, ...), custom_call_target="tpu_custom_call" | custom-call | bytes 75000000 | tf_op jit(solution)/shard_map/pallas_call | solution.py:561
  44.1 37.2 %shard_map.359 = (f32[512,1536]{1,0:T(8,128)}, bf16[512,1536]{1,0:T(8,128)(2,1)}, f32[512,384]{1,0:T(8,128)}, f32[512,384]{1,0:T(8,128)}, bf16[512,384]{1,0:T(8,...) custom-call(bf16[512,1536]{1,0:T(8,128)(2,1)} %refs_1_.2, ...), custom_call_target="tpu_custom_call" | custom-call | bytes 45000000 | tf_op jit(solution)/shard_map/pallas_call | solution.py:561
  81.3 33.3 %shard_map.360 = (bf16[3,3,2,512,128]{4,3,2,1,0:T(8,128)(2,1)}, bf16[512,384]{1,0:T(8,128)(2,1)}, f32[8,512]{1,0:T(8,128)}, bf16[512,1536]{1,0:T(8,128)(2,1)}) custom-call(f32[4,8,512]{2,1,0:T(8,128)} %get-tuple-element.158.refs_0_, bf16[512,384]{1,0:T(8,128)(2,1)} %get-tuple-element.159.refs_1_.refs_7_, ...), custom_call_target="tpu_custom_call" | custom-call | bytes 90000000 | tf_op jit(solution)/shard_map/pallas_call | solution.py:561
  114.5 57.0 %shard_map.361 = (bf16[512,1536]{1,0:T(8,128)(2,1)}, f32[512,384]{1,0:T(8,128)}, bf16[512,384]{1,0:T(8,128)(2,1)}, bf16[512,384]{1,0:T(8,128)(2,1)}, f32[4,8,512]{2,1,0:T(8,128)}, /*index=5*/bf16[1536,2240]{1,0:T(8,128)(2,1)}) custom-call(bf16[512,384]{1,0:T(8,128)(2,1)} %get-tuple-element.161.refs_0_, ...), custom_call_target="tpu_custom_call" | custom-call | bytes 135000000 | tf_op jit(solution)/shard_map/pallas_call | solution.py:561
  171.5 69.8 %shard_map.362 = (f32[512,1536]{1,0:T(8,128)}, bf16[512,1536]{1,0:T(8,128)(2,1)}, f32[512,384]{1,0:T(8,128)}, bf16[512,384]{1,0:T(8,128)(2,1)}, bf16[512,384]{1,...) custom-call(f32[512,1536]{1,0:T(8,128)} %get-tuple-element.157.refs_, ...), custom_call_target="tpu_custom_call" | custom-call | bytes 150000000 | tf_op jit(solution)/shard_map/pallas_call | solution.py:561
  241.3 68.8 %shard_map.363 = (f32[512,1536]{1,0:T(8,128)}, bf16[512,1536]{1,0:T(8,128)(2,1)}, bf16[512,2240]{1,0:T(8,128)(2,1)}, bf16[512,2240]{1,0:T(8,128)(2,1)}, bf16[512...) custom-call(f32[512,1536]{1,0:T(8,128)} %get-tuple-element.168.refs_0_.refs_3_, ...), custom_call_target="tpu_custom_call" | custom-call | bytes 165000000 | tf_op jit(solution)/shard_map/pallas_call | solution.py:561
  310.1 18.5 %shard_map.364 = (f32[512,1536]{1,0:T(8,128)}, bf16[512,1536]{1,0:T(8,128)(2,1)}, f32[512,384]{1,0:T(8,128)}, f32[512,384]{1,0:T(8,128)}, bf16[512,384]{1,0:T(8,...) custom-call(f32[512,1536]{1,0:T(8,128)} %get-tuple-element.173.refs_0_.refs_2_, ...), custom_call_target="tpu_custom_call" | custom-call | bytes 45000000 | tf_op jit(solution)/shard_map/pallas_call | solution.py:561
  328.6 24.2 %shard_map.365 = (bf16[3,3,2,512,128]{4,3,2,1,0:T(8,128)(2,1)}, bf16[512,384]{1,0:T(8,128)(2,1)}, f32[8,512]{1,0:T(8,128)}) custom-call(f32[4,8,512]{2,1,0:T(8,128)} %get-tuple-element.158.refs_0_, bf16[512,384]{1,0:T(8,128)(2,1)} %get-tuple-element.179.refs_1_.refs_7_, bf16[3,2,512,128]{3,2,1,0:T(8,128)(2,1)} %get-tuple-element.180.refs_2_.refs_8_), custom_call_target="tpu_custom_call" | custom-call | bytes 90000000 | tf_op jit(solution)/shard_map/pallas_call | solution.py:561
  352.8 58.0 %shard_map.366 = (bf16[512,1536]{1,0:T(8,128)(2,1)}, f32[512,384]{1,0:T(8,128)}, bf16[512,384]{1,0:T(8,128)(2,1)}, bf16[512,384]{1,0:T(8,128)(2,1)}, f32[4,8,512]{2,1,0:T(8,128)}, /*index=5*/bf16[1536,2240]{1,0:T(8,128)(2,1)}) custom-call(bf16[512,384]{1,0:T(8,128)(2,1)} %get-tuple-element.181.refs_0_, ...), custom_call_target="tpu_custom_call" | custom-call | bytes 135000000 | tf_op jit(solution)/shard_map/pallas_call | solution.py:561
  410.7 64.4 %shard_map.367 = (f32[512,1536]{1,0:T(8,128)}, bf16[512,1536]{1,0:T(8,128)(2,1)}, f32[512,384]{1,0:T(8,128)}, bf16[512,384]{1,0:T(8,128)(2,1)}, bf16[512,384]{1,...) custom-call(f32[512,1536]{1,0:T(8,128)} %get-tuple-element.178.refs_, ...), custom_call_target="tpu_custom_call" | custom-call | bytes 150000000 | tf_op jit(solution)/shard_map/pallas_call | solution.py:561
  475.1 67.8 %shard_map.368 = (f32[512,1536]{1,0:T(8,128)}, bf16[512,1536]{1,0:T(8,128)(2,1)}, bf16[512,2240]{1,0:T(8,128)(2,1)}, bf16[512,2240]{1,0:T(8,128)(2,1)}, bf16[512,1536]{1,0:T(8,128)(2,1)}) custom-call(f32[512,1536]{1,0:T(8,128)} %get-tuple-element.187.refs_0_.refs_3_, bf16[512,1536]{1,0:T(8,128)(2,1)} %get-tuple-element.188.refs_1_, ...), custom_call_target="tpu_custom_call" | custom-call | bytes 165000000 | tf_op jit(solution)/shard_map/pallas_call | solution.py:561
  542.9 6.7 multiply_reduce_fusion
  549.6 65.5 %shard_map.369 = (bf16[512,1536]{1,0:T(8,128)(2,1)}, bf16[512,2240]{1,0:T(8,128)(2,1)}, bf16[512,1536]{1,0:T(8,128)(2,1)}, f32[8,1536]{1,0:T(8,128)}, f32[8,2240]{1,0:T(8,128)}) custom-call(f32[512,1536]{1,0:T(8,128)} %get-tuple-element.349.refs_0_, bf16[512,1536]{1,0:T(8,128)(2,1)} %get-tuple-element.193.refs_1_, ...), custom_call_target="tpu_custom_call" | custom-call | bytes 165000000 | tf_op jit(solution)/shard_map/pallas_call | solution.py:561
  615.1 7.2 convolution_convert_fusion.2
  622.4 9.9 copy.91.refs_14_
  632.3 7.2 convolution_convert_fusion.3
  639.5 10.2 copy.90.refs_13_
  649.7 83.6 %shard_map.370 = (f32[512,1536]{1,0:T(8,128)}, bf16[512,1536]{1,0:T(8,128)(2,1)}, f32[2,512,384]{2,1,0:T(8,128)}, bf16[512,384]{1,0:T(8,128)(2,1)}, f32[8,1536]{...) custom-call(f32[512,1536]{1,0:T(8,128)} %get-tuple-element.349.refs_0_, ...), custom_call_target="tpu_custom_call" | custom-call | bytes 180000000 | tf_op jit(solution)/shard_map/pallas_call | solution.py:561
  733.3 36.6 %shard_map.371 = (f32[512,1536]{1,0:T(8,128)}, bf16[512,1536]{1,0:T(8,128)(2,1)}, f32[8,1536]{1,0:T(8,128)}, f32[512,384]{1,0:T(8,128)}, f32[2,512,384]{2,1,0:T(8,128)}, /*index=5*/f32[2,128,384]{2,1,0:T(8,128)}) custom-call(f32[4,8,512]{2,1,0:T(8,128)} %get-tuple-element.158.refs_0_, f32[512,1536]{1,0:T(8,128)} %get-tuple-element.204.refs_1_, ...), custom_call_target="tpu_custom_call" | custom-call | bytes 105000000 | tf_op jit(solution)/shard_map/pallas_call | solution.py:561
  778.0 63.5 %shard_map.372 = (bf16[512,1152]{1,0:T(8,128)(2,1)}, bf16[128,768]{1,0:T(8,128)(2,1)}, f32[16,384]{1,0:T(8,128)}, bf16[512,1536]{1,0:T(8,128)(2,1)}, f32[192,384]{1,0:T(8,128)}, /*index=5*/f32[192,384]{1,0:T(8,128)}) custom-call(f32[512,384]{1,0:T(8,128)} %get-tuple-element.210.refs_0_, f32[2,512,384]{2,1,0:T(8,128)} %get-tuple-element.211.refs_1_, ...), custom_call_target="tpu_custom_call" | custom-call | bytes 150000000 | tf_op jit(solution)/shard_map/pallas_call | solution.py:561
  844.7 7.6 shard_map.373
  856.4 70.6 %shard_map.374 = (bf16[512,1536]{1,0:T(8,128)(2,1)}, bf16[512,2240]{1,0:T(8,128)(2,1)}, bf16[512,1536]{1,0:T(8,128)(2,1)}, f32[8,1536]{1,0:T(8,128)}, f32[8,2240...) custom-call(f32[512,1536]{1,0:T(8,128)} %get-tuple-element.223.refs_0_, ...), custom_call_target="tpu_custom_call" | custom-call | bytes 165000000 | tf_op jit(solution)/shard_map/pallas_call | solution.py:561
  927.0 7.4 convolution_convert_fusion
  934.3 10.2 copy.94.refs_14_
  944.5 7.2 convolution_convert_fusion.1
  951.7 9.7 copy.93.refs_13_
  961.5 82.2 %shard_map.375 = (f32[512,1536]{1,0:T(8,128)}, bf16[512,1536]{1,0:T(8,128)(2,1)}, f32[2,512,384]{2,1,0:T(8,128)}, bf16[512,384]{1,0:T(8,128)(2,1)}, f32[8,1536]{...) custom-call(f32[512,1536]{1,0:T(8,128)} %get-tuple-element.223.refs_0_, ...), custom_call_target="tpu_custom_call" | custom-call | bytes 180000000 | tf_op jit(solution)/shard_map/pallas_call | solution.py:561
  1043.6 37.2 %shard_map.376 = (f32[512,1536]{1,0:T(8,128)}, bf16[512,1536]{1,0:T(8,128)(2,1)}, f32[8,1536]{1,0:T(8,128)}, f32[512,384]{1,0:T(8,128)}, f32[2,512,384]{2,1,0:T(8,128)}, /*index=5*/f32[2,128,384]{2,1,0:T(8,128)}) custom-call(f32[4,8,512]{2,1,0:T(8,128)} %get-tuple-element.158.refs_0_, f32[512,1536]{1,0:T(8,128)} %get-tuple-element.238.refs_1_, ...), custom_call_target="tpu_custom_call" | custom-call | bytes 105000000 | tf_op jit(solution)/shard_map/pallas_call | solution.py:561
  1088.9 63.2 %shard_map.377 = (bf16[512,1152]{1,0:T(8,128)(2,1)}, bf16[128,768]{1,0:T(8,128)(2,1)}, f32[16,384]{1,0:T(8,128)}, bf16[512,1536]{1,0:T(8,128)(2,1)}, f32[192,384...) custom-call(f32[512,384]{1,0:T(8,128)} %get-tuple-element.244.refs_0_, ...), custom_call_target="tpu_custom_call" | custom-call | bytes 150000000 | tf_op jit(solution)/shard_map/pallas_call | solution.py:561
  1152.2 7.6 shard_map.378
  1189.4 23.1 %all-reduce = (bf16[2,24,384]{2,1,0:T(8,128)(2,1)S(1)}, bf16[2,2240]{1,0:T(2,128)(2,1)S(1)}) all-reduce(bf16[2,24,384]{2,1,0:T(8,128)(2,1)S(1)} %bitcast.175, bf16[2,2240]{1,0:T(2,128)(2,1)S(1)} %pad_maximum_fusion.9), channel_id=1, replica_groups=mesh['dp'=8,'tensor'=4] {'dp'}, use_global_device_ids=true, to_apply=%region_6.7 | all-reduce | flops 22912 | bytes 91648 | tf_op jit(solution)/shard_map/psum | solution.py:1872
  1223.5 32.9 %shard_map.379 = (f32[192,1152]{1,0:T(8,128)}, f32[192,768]{1,0:T(8,128)}) custom-call(bf16[1536,1152]{1,0:T(8,128)(2,1)} %convolution_convert_fusion.4.refs_0_, bf16[1536,768]{1,0:T(8,128)(2,1)} %fusion.1.refs_1_), custom_call_target="tpu_custom_call" | custom-call | bytes 120000000 | tf_op jit(solution)/shard_map/pallas_call | solution.py:561
  (195 shorter events, 96.6 us)
Async XLA Ops:
  7.2 34.9 %copy-start.33 = (f32[128]{0:T(128)S(1)}, f32[128]{0:T(128)}, u32[]{:S(2)}) copy-start(f32[128]{0:T(128)} %constant.41) | copy-start | bytes 1540
  7.2 34.9 %copy-start.34 = (f32[128]{0:T(128)S(1)}, f32[128]{0:T(128)}, u32[]{:S(2)}) copy-start(f32[128]{0:T(128)} %constant.40) | copy-start | bytes 1540
  7.2 34.9 %copy-start.35 = (f32[128]{0:T(128)S(1)}, f32[128]{0:T(128)}, u32[]{:S(2)}) copy-start(f32[128]{0:T(128)} %constant.39) | copy-start | bytes 1540
  7.2 1263.9 %all-reduce.4.cloned.1.call-start = ((), (), s32[]{:S(2)}) async-start(), calls=%async_computation | async-start | bytes 245760 | tf_op jit(solution)/shard_map/psum | solution.py:1872
  475.1 67.8 %copy-start.8 = (bf16[512,1536]{1,0:T(8,128)(2,1)S(1)}, bf16[512,1536]{1,0:T(8,128)(2,1)}, u32[]{:S(2)}) copy-start(bf16[512,1536]{1,0:T(8,128)(2,1)} %param.26) | copy-start | bytes 4718596
  549.6 65.5 %copy-start.37 = (bf16[512,2240]{1,0:T(8,128)(2,1)S(1)}, bf16[512,2240]{1,0:T(8,128)(2,1)}, u32[]{:S(2)}) copy-start(bf16[512,2240]{1,0:T(8,128)(2,1)} %get-tuple-element.203) | copy-start | bytes 6881284
  622.4 9.9 copy-start.39
  733.3 36.6 %copy-start.14 = (bf16[512,384]{1,0:T(8,128)(2,1)S(1)}, bf16[512,384]{1,0:T(8,128)(2,1)}, u32[]{:S(2)}) copy-start(bf16[512,384]{1,0:T(8,128)(2,1)} %get-tuple-element.181.refs_0_) | copy-start | bytes 1179652
  769.9 3.6 copy-start.42
  769.9 3.6 copy-start.49
  778.0 63.5 %copy-start.2 = (bf16[128,1536]{1,0:T(8,128)(2,1)S(1)}, bf16[128,1536]{1,0:T(8,128)(2,1)}, u32[]{:S(2)}) copy-start(bf16[128,1536]{1,0:T(8,128)(2,1)} %refs_3_.2) | copy-start | bytes 1179652
  844.7 7.6 copy-start.41
  844.7 7.6 copy-start.45
  856.4 70.6 %copy-start.36 = (bf16[512,2240]{1,0:T(8,128)(2,1)S(1)}, bf16[512,2240]{1,0:T(8,128)(2,1)}, u32[]{:S(2)}) copy-start(bf16[512,2240]{1,0:T(8,128)(2,1)} %get-tuple-element.237) | copy-start | bytes 6881284
  934.3 10.2 copy-start.38
  1043.6 37.2 %copy-start.13 = (bf16[512,384]{1,0:T(8,128)(2,1)S(1)}, bf16[512,384]{1,0:T(8,128)(2,1)}, u32[]{:S(2)}) copy-start(bf16[512,384]{1,0:T(8,128)(2,1)} %get-tuple-element.161.refs_0_) | copy-start | bytes 1179652
  1080.8 3.6 copy-start.40
  1080.8 3.6 copy-start.48
  1152.1 8.5 copy-start.27
  1152.2 8.5 copy-start.26
  1152.2 8.5 copy-start.25
  1152.2 8.6 copy-start.24
  1152.2 8.6 copy-start.23
  1152.2 8.6 copy-start.22
  1152.2 8.6 copy-start.21
  1152.2 29.7 %copy-start = (bf16[3,1536,384]{2,1,0:T(8,128)(2,1)S(1)}, bf16[3,1536,384]{2,1,0:T(8,128)(2,1)}, u32[]{:S(2)}) copy-start(bf16[3,1536,384]{2,1,0:T(8,128)(2,1)} %get-tuple-element.183.refs_3_.refs_4_.refs_12_) | copy-start | bytes 10616836
  1181.9 96.6 %all-reduce.6.cloned.1.call-start = ((), (), s32[]{:S(2)}) async-start(), calls=%async_computation.1 | async-start | bytes 786432 | tf_op jit(solution)/shard_map/psum | solution.py:1880
  1185.5 3.8 copy-start.31
  1185.5 3.8 copy-start.29
  1185.5 27.0 %copy-start.3 = (bf16[128,1536]{1,0:T(8,128)(2,1)S(1)}, bf16[128,1536]{1,0:T(8,128)(2,1)}, u32[]{:S(2)}) copy-start(bf16[128,1536]{1,0:T(8,128)(2,1)} %refs_3_.2) | copy-start | bytes 1179652
  1185.5 27.0 %copy-start.11 = (bf16[128,768]{1,0:T(8,128)(2,1)S(1)}, bf16[128,768]{1,0:T(8,128)(2,1)}, u32[]{:S(2)}) copy-start(bf16[128,768]{1,0:T(8,128)(2,1)} %get-tuple-element.267) | copy-start | bytes 589828
  1186.8 28.6 %copy-start.12 = (f32[192,768]{1,0:T(8,128)S(1)}, f32[192,768]{1,0:T(8,128)}, u32[]{:S(2)}) copy-start(f32[192,768]{1,0:T(8,128)} %get-tuple-element.275) | copy-start | bytes 1769476
  (20 other events, 43.8 us)
Sparse Core Ops, SparseCore 0:
  1182.0 52.9 all-reduce.3
  1238.1 36.8 all-reduce.5

commit v2 on v1

--- a/solution.py
+++ b/solution.py
@@ -9,6 +9,48 @@
 from jax.experimental.pallas import tpu as pltpu
 from jax.sharding import PartitionSpec as P
 
+BIAS = "bias"
+BRANCH = "branch"
+CONTEXT = "context"
+COSINE = "cosine"
+CROSS = "cross"
+DOWN = "down"
+DP = "dp"
+GAIN = "gain"
+GELU_B_NAME = "gelu_b"
+GRAD = "grad"
+HIDDEN = "hidden"
+HIDDEN_F = "hidden_f"
+KEY = "key"
+KEY_VALUE = "key_value"
+LOSS = "loss"
+MATRIX_GRAD = "matrix_grad"
+NEW_GRAD = "new_grad"
+NORMAL = "normal"
+NORMAL_F = "normal_f"
+OTHERS = "others"
+OUT = "out"
+OUT0 = "out0"
+OUTPUT = "output"
+QUERY = "query"
+QUERY_B = "query_b"
+QUERY_GRAD = "query_grad"
+QUERY_ROT = "query_rot"
+RESULT = "result"
+SELF = "self"
+SELF_GRAD = "self_grad"
+SHIFT = "shift"
+SINE = "sine"
+SLOPE = "slope"
+TENSOR = "tensor"
+TEXT = "text"
+TEXT_GRAD = "text_grad"
+TEXT_KB = "text_kb"
+TEXT_MATRIX = "text_matrix"
+TEXT_VB = "text_vb"
+TEXT_WEIGHT = "text_weight"
+UP = "up"
+WEIGHT = "weight"
 MESH = pl.DeviceIdType.MESH
 F32, BF16 = jnp.float32, jnp.bfloat16
 NN = (((1,), (0,)), ((), ()))
@@ -44,17 +86,6 @@
     return table
 
 
-def rope_angles(positions, head_size):
-    table = rope_table(head_size)
-    places = positions.astype(F32)
-    angles = (
-        places[0][:, None] * table[0][None, :]
-        + places[1][:, None] * table[1][None, :]
-        + places[2][:, None] * table[2][None, :]
-    )
-    return (jnp.cos(angles), jnp.sin(angles))
-
-
 def signal(**device):
     pl.semaphore_signal(
         pltpu.get_barrier_semaphore(), inc=1, device_id=device, device_id_type=MESH
@@ -62,7 +93,7 @@
 
 
 def bits_of_dp():
-    return max(lax.axis_size("dp").bit_length() - 1, 1)
+    return max(lax.axis_size(DP).bit_length() - 1, 1)
 
 
 def flip(index, mask):
@@ -76,7 +107,7 @@
 
 
 def greet(tensor, masks):
-    place, me = lax.axis_index("tensor"), lax.axis_index("dp")
+    place, me = lax.axis_index(TENSOR), lax.axis_index(DP)
     if tensor:
         for step in range(1, CHAIN):
             signal(tensor=lax.rem(place + step, CHAIN))
@@ -88,7 +119,7 @@
 
 
 def holders():
-    me = lax.axis_index("dp")
+    me = lax.axis_index(DP)
     return flip(me, 1), flip(me, 2)
 
 
@@ -120,14 +151,30 @@
     return (rising, rising[::-1])
 
 
-class Gather:
-    def __init__(self, source, layer):
-        self.layer = layer
+class Job:
+    phase = 0
+    wave = 0
+    name = None
+    ended = False
+    midway = False
+
+    def middle(self):
+        pass
+
+    def move(self, target):
+        while self.phase < min(target, self.bits - 1):
+            self.phase += 1
+            self.advance(self.phase)
+
+
+class Gather(Job):
+    def __init__(self, source, layer, name=None, wave=0, held=False):
+        self.layer, self.name, self.wave, self.is_held = layer, name, wave, held
         self.operands = [source]
         shape = source.shape[1:]
         self.lead = shape[:-2]
         self.size = shape[-2]
-        devices = lax.axis_size("dp")
+        devices = lax.axis_size(DP)
         self.outs = [(self.lead + (self.size * devices, shape[-1]), source.dtype)]
         self.spaces = [pl.ANY]
         self.bits = bits_of_dp()
@@ -145,14 +192,24 @@
             pltpu.SemaphoreType.DMA((count,)),
             pltpu.SemaphoreType.DMA,
         ]
+        if held:
+            self.scratch += [
+                pltpu.VMEM(self.outs[0][0], source.dtype),
+                pltpu.SemaphoreType.DMA,
+            ]
 
     def key(self):
-        return ("gather", self.layer, self.outs[0][0])
+        return ("gather", self.layer, self.outs[0][0], self.wave, self.is_held)
 
     def bind(self, sources, outs, scratch):
         self.source = sources[0].at[self.layer]
         self.out = outs[0]
-        self.send_sems, self.recv_sems, self.own_sem = scratch
+        self.send_sems, self.recv_sems, self.own_sem = scratch[:3]
+        self.store = None
+        if self.is_held:
+            held, sem = scratch[3:]
+            self.store = pltpu.make_async_copy(held, self.out, sem)
+            self.out = held
 
     def block(self, ref, index, half):
         low, size = (0, self.size) if half is None else halves_of(self.size)[half]
@@ -160,9 +217,11 @@
         rows = pl.ds(pl.multiple_of(start, 16), size)
         return ref.at[:, rows] if self.lead else ref.at[rows]
 
-    def copies(self, phase, own=None):
-        me = lax.axis_index("dp")
+    def copies(self, phase, own=None, only=None):
+        me = lax.axis_index(DP)
         for number, (step, half, bit, mask) in enumerate(self.plan):
+            if only is not None and mask not in only:
+                continue
             if step == phase and own in (None, mask == 0):
                 index = flip(me, mask)
                 source = (
@@ -179,7 +238,7 @@
                 )
 
     def own_copy(self):
-        me = lax.axis_index("dp")
+        me = lax.axis_index(DP)
         return pltpu.make_async_copy(
             self.source, self.block(self.out, me, None), self.own_sem
         )
@@ -190,7 +249,22 @@
                 copy.start()
         self.own_copy().start()
 
+    def middle(self):
+        if self.bits == 3 and not self.midway:
+            self.midway = True
+            for copy in self.copies(1, True):
+                copy.wait_recv()
+            for copy in self.copies(2, only=(2, 4)):
+                copy.start()
+
     def advance(self, phase):
+        if phase == self.bits - 1 == 2:
+            self.middle()
+            for copy in self.copies(1, False):
+                copy.wait_recv()
+            for copy in self.copies(2, only=(6,)):
+                copy.start()
+            return
         for copy in self.copies(phase - 1):
             copy.wait_recv()
         for copy in self.copies(phase, False):
@@ -203,14 +277,18 @@
             for copy in self.copies(phase):
                 copy.wait_send()
         self.own_copy().wait()
-
-
-class Scatter:
-    def __init__(self, source):
-        self.operands = [source]
+        if self.store is not None:
+            self.store.start()
+
+
+class Scatter(Job):
+    def __init__(self, source=None, name=None, shape=None):
+        self.name = name
+        self.operands = [] if source is None else [source]
+        shape = source.shape if shape is None else shape
         self.bits = bits_of_dp()
-        self.size = source.shape[0] // lax.axis_size("dp")
-        self.width = source.shape[1]
+        self.size = shape[0] // lax.axis_size(DP)
+        self.width = shape[1]
         self.outs = [((self.size, self.width), F32)]
         self.spaces = [pltpu.VMEM]
         self.slots = 1 << self.bits - 1
@@ -223,7 +301,8 @@
                     plan.append((phase + 1, half, bit, mask, place))
         self.plan = plan
         count = len(plan)
-        buffers = [pltpu.VMEM((self.slots, self.size, self.width), BF16)] * 2
+        buffers = [pltpu.VMEM((self.slots, self.size, self.width), BF16)]
+        buffers += buffers * len(self.operands)
         for phase in range(1, self.bits):
             places = 1 << self.bits - 1 - phase
             buffers += [
@@ -237,19 +316,29 @@
         ]
 
     def key(self):
-        return ("scatter", self.width)
+        return ("scatter", self.width, len(self.operands))
 
     def bind(self, sources, outs, scratch):
-        self.source, self.out = sources[0], outs[0]
-        self.held, self.landed = scratch[:2]
-        self.parts = scratch[2:-3]
+        self.out = outs[0]
+        self.landed, self.own = scratch[0], None
+        scratch = scratch[1:]
+        if sources:
+            self.source, self.own = sources[0], scratch[0]
+            scratch = scratch[1:]
+        self.parts = scratch[:-3]
         self.send_sems, self.recv_sems, self.own_sems = scratch[-3:]
 
     def rows(self, index):
         return pl.ds(pl.multiple_of(index * self.size, 16), self.size)
 
+    def held(self, mask, low, size):
+        if self.own is not None:
+            return self.own.at[mask >> 1, pl.ds(pl.multiple_of(low, 16), size)]
+        start = flip(lax.axis_index(DP), mask) * self.size + low
+        return self.source.at[pl.ds(pl.multiple_of(start, 16), size)]
+
     def copies(self, phase):
-        me = lax.axis_index("dp")
+        me = lax.axis_index(DP)
         for number, (step, half, bit, mask, place) in enumerate(self.plan):
             if step != phase:
                 continue
@@ -258,7 +347,7 @@
                 target = self.landed.at[mask >> 1]
             else:
                 low, size = halves_of(self.size)[half]
-                source = self.held.at[(mask | 1 << bit) >> 1, pl.ds(low, size)]
+                source = self.held(mask | 1 << bit, low, size)
                 target = self.parts[2 * (phase - 1) + half].at[place]
             yield send(
                 source,
@@ -269,13 +358,14 @@
             )
 
     def own_copies(self):
-        me = lax.axis_index("dp")
-        for slot in range(self.slots):
-            yield pltpu.make_async_copy(
-                self.source.at[self.rows(flip(me, slot << 1))],
-                self.held.at[slot],
-                self.own_sems.at[slot],
-            )
+        me = lax.axis_index(DP)
+        if self.own is not None:
+            for slot in range(self.slots):
+                yield pltpu.make_async_copy(
+                    self.source.at[self.rows(flip(me, slot << 1))],
+                    self.own.at[slot],
+                    self.own_sems.at[slot],
+                )
 
     def start(self):
         for copy in self.copies(0):
@@ -292,7 +382,8 @@
             for slot in range(self.slots):
 
                 def step(rows, index, slot=slot):
-                    self.held[slot, rows] = self.held[slot, rows] + self.landed[slot, rows]
+                    held = self.held(slot << 1, index * 16, 16)
+                    held[...] = held[...] + self.landed[slot, rows]
 
                 loop_rows(self.size, 16, step)
             return
@@ -301,20 +392,15 @@
                 low, size = halves_of(self.size)[half]
                 part = self.parts[2 * (phase - 1) + half]
 
-                def step(index, carry, mask=mask, place=place, low=low, part=part):
-                    near = pl.ds(pl.multiple_of(index * 16, 16), 16)
-                    rows = pl.ds(pl.multiple_of(low + index * 16, 16), 16)
+                def step(rows, index, mask=mask, place=place, low=low, part=part):
+                    held = self.held(mask, low + index * 16, 16)
                     if phase == self.bits - 1:
-                        self.out[rows] = self.held[0, rows].astype(F32) + part[place, near].astype(
-                            F32
-                        )
+                        target = pl.ds(pl.multiple_of(low + index * 16, 16), 16)
+                        self.out[target] = held[...].astype(F32) + part[place, rows].astype(F32)
                     else:
-                        self.held[mask >> 1, rows] = (
-                            self.held[mask >> 1, rows] + part[place, near]
-                        )
-                    return carry
-
-                lax.fori_loop(0, size // 16, step, 0)
+                        held[...] = held[...] + part[place, rows]
+
+                loop_rows(size, 16, step)
 
     def advance(self, phase):
         self.add(phase - 1)
@@ -328,43 +414,97 @@
                 copy.wait_send()
 
 
+class Late:
+    def __init__(self, name, value, low=None, high=None):
+        self.name, self.value, self.low, self.high = name, value, low, high
+        shape = value.shape
+        if high is not None:
+            shape = (high - low,) + shape[1:]
+        elif low is not None:
+            shape = shape[1:]
+        self.scratch = [pltpu.VMEM(shape, value.dtype), pltpu.SemaphoreType.DMA]
+
+    def source(self, ref):
+        if self.high is not None:
+            return ref.at[self.low : self.high]
+        return ref if self.low is None else ref.at[self.low]
+
+
+class Early:
+    def __init__(self, name, shape, kind, over=None):
+        self.name, self.shape, self.kind, self.over = name, shape, kind, over
+        self.scratch = [pltpu.SemaphoreType.DMA]
+        if over is None:
+            self.scratch = [pltpu.VMEM(shape, kind)] + self.scratch
+
+
 class Side:
     def __init__(self, jobs):
         self.jobs = jobs
         self.masks = [1 << bit for bit in range(bits_of_dp())] if jobs else []
-
-    def start(self):
+        self.loads, self.stores, self.open = {}, {}, []
+        self.first_loads = []
+
+    def need(self, *names):
+        for name in names:
+            self.loads[name].wait()
+
+    def store(self, *names):
+        for name in names:
+            self.stores[name].start()
+            self.open.append(name)
+
+    def start(self, wave=0):
         for job in self.jobs:
-            job.start()
+            if job.operands and job.wave == wave:
+                job.start()
+        while self.first_loads:
+            self.first_loads.pop(0).wait()
+
+    def launch(self, name, source):
+        for job in self.jobs:
+            if job.name == name:
+                job.source = source
+                job.start()
+
+    def move(self, target, *names):
+        for job in self.jobs:
+            if not names or job.name in names:
+                job.move(target)
 
     def early(self):
-        for phase in range(1, bits_of_dp() - 1):
-            for job in self.jobs:
-                job.advance(phase)
-
-    def early_first(self):
-        if bits_of_dp() > 2:
-            for job in self.jobs:
-                job.advance(1)
-
-    def early_rest(self):
-        for phase in range(2, bits_of_dp() - 1):
-            for job in self.jobs:
-                job.advance(phase)
+        self.move(bits_of_dp() - 2)
 
     def late(self):
+        self.move(bits_of_dp() - 1)
+
+    def middle(self):
+        self.early()
         for job in self.jobs:
-            job.advance(bits_of_dp() - 1)
-
-    def finish(self):
+            job.middle()
+
+    def finish(self, *names):
         for job in self.jobs:
-            job.finish()
+            if not job.ended and (not names or job.name in names):
+                job.move(job.bits - 1)
+                job.finish()
+                job.ended = True
+
+    def close(self):
+        for name in self.stores:
+            if name not in self.open:
+                self.store(name)
+        for copy in self.stores.values():
+            copy.wait()
+        for job in self.jobs:
+            if isinstance(job, Gather) and job.store is not None:
+                job.store.wait()
 
 
 class Exchange:
     def __init__(self, slots, send_sems, recv_sems):
         self.slots = slots
-        place = lax.axis_index("tensor")
+        place = lax.axis_index(TENSOR)
         self.place = place
         self.copies = [
             send(
@@ -407,13 +547,14 @@
         self.part, self.total = part, total
         self.came, self.pair, self.peers = buffers
         self.sems = sems
-        place = lax.axis_index("tensor")
+        place = lax.axis_index(TENSOR)
         self.is_end = (place == 0) | (place == 3)
         self.is_mid = jnp.logical_not(self.is_end)
         self.inner = jnp.where(place == 0, 1, 2)
         self.outer = jnp.where(place == 1, 0, 3)
         self.peer = 3 - place
         self.chunks = part.shape[0] // CHUNK
+        self.closed = False
 
     @staticmethod
     def scratch(rows, width):
@@ -486,8 +627,10 @@
                 return carry
 
             lax.fori_loop(low, high, both, 0)
-            if high == self.chunks:
+            if high == self.chunks and not self.closed:
                 self.second(self.chunks - 1)
+
+        self.closed = self.closed or high == self.chunks
 
         @pl.when(self.is_end)
         def _():
@@ -511,7 +654,9 @@
             low, done = cut, cut - 1
             late()
         self.segment(low, last, done, last)
-
+        self.close()
+
+    def close(self):
         @pl.when(self.is_mid)
         def _():
             def close(k, carry):
@@ -532,13 +677,22 @@
 def run(name, kernel, ins, outs, scratch=(), remote=True, jobs=(), scalars=0, micros=0):
     whole = pl.BlockSpec(memory_space=pltpu.VMEM)
     far = pl.BlockSpec(memory_space=pl.ANY)
+    if remote:
+        ins = tuple(ins[:scalars]) + tuple(
+            item if isinstance(item, Late) else Late(None, item) for item in ins[scalars:]
+        )
+        outs = tuple(
+            item if isinstance(item, Early) or len(item) > 2 else Early(place, *item)
+            for place, item in enumerate(outs)
+        )
     job_ins = [item for job in jobs for item in job.operands]
     job_outs = [item for job in jobs for item in job.outs]
     job_spaces = [pl.BlockSpec(memory_space=space) for job in jobs for space in job.spaces]
-    job_scratch = [item for job in jobs for item in job.scratch]
-    side = Side(jobs)
+    moved = [item for item in tuple(ins) + tuple(outs) if isinstance(item, (Late, Early))]
+    own_scratch = list(scratch) + [item for job in jobs for item in job.scratch]
 
     def body(*refs):
+        side = Side(jobs)
         refs = list(refs)
 
         def take(count):
@@ -548,24 +702,47 @@
 
         own_in, side_in = take(len(ins)), take(len(job_ins))
         own_out, side_out = take(len(outs)), take(len(job_outs))
-        own_scratch = take(len(scratch))
+        own = take(len(scratch))
         for job in jobs:
+            job.phase, job.ended, job.midway = 0, False, False
             job.bind(
                 [side_in.pop(0) for _ in job.operands],
                 [side_out.pop(0) for _ in job.outs],
                 take(len(job.scratch)),
             )
-        kernel(side, *own_in, *own_out, *own_scratch)
+        for place, item in enumerate(ins):
+            if isinstance(item, Late):
+                held, sem = take(2)
+                copy = pltpu.make_async_copy(item.source(own_in[place]), held, sem)
+                copy.start()
+                if item.name is None:
+                    side.first_loads.append(copy)
+                side.loads[item.name] = copy
+                own_in[place] = held
+        for place, item in enumerate(outs):
+            if isinstance(item, Early):
+                held = take(1)[0] if item.over is None else own_in[item.over]
+                sem = take(1)[0]
+                side.stores[item.name] = pltpu.make_async_copy(held, own_out[place], sem)
+                own_out[place] = held
+        kernel(side, *own_in, *own_out, *own)
+        side.close()
 
     key = (name,) + tuple(job.key() for job in jobs)
+    shapes = [
+        (item.shape, item.kind) if isinstance(item, Early) else item[:2] for item in outs
+    ] + job_outs
     results = pl.pallas_call(
         body,
-        out_shape=tuple(jax.ShapeDtypeStruct(shape, kind) for shape, kind in outs + tuple(job_outs)),
+        out_shape=tuple(jax.ShapeDtypeStruct(shape, kind) for shape, kind in shapes),
         in_specs=[pl.BlockSpec(memory_space=pltpu.SMEM)] * scalars
-        + [whole] * (len(ins) - scalars)
+        + [far if isinstance(item, Late) else whole for item in ins[scalars:]]
         + [far] * len(job_ins),
-        out_specs=tuple([whole] * len(outs) + job_spaces),
-        scratch_shapes=list(scratch) + job_scratch,
+        out_specs=tuple(
+            [far if isinstance(item, Early) or len(item) > 2 else whole for item in outs]
+            + job_spaces
+        ),
+        scratch_shapes=own_scratch + [part for item in moved for part in item.scratch],
         cost_estimate=pl.CostEstimate(
             flops=0, bytes_accessed=micros * 3000000, transcendentals=0
         ),
@@ -574,8 +751,15 @@
             has_side_effects=remote,
             vmem_limit_bytes=VMEM_BYTES,
         ),
-    )(*ins, *job_ins)
+    )(*[item.value if isinstance(item, Late) else item for item in ins], *job_ins)
     return results[: len(outs)], results[len(outs) :]
+
+
+def tiled_grad(left, right, store, serve, size=384):
+    for tile in range(left.shape[1] // size):
+        cols = slice(tile * size, (tile + 1) * size)
+        store(tile, size, dot(left[:, cols], right[...], TN).astype(BF16))
+        serve(tile)
 
 
 def normed(hidden):
@@ -644,14 +828,18 @@
     key_bias,
     norm_gains,
     ffn_bias,
+    positions,
+    table,
     counts,
+    cosine,
+    sine,
     *rest,
 ):
     packs, (send_sems, recv_sems) = rest[:-2], rest[-2:]
     greet(False, side.masks)
     near, far = holders()
     tokens = counts.shape[2]
-    clip = lax.axis_index("dp") // HOLD
+    clip = lax.axis_index(DP) // HOLD
     mine = (lengths[clip] - block_order[0] * tokens).astype(F32)
     counts[0] = jnp.full(counts.shape[1:], mine, F32)
 
@@ -672,14 +860,23 @@
         rows_d, rows_w, rows_f = packs[3 * layer : 3 * layer + 3]
         rows_d[...] = jnp.zeros(rows_d.shape, F32)
         rows_w[...] = jnp.zeros(rows_w.shape, F32)
-        rows_d[MODS : MODS + 6] = modulation[layer] + time_embed[clip]
-        rows_d[OUT_BIAS : OUT_BIAS + 3] = out_bias[layer]
+        for row in range(6):
+            embed = jnp.zeros((1, rows_d.shape[1]), F32)
+            for index in range(time_embed.shape[1]):
+                embed = embed + jnp.where(clip == index, row_of(time_embed.at[row], index), 0.0)
+            rows_d[row : row + 1] = row_of(modulation.at[row], layer) + embed
+        for row in range(3):
+            rows_d[OUT_BIAS + row : OUT_BIAS + row + 1] = row_of(out_bias.at[row], layer)
         rows_d[CROSS_GAIN : CROSS_GAIN + 1] = row_of(cross_gain, layer)
         rows_d[CROSS_SHIFT : CROSS_SHIFT + 1] = row_of(cross_shift, layer)
-        rows_w[0:5] = proj_bias[layer]
+        for row in range(5):
+            rows_w[row : row + 1] = row_of(proj_bias.at[row], layer)
         rows_w[KEY_BIAS : KEY_BIAS + 1] = row_of(key_bias, layer)
         rows_w[GAINS : GAINS + 4] = norm_gains[layer]
         rows_f[...] = row_of(ffn_bias, layer)
+    angles = dot(positions[...].astype(F32), table[...], TN, exact=True)
+    cosine[...] = jnp.cos(angles)
+    sine[...] = jnp.sin(angles)
     to_far.wait_recv()
     onward.start()
     side.early()
@@ -695,7 +892,7 @@
     return base + (tot.astype(F32) + bias_row) * gate_row
 
 
-def qkv_kernel(
+def attend_kernel(
     first,
     side,
     base,
@@ -706,17 +903,16 @@
     weight,
     cosine,
     sine,
-    hidden,
-    normal,
-    query,
-    key,
-    query_rot,
-    key_value,
-    slots,
-    send_sems,
-    recv_sems,
+    counts,
+    *refs,
 ):
-    greet(True, side.masks)
+    refs = list(refs)
+    context = refs.pop(0) if first else None
+    hidden, normal, query, key, query_rot, key_value, slots = refs[:7]
+    others, result, lse = refs[7:10]
+    clip_context = refs[10] if first else None
+    scores, send_sems, recv_sems, hold_sends, hold_recvs = refs[-5:]
+    greet(True, side.masks or [1, 2])
     side.start()
     tokens, width = query.shape
     features = hidden.shape[1]
@@ -740,48 +936,18 @@
         for head in range(heads):
             key_value[head, 1, rows] = value[:, head_cols(head)]
 
+    side.need(WEIGHT)
     loop_rows(tokens, 256, project)
+    side.store(HIDDEN, NORMAL, QUERY, KEY)
     exchange = Exchange(slots, send_sems, recv_sems)
     exchange.start(
         stat_rows(query[...] * query[...], 0) + stat_rows(key[...] * key[...], 1)
     )
     side.early()
-    exchange.finish()
-    query_inv = inverse_rms(stat_column(slots, 0, HEAD_DIM), features)
-    key_inv = inverse_rms(stat_column(slots, 1, HEAD_DIM), features)
-    for head in range(heads):
-        cols = head_cols(head)
-        rows = query[:, cols] * query_inv * rows_w[GAINS : GAINS + 1, cols]
-        query_rot[:, cols] = (rows * cosine[...] + turned(rows) * sine[...]).astype(BF16)
-        rows = key[:, cols] * key_inv * rows_w[GAINS + 1 : GAINS + 2, cols]
-        key_value[head, 0] = (rows * cosine[...] + turned(rows) * sine[...]).astype(BF16)
-    side.late()
-    side.finish()
-
-
-def below(counts, slot, shape):
-    index = lax.broadcasted_iota(jnp.int32, shape, 0).astype(F32)
-    return index < counts[slot, 0:1]
-
-
-def softmax_back(scores, lse_row, mask):
-    probs = jnp.exp2(scores * (SCALE * LOG2E) - lse_row)
-    return probs if mask is None else jnp.where(mask, probs, 0.0)
-
-
-def attend_kernel(with_context, side, counts, query, key_value, *refs):
-    refs = list(refs)
-    context = refs.pop(0) if with_context else None
-    others, result, lse = refs[:3]
-    clip_context = refs[3] if with_context else None
-    scores, send_sems, recv_sems = refs[-3:]
-    greet(False, [1, 2])
     near, far = holders()
-    tokens, width = query.shape
-    heads = width // HEAD_DIM
 
     def copy(source, target, number, device):
-        return send(source, target, send_sems.at[number], recv_sems.at[number], dp=device)
+        return send(source, target, hold_sends.at[number], hold_recvs.at[number], dp=device)
 
     to_near = copy(key_value, others.at[0], 0, near)
     to_far = [
@@ -791,12 +957,19 @@
         copy(others.at[1, head], others.at[2, head], 1 + heads + head, near)
         for head in range(heads)
     ]
-    for item in to_far:
-        item.start()
+    exchange.finish()
+    query_inv = inverse_rms(stat_column(slots, 0, HEAD_DIM), features)
+    key_inv = inverse_rms(stat_column(slots, 1, HEAD_DIM), features)
+    side.need(COSINE, SINE)
+    for head in range(heads):
+        cols = head_cols(head)
+        rows = key[:, cols] * key_inv * rows_w[GAINS + 1 : GAINS + 2, cols]
+        key_value[head, 0] = (rows * cosine[...] + turned(rows) * sine[...]).astype(BF16)
+        to_far[head].start()
     to_near.start()
     text = []
-    if with_context:
-        place = lax.rem(lax.axis_index("dp"), HOLD)
+    if first:
+        place = lax.rem(lax.axis_index(DP), HOLD)
         size = context.shape[0]
 
         def block(index):
@@ -811,9 +984,15 @@
         ]
         text[0].start()
         text[1].start()
+    for head in range(heads):
+        cols = head_cols(head)
+        rows = query[:, cols] * query_inv * rows_w[GAINS : GAINS + 1, cols]
+        query_rot[:, cols] = (rows * cosine[...] + turned(rows) * sine[...]).astype(BF16)
+    side.store(QUERY_ROT)
+    side.middle()
 
     def score(head, slot, keys):
-        block = dot(keys, query[:, head_cols(head)], NT) * (SCALE * LOG2E)
+        block = dot(keys, query_rot[:, head_cols(head)], NT) * (SCALE * LOG2E)
         scores[head, slot] = jnp.where(below(counts, slot, block.shape), block, -1e30)
 
     for head in range(heads):
@@ -825,6 +1004,8 @@
     for head in range(heads):
         to_far[head].wait_recv()
         onward[head].start()
+        if head == 0:
+            side.late()
         score(head, 2, others[1, head, 0])
         onward[head].wait_recv()
         score(head, 3, others[2, head, 0])
@@ -840,13 +1021,24 @@
             summed = summed + dot(values, probs.astype(BF16), TN)
         result[:, head_cols(head)] = (summed / total).T.astype(BF16)
         lse[head : head + 1] = top + jnp.log2(total)
-    if with_context:
+    if first:
         text[1].wait_recv()
         text[2].start()
         text[0].wait_recv()
         text[2].wait_recv()
     for item in [to_near] + to_far + onward + text:
         item.wait_send()
+    side.finish()
+
+
+def below(counts, slot, shape):
+    index = lax.broadcasted_iota(jnp.int32, shape, 0).astype(F32)
+    return index < counts[slot, 0:1]
+
+
+def softmax_back(scores, lse_row, mask):
+    probs = jnp.exp2(scores * (SCALE * LOG2E) - lse_row)
+    return probs if mask is None else jnp.where(mask, probs, 0.0)
 
 
 def out_sum_kernel(
@@ -876,18 +1068,20 @@
     per_block = 128 // CHUNK
 
     def project(rows, index):
-        part[rows] = dot(rows_in[rows], weight[0], NT).astype(BF16)
+        part[rows] = dot(rows_in[rows], weight[...], NT).astype(BF16)
         chain.begin(index * per_block, per_block)
 
+    side.need(OUT)
     loop_rows(tokens, 128, project)
+    side.need(CONTEXT, TEXT_WEIGHT)
     text_count, width = text_key.shape
     blocks = text_count // 128
 
     def text(rows, index):
         block = context[rows]
-        text_key[rows] = dot(block, text_weight[1]) + row_of(rows_w, 3)
+        text_key[rows] = dot(block, text_weight[0]) + row_of(rows_w, 3)
         chain.serve(2 * index)
-        text_vb[rows] = (dot(block, text_weight[2]) + row_of(rows_w, 4)).astype(BF16)
+        text_vb[rows] = (dot(block, text_weight[1]) + row_of(rows_w, 4)).astype(BF16)
         chain.serve(2 * index + 1)
 
     loop_rows(text_count, 128, text)
@@ -897,49 +1091,43 @@
         side.early()
         exchange.start(stat_rows(text_key[...] * text_key[...], 0))
 
-    def late():
-        exchange.finish()
-        text_inv = inverse_rms(stat_column(slots, 0, HEAD_DIM), features)
-        for head in range(width // HEAD_DIM):
-            cols = head_cols(head)
-            text_kb[:, cols] = (
-                text_key[:, cols] * text_inv * rows_w[GAINS + 3 : GAINS + 4, cols]
-            ).astype(BF16)
-        side.late()
-
-    chain.drain(2 * blocks, early, late)
+    chain.drain(2 * blocks, early, side.middle)
+    exchange.finish()
+    text_inv = inverse_rms(stat_column(slots, 0, HEAD_DIM), features)
+    for head in range(width // HEAD_DIM):
+        cols = head_cols(head)
+        text_kb[:, cols] = (
+            text_key[:, cols] * text_inv * rows_w[GAINS + 3 : GAINS + 4, cols]
+        ).astype(BF16)
     side.finish()
 
 
-def cross_kernel(
+def cross_ffn_kernel(
+    gathered,
     side,
     base,
     tot,
     rows_d,
     rows_w,
+    rows_f,
     weight,
     text_kb,
     text_vb,
     out_weight,
-    hidden,
-    normal,
-    query,
-    query_b,
-    result,
-    lse,
-    slots,
-    total,
-    send_sems,
-    recv_sems,
-    part,
-    came,
-    pair,
-    peers,
-    sems,
+    up,
+    *refs,
 ):
+    refs = list(refs)
+    down = side.jobs[0].out if gathered else refs.pop(0)
+    hidden, normal, query, query_b, result, lse, slots = refs[:7]
+    hidden_f, normal_f, gelu_b, slope, total_f = refs[7:12]
+    send_sems, recv_sems, total = refs[12:15]
+    part, came, pair, peers, sems = refs[15:20]
+    part_f, came_f, pair_f, peers_f, sems_f = refs[20:25]
     greet(True, side.masks)
     side.start()
     chain = Chain(part, total, (came, pair, peers), sems)
+    chain_f = Chain(part_f, total_f, (came_f, pair_f, peers_f), sems_f)
     tokens, width = query.shape
     features = hidden.shape[1]
     heads = width // HEAD_DIM
@@ -952,13 +1140,16 @@
         block = normed(block)[0] * row_of(rows_d, CROSS_GAIN) + row_of(rows_d, CROSS_SHIFT)
         block = block.astype(BF16)
         normal[rows] = block
-        query[rows] = dot(block, weight[0]) + row_of(rows_w, 2)
-
+        query[rows] = dot(block, weight[...]) + row_of(rows_w, 2)
+
+    side.need(WEIGHT)
     loop_rows(tokens, 256, project)
+    side.store(HIDDEN, NORMAL, QUERY)
     exchange = Exchange(slots, send_sems, recv_sems)
     exchange.start(stat_rows(query[...] * query[...], 0))
     exchange.finish()
     query_inv = inverse_rms(stat_column(slots, 0, HEAD_DIM), features)
+    side.need(TEXT_KB, TEXT_VB)
     lse[...] = jnp.zeros(lse.shape, F32)
     for head in range(heads):
         cols = head_cols(head)
@@ -975,108 +1166,22 @@
     per_block = 128 // CHUNK
 
     def project_out(rows, index):
-        part[rows] = dot(result[rows], out_weight[1], NT).astype(BF16)
+        part[rows] = dot(result[rows], out_weight[...], NT).astype(BF16)
         chain.begin(index * per_block, per_block)
 
+    side.store(QUERY_B, RESULT)
+    side.need(OUT)
     loop_rows(tokens, 128, project_out)
-    chain.drain(0, side.early, side.late)
-    side.finish()
-
-
-def column_cuts(width):
-    cuts, low = [], 0
-    while low < width:
-        high = low + 512 if width - low >= 1024 else width
-        cuts.append((low, high))
-        low = high
-    return cuts
-
-
-GELU_A = 0.7978845608028654
-GELU_B = 0.044715
-
-
-def mlp_loop(side, tokens, rows_of, inner, second, chain, middle):
-    size = 128
-    per_block = size // CHUNK
-    features, hidden_width = second.shape
-    cuts = column_cuts(hidden_width)
-    half = features // 2
-    blocks = tokens // size
-
-    def step(index, carry):
-        rows = pl.ds(pl.multiple_of(index * size, size), size)
-        block = rows_of(rows)
-
-        def serve(offset):
-            @pl.when(index > 0)
-            def _():
-                chain.serve(jnp.maximum(index - 1, 0) * per_block + offset)
-
-        served = 0
-        for place, (low, high) in enumerate(cuts):
-            inner(rows, block, low, high)
-            if place % 2 == 1 and served < 2:
-                serve(served)
-                served += 1
-        while served < 2:
-            serve(served)
-            served += 1
-        for part_index in range(2):
-            cols = slice(part_index * half, (part_index + 1) * half)
-            chain.part[rows, cols] = dot(middle[rows], second[cols], NT).astype(BF16)
-            if part_index == 0:
-                serve(2)
-        chain.begin(index * per_block, per_block)
-        serve(3)
-        if side.jobs:
-
-            @pl.when(index == 1)
-            def _():
-                side.early()
-
-            @pl.when(index == blocks - 1)
-            def _():
-                side.late()
-
-        return carry
-
-    lax.fori_loop(0, blocks, step, 0)
-    chain.drain((blocks - 1) * per_block)
-    side.finish()
-
-
-def ffn_kernel(
-    side,
-    base,
-    tot,
-    rows_d,
-    up,
-    rows_f,
-    down,
-    hidden,
-    normal,
-    gelu_b,
-    slope,
-    total,
-    part,
-    came,
-    pair,
-    peers,
-    sems,
-):
-    greet(True, side.masks)
-    side.start()
-    chain = Chain(part, total, (came, pair, peers), sems)
-    tokens = hidden.shape[0]
+    side.move(1, DOWN)
+    side.start(1)
     scale_row = 1.0 + row_of(rows_d, MODS + 4)
     shift_row = row_of(rows_d, MODS + 3)
 
     def rows_of(rows):
-        block = add_branch(base[rows], tot[rows], row_of(rows_d, OUT_BIAS + 1), 1.0)
-        hidden[rows] = block
+        block = add_branch(hidden[rows], total[rows], row_of(rows_d, OUT_BIAS + 1), 1.0)
+        hidden_f[rows] = block
         block = (normed(block)[0] * scale_row + shift_row).astype(BF16)
-        normal[rows] = block
+        normal_f[rows] = block
         return block
 
     def inner(rows, block, low, high):
@@ -1090,37 +1195,187 @@
             + 0.5 * z * (1.0 - tanh * tanh) * (GELU_A * (1.0 + 3.0 * GELU_B * square))
         ).astype(BF16)
 
-    mlp_loop(side, tokens, rows_of, inner, down, chain, gelu_b)
+    def before_second():
+        if gathered:
+            side.finish(DOWN)
+        else:
+            side.need(DOWN)
+
+    def after(left):
+        side.store(HIDDEN_F, NORMAL_F, GELU_B_NAME, SLOPE)
+
+    side.need(UP)
+    mlp_loop(
+        side, tokens, rows_of, inner, down, chain_f, gelu_b, before_second, after, chain
+    )
+
+
+def column_cuts(width):
+    cuts, low = [], 0
+    while low < width:
+        high = low + 512 if width - low >= 1024 else width
+        cuts.append((low, high))
+        low = high
+    return cuts
+
+
+GELU_A = 0.7978845608028654
+GELU_B = 0.044715
+
+
+def mlp_loop(side, tokens, rows_of, inner, second, chain, middle, before_second, after, feed=None):
+    size = 128
+    per_block = size // CHUNK
+    features, hidden_width = second.shape
+    cuts = column_cuts(hidden_width)
+    half = features // 2
+    blocks = tokens // size
+    if feed is not None:
+
+        @pl.when(feed.is_mid)
+        def _():
+            feed.first(0)
+            for k in range(1, per_block):
+                feed.first(k)
+                feed.second(k - 1)
+
+    def step(index, carry):
+        rows = pl.ds(pl.multiple_of(index * size, size), size)
+        low = index * per_block
+
+        def serve(offset):
+            if feed is None:
+
+                @pl.when(index > 0)
+                def _():
+                    chain.serve(jnp.maximum(low - per_block, 0) + offset)
+
+                return
+            if offset > 0:
+
+                @pl.when(feed.is_mid & (index < blocks - 1))
+                def _():
+                    ahead = jnp.minimum(low + per_block, feed.chunks - per_block)
+                    feed.first(ahead + offset)
+                    feed.second(ahead + offset - 1)
+
+            @pl.when(index == blocks - 1)
+            def _():
+                chain.serve(offset)
+
+        if feed is not None:
+
+            @pl.when(feed.is_mid)
+            def _():
+                @pl.when(index < blocks - 1)
+                def _():
+                    feed.first(jnp.minimum(low + per_block, feed.chunks - per_block))
+
+                feed.second(low + per_block - 1)
+
+            @pl.when(feed.is_end)
+            def _():
+                for offset in range(per_block):
+                    feed.inward(low + offset, feed.inner).wait_send()
+                    feed.outward(low + offset, feed.inner).wait_recv()
+
+        block = rows_of(rows)
+        served = 0
+        for place, (left, right) in enumerate(cuts):
+            inner(rows, block, left, right)
+            if place % 2 == 1 and served < 2:
+                serve(served)
+                served += 1
+        while served < 2:
+            serve(served)
+            served += 1
+
+        @pl.when(index == 0)
+        def _():
+            before_second()
+
+        for part_index in range(2):
+            cols = slice(part_index * half, (part_index + 1) * half)
+            chain.part[rows, cols] = dot(middle[rows], second[cols], NT).astype(BF16)
+            if part_index == 0:
+                serve(2)
+        chain.begin(low, per_block)
+        serve(3)
+        if side.jobs:
+            if feed is None:
+                points = ((1, bits_of_dp() - 2), (blocks - 1, bits_of_dp() - 1))
+            else:
+                points = ((blocks - 1, bits_of_dp() - 2),)
+            for point, target in points:
+
+                @pl.when(index == point)
+                def _(target=target):
+                    side.move(target)
+
+        return carry
+
+    lax.fori_loop(0, blocks, step, 0)
+    left = (blocks - 1) * per_block if feed is None else per_block
+    left = after(left) or left
+    chain.drain(left, None, None if feed is None else side.late)
+    if feed is not None:
+        feed.close()
+    side.finish()
 
 
 def ffn_back_kernel(
+    joined,
     side,
     grad,
-    tot,
-    rows_d,
-    down,
-    up,
-    slope,
-    down_in,
-    inner_b,
-    total,
-    sums,
-    bias_sum,
-    part,
-    came,
-    pair,
-    peers,
-    sems,
+    *refs,
 ):
+    refs = list(refs)
+
+    def take(count):
+        taken = refs[:count]
+        del refs[:count]
+        return taken
+
+    if joined:
+        branch, hidden, rows_above = take(3)
+    else:
+        teacher, counts = take(2)
+    tot, rows_d, down, up, slope, normal, gelu_b = take(7)
+    if joined:
+        new_grad, sums_above = take(2)
+    else:
+        new_grad, output = take(2)
+    (total, sums, bias_sum, up_grad, down_grad) = take(5)
+    down_in, inner_b, stage, stage_sems, part, came, pair, peers, sems = refs
     greet(True, side.masks)
     side.start()
     chain = Chain(part, total, (came, pair, peers), sems)
     tokens = grad.shape[0]
     sums[...] = jnp.zeros(sums.shape, F32)
     bias_sum[...] = jnp.zeros(bias_sum.shape, F32)
+    if joined:
+        sums_above[...] = jnp.zeros(sums_above.shape, F32)
+        scale_row = 1.0 + row_of(rows_above, MODS + 1)
 
     def rows_of(rows):
         block = grad[rows]
+        if joined:
+            step = branch[rows].astype(F32)
+            back, hat = norm_back(hidden[rows], scale_row, step)
+            add_sum(sums_above, 0, step)
+            add_sum(sums_above, 1, step * hat)
+            block = block + back
+            new_grad[rows] = block
+        else:
+            block = add_branch(
+                block, tot[rows], row_of(rows_d, OUT_BIAS + 2), row_of(rows_d, MODS + 5)
+            )
+            output[rows] = block
+            block = block - teacher[rows].astype(F32)
+            place = lax.broadcasted_iota(jnp.int32, (block.shape[0], 1), 0) + rows.start
+            block = jnp.where(place.astype(F32) < counts[0, 0:1, 0:1], block, 0.0)
+            new_grad[rows] = block
+            add_sum(sums, 2, block * block)
         add_sum(sums, 0, block * (tot[rows].astype(F32) + row_of(rows_d, OUT_BIAS + 2)))
         block = (block * row_of(rows_d, MODS + 5)).astype(BF16)
         down_in[rows] = block
@@ -1132,7 +1387,44 @@
         inner_b[rows, low:high] = cols
         bias_sum[0:1, low:high] += jnp.sum(cols.astype(F32), axis=0, keepdims=True)
 
-    mlp_loop(side, tokens, rows_of, inner, up, chain, inner_b)
+    def after(left):
+        side.store(NEW_GRAD)
+        if not joined:
+            side.store(OUTPUT)
+        side.need(NORMAL, GELU_B_NAME)
+        copies = []
+
+        def keep(target):
+            def store(tile, size, block):
+                number = len(copies)
+                if number >= 2:
+                    copies[number - 2].wait()
+                stage[number % 2] = block
+                copy = pltpu.make_async_copy(
+                    stage.at[number % 2],
+                    target.at[tile * size : (tile + 1) * size],
+                    stage_sems.at[number % 2],
+                )
+                copy.start()
+                copies.append(copy)
+
+            return store
+
+        def serve(tile):
+            if left + tile < chain.chunks:
+                chain.serve(left + tile)
+
+        tiled_grad(normal, inner_b, keep(up_grad), serve, stage.shape[1])
+        chain.segment(chain.chunks, chain.chunks, 0, 0)
+        tiled_grad(down_in, gelu_b, keep(down_grad), lambda tile: None, stage.shape[1])
+        copies[-2].wait()
+        copies[-1].wait()
+        return chain.chunks
+
+    side.need(GRAD, DOWN, SLOPE)
+    mlp_loop(
+        side, tokens, rows_of, inner, up, chain, inner_b, lambda: side.need(UP), after
+    )
 
 
 def cross_back_kernel(
@@ -1150,13 +1442,16 @@
     text_kb,
     text_vb,
     weight,
+    normal,
+    result,
     new_grad,
-    out_in,
     text_grad,
-    query_grad_b,
     sums,
     width_sums,
     total,
+    matrix_grad,
+    out_in,
+    query_grad_b,
     out_grad,
     query_n,
     slots,
@@ -1189,10 +1484,12 @@
         block = block.astype(BF16)
         out_in[rows] = block
         add_sum(sums, 2, block.astype(F32))
-        out_grad[rows] = dot(block, out_weight[1]).astype(BF16)
-
+        out_grad[rows] = dot(block, out_weight[...]).astype(BF16)
+
+    side.need(OUT)
     loop_rows(tokens, 256, enter)
-    side.early_first()
+    side.store(NEW_GRAD)
+    side.need(QUERY, QUERY_B, TEXT_KB, TEXT_VB)
     for head in range(heads):
         cols = head_cols(head)
         query_h, out_grad_h = query_b[:, cols], out_grad[:, cols]
@@ -1207,6 +1504,7 @@
     exchange = Exchange(slots, send_sems, recv_sems)
     exchange.start(stat_rows(query[...] * query_n[...] * gain, 0))
     inverse = inverse_rms(stat_column(slots_q, 0, HEAD_DIM), features)
+    side.move(1)
     exchange.finish()
     term = stat_column(slots, 0, HEAD_DIM) * inverse * inverse * inverse / features
     for head in range(heads):
@@ -1221,11 +1519,24 @@
     per_block = 128 // CHUNK
 
     def leave(rows, index):
-        part[rows] = dot(query_grad_b[rows], weight[0], NT).astype(BF16)
+        part[rows] = dot(query_grad_b[rows], weight[...], NT).astype(BF16)
         chain.begin(index * per_block, per_block)
 
+    side.store(TEXT_GRAD)
+    side.need(WEIGHT)
     loop_rows(tokens, 128, leave)
-    chain.drain(0, side.early_rest, side.late)
+    side.need(NORMAL, RESULT)
+
+    def keep(low):
+        def store(tile, size, block):
+            matrix_grad[tile * size : (tile + 1) * size, low : low + width] = block
+
+        return store
+
+    tiled_grad(normal, query_grad_b, keep(0), lambda tile: None if tile % 2 else chain.serve(tile // 2))
+    tiled_grad(out_in, result, keep(width), lambda tile: None if tile % 2 else chain.serve(2 + tile // 2))
+    side.store(MATRIX_GRAD)
+    chain.drain(4, side.late)
     side.finish()
 
 
@@ -1243,12 +1554,14 @@
     others,
     lse,
     text_grad,
+    result,
     new_grad,
-    out_in,
+    matrix_grad,
     sums,
     query_grad,
     key_value_grad,
     text_sum,
+    out_in,
     out_grad,
     probs,
     prob_grads,
@@ -1260,6 +1573,7 @@
     recv_sems,
 ):
     greet(False, [1, 2])
+    side.start()
     near, far = holders()
     tokens, width = query.shape
     heads = width // HEAD_DIM
@@ -1284,7 +1598,7 @@
             dp=far if kind == 1 else near,
         )
 
-    place = lax.rem(lax.axis_index("dp"), HOLD)
+    place = lax.rem(lax.axis_index(DP), HOLD)
 
     def text_part(slot):
         start = pl.multiple_of(flip(place, slot) * text_rows, text_rows)
@@ -1306,9 +1620,12 @@
         block = (block * row_of(rows_d, MODS + 2)).astype(BF16)
         out_in[rows] = block
         add_sum(sums, 3, block.astype(F32))
-        out_grad[rows] = dot(block, out_weight[0]).astype(BF16)
-
+        out_grad[rows] = dot(block, out_weight[...]).astype(BF16)
+
+    side.need(OUT)
     loop_rows(tokens, 256, enter)
+    side.store(NEW_GRAD)
+    side.need(QUERY, KEY_VALUE, OTHERS, RESULT)
     text_copy(2).wait_recv()
     text_away[1] = (text_part(2) + text_landed[2].astype(F32)).astype(BF16)
     text_copy(1).start()
@@ -1355,6 +1672,13 @@
                 away[slot - 1, head, 1] = value_g.astype(BF16)
                 copy(slot - 1, head).start()
         query_grad[:, cols] = query_n.T
+    side.store(QUERY_GRAD)
+
+    def keep(tile, size, block):
+        matrix_grad[tile * size : (tile + 1) * size] = block
+
+    tiled_grad(out_in, result, keep, lambda tile: None)
+    side.store(MATRIX_GRAD)
     text_copy(0).wait_recv()
     text_copy(1).wait_recv()
     text_sum[...] = text_part(0) + text_landed[0].astype(F32) + text_landed[1].astype(F32)
@@ -1386,10 +1710,17 @@
     cosine,
     sine,
     weight,
+    normal,
+    context,
+    text_weight,
+    context_before,
+    width_sums,
+    context_part,
+    total,
+    self_grad,
+    text_matrix,
     grads_b,
     text_b,
-    width_sums,
-    total,
     query_n,
     key_n,
     slots,
@@ -1408,7 +1739,7 @@
     features = total.shape[1]
     heads = width // HEAD_DIM
     text_rows = text_grad.shape[1]
-    place = lax.rem(lax.axis_index("dp"), HOLD)
+    place = lax.rem(lax.axis_index(DP), HOLD)
     mine = pl.ds(pl.multiple_of(place * text_rows, text_rows), text_rows)
     text_k = text_key[mine]
     width_sums[...] = jnp.zeros(width_sums.shape, F32)
@@ -1432,7 +1763,7 @@
     query_inv = inverse_rms(stat_column(slots_in, 0, HEAD_DIM), features)
     key_inv = inverse_rms(stat_column(slots_in, 1, HEAD_DIM), features)
     text_inv = inverse_rms(stat_column(text_slots.at[:, :, mine], 0, HEAD_DIM), features)
-    side.early_first()
+    side.move(1)
     exchange.finish()
 
     def cubed(inverse, term):
@@ -1481,14 +1812,75 @@
         ).astype(BF16)
         chain.begin(index * per_block, per_block)
 
+    side.need(WEIGHT)
     loop_rows(tokens, 128, leave)
-    chain.drain(0, side.early_rest, side.late)
+    side.need(NORMAL, CONTEXT, TEXT_WEIGHT)
+
+    def keep(target):
+        def store(tile, size, block):
+            target[tile * size : (tile + 1) * size] = block
+
+        return store
+
+    tiled_grad(normal, grads_b, keep(self_grad), chain.serve)
+    side.store(SELF_GRAD)
+    tiled_grad(context, text_b, keep(text_matrix), lambda tile: None)
+    side.store(TEXT_MATRIX)
+    chain.serve(4)
+    context_part[...] = (
+        context_before[...]
+        + dot(text_b[:, :width], text_weight[0], NT)
+        + dot(text_b[:, width:], text_weight[1], NT)
+    )
+    chain.drain(5, side.late)
     side.finish()
 
 
-def norm_back_kernel(side, grad, branch, hidden, rows_d, new_grad, sums):
+def small_rows(clips):
+    low = 6 * LAYERS + 6 * clips
+    places = {BIAS: low, GAIN: low + 3 * LAYERS, SHIFT: low + 4 * LAYERS}
+    places[LOSS] = low + 5 * LAYERS
+    return places, (low + 5 * LAYERS + 1 + 15) // 16 * 16
+
+
+def last_kernel(
+    clips,
+    side,
+    context_part,
+    grad,
+    branch,
+    hidden,
+    rows_d,
+    *refs,
+):
+    refs = list(refs)
+
+    def take(count):
+        taken = refs[:count]
+        del refs[:count]
+        return taken
+
+    above = take(1)[0]
+    small = [take(6) for _ in range(LAYERS)]
+    new_grad, total, out_d, out_w, out_f = take(5)
+    sums = take(1)[0]
+    part, came, pair, peers, sems = take(5)
+    bits = bits_of_dp()
+    away = [take(3) for _ in range(bits)]
+    landed = [take(3) for _ in range(bits)]
+    send_sems, recv_sems = take(2)
+    greet(True, side.masks)
+    side.start()
+    me = lax.axis_index(DP)
+    clip = me // HOLD
+    chain = Chain(part, total, (came, pair, peers), sems)
+    part[...] = context_part[...].astype(BF16)
+    chain.begin(0, chain.chunks)
     sums[...] = jnp.zeros(sums.shape, F32)
     scale_row = 1.0 + row_of(rows_d, MODS + 1)
+    tokens = grad.shape[0]
+    size = tokens // chain.chunks
+    side.need(GRAD, BRANCH, HIDDEN)
 
     def enter(rows, index):
         step = branch[rows].astype(F32)
@@ -1496,20 +1888,87 @@
         add_sum(sums, 0, step)
         add_sum(sums, 1, step * hat)
         new_grad[rows] = grad[rows] + back
-
-    loop_rows(grad.shape[0], 128, enter)
-
-
-def scatter_kernel(side):
-    greet(False, side.masks)
-    side.start()
-    side.early()
-    side.late()
+        chain.serve(index)
+
+    loop_rows(tokens, size, enter)
+    side.store(NEW_GRAD)
+    side.move(1)
+    places, count = small_rows(clips)
+    out_d[...] = jnp.zeros(out_d.shape, F32)
+    out_f[...] = jnp.zeros(out_f.shape, F32)
+    time_rows = [jnp.zeros((1, grad.shape[1]), F32) for _ in range(6)]
+    for layer in range(LAYERS):
+        sums1, sums2, sums3, width1, width2, hidden_sum = small[layer]
+        sums0 = sums if layer == 0 else above
+        mods = [(sums0, 0), (sums0, 1), (sums1, 2), (sums2, 0), (sums2, 1), (sums3, 0)]
+        for row, (ref, index) in enumerate(mods):
+            value = row_of(ref, index)
+            time_rows[row] = time_rows[row] + value
+            out_d[6 * layer + row : 6 * layer + row + 1] = value
+        for row, (ref, index) in enumerate([(sums1, 3), (sums2, 2), (sums3, 1)]):
+            place = places[BIAS] + 3 * layer + row
+            out_d[place : place + 1] = row_of(ref, index)
+        place = places[GAIN] + layer
+        out_d[place : place + 1] = row_of(sums1, 0)
+        place = places[SHIFT] + layer
+        out_d[place : place + 1] = row_of(sums1, 1)
+        out_w[24 * layer : 24 * layer + 16] = width1[...]
+        out_w[24 * layer + 16 : 24 * layer + 24] = width2[...]
+        out_f[layer : layer + 1] = row_of(hidden_sum, 0)
+    for index in range(clips):
+        for row in range(6):
+            place = 6 * LAYERS + 6 * index + row
+            out_d[place : place + 1] = jnp.where(clip == index, time_rows[row], 0.0)
+    out_d[places[LOSS] : places[LOSS] + 1] = row_of(small[LAYERS - 1][2], 2)
+    for bit in range(bits):
+        copies = []
+        for number, ref in enumerate((out_d, out_w, out_f)):
+            away[bit][number][...] = ref[...].astype(BF16)
+            copy = send(
+                away[bit][number],
+                landed[bit][number],
+                send_sems.at[bit, number],
+                recv_sems.at[bit, number],
+                dp=flip(me, 1 << bit),
+            )
+            copy.start()
+            copies.append(copy)
+        if bit == 0:
+            chain.drain(chain.chunks)
+        side.move(bit)
+        for number, ref in enumerate((out_d, out_w, out_f)):
+            copies[number].wait()
+            ref[...] = away[bit][number][...].astype(F32) + landed[bit][number][...].astype(F32)
     side.finish()
 
 
-def weight_grad(left, right):
-    return dot(left, right, TN).astype(BF16)
+def unpack_kernel(
+    clips, side, lengths, rows_d, rows_w, rows_f, loss, time, bias, key_bias, gains, hidden, out,
+    gain, shift, mods
+):
+    places, count = small_rows(clips)
+    for layer in range(LAYERS):
+        for row in range(6):
+            mods[row, layer : layer + 1] = row_of(rows_d, 6 * layer + row)
+        for row in range(3):
+            out[row, layer : layer + 1] = row_of(rows_d, places[BIAS] + 3 * layer + row)
+        base = 24 * layer
+        for row, place in enumerate((4, 6, 17, 7, 8)):
+            bias[row, layer : layer + 1] = row_of(rows_w, base + place)
+        key_bias[layer : layer + 1] = row_of(rows_w, base + 5)
+        for row, place in enumerate((0, 1, 16, 3)):
+            gains[layer, row : row + 1] = row_of(rows_w, base + place)
+    for index in range(clips):
+        for row in range(6):
+            time[row, index : index + 1] = row_of(rows_d, 6 * LAYERS + 6 * index + row)
+    hidden[...] = rows_f[0:LAYERS]
+    gain[...] = rows_d[places[GAIN] : places[GAIN] + LAYERS]
+    shift[...] = rows_d[places[SHIFT] : places[SHIFT] + LAYERS]
+    count = lengths[0]
+    for index in range(1, clips):
+        count = count + lengths[index]
+    total = jnp.sum(row_of(rows_d, places[LOSS]), axis=1, keepdims=True)
+    loss[...] = jnp.broadcast_to(total, loss.shape) / (count.astype(F32) * rows_d.shape[1])
 
 
 def per_device(
@@ -1541,7 +2000,7 @@
     clip_count = time_embed.shape[0]
     text_rows = context.shape[0]
     text_all = text_rows * HOLD
-    clip = lax.axis_index("dp") // HOLD
+    clip = lax.axis_index(DP) // HOLD
     out_t = jnp.swapaxes(out_proj, 2, 3)
     down_t = jnp.swapaxes(ffn_down, 1, 2)
 
@@ -1560,34 +2019,36 @@
         (
             lengths,
             block_order,
-            time_embed,
-            modulation,
-            out_bias,
+            jnp.swapaxes(time_embed, 0, 1),
+            jnp.swapaxes(modulation, 0, 1),
+            jnp.swapaxes(out_bias, 0, 1),
             cross_gain,
             cross_shift,
-            proj_bias,
+            jnp.swapaxes(proj_bias, 0, 1),
             key_bias,
             norm_gains,
             ffn_bias,
+            positions,
+            rope_table(HEAD_DIM),
         ),
-        (((HOLD, 8, tokens), F32),) + pack * LAYERS,
+        (((HOLD, 8, tokens), F32), ((tokens, HEAD_DIM), F32), ((tokens, HEAD_DIM), F32))
+        + pack * LAYERS,
         [three, three],
         jobs=[Gather(self_proj, 0)],
         scalars=2,
         micros=25,
     )
-    counts = results[0]
-    packs = [results[1 + 3 * layer : 4 + 3 * layer] for layer in range(LAYERS)]
-    cosine, sine = rope_angles(positions, HEAD_DIM)
+    counts, cosine, sine = results[:3]
+    packs = [results[3 + 3 * layer : 6 + 3 * layer] for layer in range(LAYERS)]
 
     saved = []
-    weights = {"self": [self_w], "cross": [], "out": [], "up": [], "down": []}
+    weights = {SELF: [self_w], CROSS: [], OUT: [], UP: [], DOWN: []}
     sources = {
-        "self": self_proj,
-        "cross": cross_proj,
-        "out": out_t,
-        "up": ffn_up,
-        "down": down_t,
+        SELF: self_proj,
+        CROSS: cross_proj,
+        OUT: out_t,
+        UP: ffn_up,
+        DOWN: down_t,
     }
 
     def gathers(layer, *names):
@@ -1600,45 +2061,59 @@
     base, tot, before = latents, latents, packs[0][0]
     for layer in range(LAYERS):
         pack_d, pack_w, pack_f = packs[layer]
-        names = ("cross", "out") if layer == 0 else ()
-        (hidden, a1, sq, sk, q_rot, kv, stat1), found = run(
-            "qkv" + str(layer > 0),
-            functools.partial(qkv_kernel, layer == 0),
-            (base, tot, before, pack_d, pack_w, weights["self"][layer], cosine, sine),
+        names = (CROSS, OUT) if layer == 0 else ()
+        results, found = run(
+            "attend" + str(layer > 0),
+            functools.partial(attend_kernel, layer == 0),
             (
-                (rows_d, F32),
-                (rows_d, BF16),
-                (rows_w, F32),
-                (rows_w, F32),
-                (rows_w, BF16),
+                base,
+                tot,
+                before,
+                pack_d,
+                pack_w,
+                Late(WEIGHT, weights[SELF][layer]),
+                Late(COSINE, cosine),
+                Late(SINE, sine),
+                counts,
+            )
+            + ((context,) if layer == 0 else ()),
+            (
+                Early(HIDDEN, rows_d, F32),
+                Early(NORMAL, rows_d, BF16),
+                Early(QUERY, rows_w, F32),
+                Early(KEY, rows_w, F32),
+                Early(QUERY_ROT, rows_w, BF16),
                 (kv_shape, BF16),
                 (stats, F32),
-            ),
-            [three, three],
-            jobs=gathers(layer, *names),
-            micros=15,
-        )
-        keep(found, *names)
-        attended, unused = run(
-            "attend" + str(layer > 0),
-            functools.partial(attend_kernel, layer == 0),
-            (counts, q_rot, kv) + ((context,) if layer == 0 else ()),
-            (((HOLD - 1,) + kv_shape, BF16), (rows_w, BF16), ((8, tokens), F32))
+                ((HOLD - 1,) + kv_shape, BF16),
+                (rows_w, BF16),
+                ((8, tokens), F32),
+            )
             + ((((text_all, features), BF16),) if layer == 0 else ()),
             [
                 pltpu.VMEM((heads, HOLD, tokens, tokens), F32),
+                three,
+                three,
                 pltpu.SemaphoreType.DMA((4 + 2 * heads,)),
                 pltpu.SemaphoreType.DMA((4 + 2 * heads,)),
             ],
-            micros=30,
+            jobs=gathers(layer, *names),
+            micros=40,
         )
-        others, o1, lse1 = attended[:3]
+        keep(found, *names)
+        hidden, a1, sq, sk, q_rot, kv, stat1, others, o1, lse1 = results[:10]
         if layer == 0:
-            clip_context = attended[3]
+            clip_context = results[10]
         (tot1, ck, ckb, cvb, stat_t), found = run(
             "out_sum",
             out_sum_kernel,
-            (o1, weights["out"][layer], clip_context, weights["cross"][layer], pack_w),
+            (
+                o1,
+                Late(OUT, weights[OUT][layer], 0),
+                Late(CONTEXT, clip_context),
+                Late(TEXT_WEIGHT, weights[CROSS][layer], 1, 3),
+                pack_w,
+            ),
             (
                 (rows_d, BF16),
                 ((text_all, width), F32),
@@ -1647,73 +2122,66 @@
                 ((CHAIN, 8, text_all), F32),
             ),
             [three, three] + chain_scratch,
-            jobs=gathers(layer, "up"),
+            jobs=gathers(layer, UP) + gathers(1, SELF)
+            if layer == 0
+            else gathers(layer, DOWN),
             micros=45,
         )
-        keep(found, "up")
-        names = ("down",) if layer == LAYERS - 1 else ("down", "self")
-        (h1, a3, cq, cqb, o2, lse2, stat2, tot2), found = run(
-            "cross",
-            cross_kernel,
-            (hidden, tot1, pack_d, pack_w, weights["cross"][layer], ckb, cvb)
-            + (weights["out"][layer],),
+        keep(found, *((UP, SELF) if layer == 0 else (DOWN,)))
+        gathered = layer == 0
+        jobs = [
+            Gather(sources[DOWN], 0, name=DOWN, held=True),
+            Gather(sources[CROSS], 1, wave=1),
+            Gather(sources[OUT], 1, wave=1),
+            Gather(sources[UP], 1, wave=1),
+        ]
+        results, found = run(
+            "cross_ffn" + str(gathered),
+            functools.partial(cross_ffn_kernel, gathered),
             (
-                (rows_d, F32),
-                (rows_d, BF16),
-                (rows_w, F32),
-                (rows_w, BF16),
-                (rows_w, BF16),
+                hidden,
+                tot1,
+                pack_d,
+                pack_w,
+                pack_f,
+                Late(WEIGHT, weights[CROSS][layer], 0),
+                Late(TEXT_KB, ckb),
+                Late(TEXT_VB, cvb),
+                Late(OUT, weights[OUT][layer], 1),
+                Late(UP, weights[UP][layer]),
+            )
+            + (() if gathered else (Late(DOWN, weights[DOWN][layer]),)),
+            (
+                Early(HIDDEN, rows_d, F32),
+                Early(NORMAL, rows_d, BF16),
+                Early(QUERY, rows_w, F32),
+                Early(QUERY_B, rows_w, BF16),
+                Early(RESULT, rows_w, BF16),
                 ((8, tokens), F32),
                 (stats, F32),
+                Early(HIDDEN_F, rows_d, F32),
+                Early(NORMAL_F, rows_d, BF16),
+                Early(GELU_B_NAME, rows_f, BF16),
+                Early(SLOPE, rows_f, BF16),
                 (rows_d, BF16),
             ),
-            [three, three] + chain_scratch,
-            jobs=gathers(layer, "down") + (gathers(layer + 1, "self")),
-            micros=50,
+            [three, three, pltpu.VMEM(rows_d, BF16)] + chain_scratch + chain_scratch,
+            jobs=jobs if gathered else [],
+            micros=90,
         )
-        keep(found, *names)
-        (h2, a2, gelu_b, slope, tot3), found = run(
-            "ffn",
-            ffn_kernel,
-            (h1, tot2, pack_d, weights["up"][layer], pack_f, weights["down"][layer]),
-            (
-                (rows_d, F32),
-                (rows_d, BF16),
-                (rows_f, BF16),
-                (rows_f, BF16),
-                (rows_d, BF16),
-            ),
-            chain_scratch,
-            jobs=gathers(layer + 1, "cross", "out"),
-            micros=55,
-        )
-        keep(found, "cross", "out")
+        h1, a3, cq, cqb, o2, lse2, stat2, h2, a2, gelu_b, slope, tot3 = results
+        if gathered:
+            keep(found, DOWN, CROSS, OUT, UP)
         saved.append(
             (hidden, a1, sq, sk, q_rot, kv, stat1, others, o1, lse1, tot1, ck, ckb, cvb, stat_t)
             + (h1, a3, cq, cqb, o2, lse2, stat2, h2, a2, gelu_b, slope, tot3)
         )
         base, tot, before = h2, tot3, pack_d
-    output = add_branch(base, tot, before[OUT_BIAS + 2], before[MODS + 5])
-    valid = jnp.arange(tokens, dtype=jnp.int32).astype(F32) < counts[0, 0, 0]
-    error = jnp.where(valid[:, None], output - teacher.astype(F32), 0.0)
-    sse = jnp.sum(error * error)
-    grad = error
-
-    pending = []
+    grad = base
     reduced = {}
-
-    def scatter_some(names):
-        chosen = [item for item in pending if item[0] in names]
-        for item in chosen:
-            pending.remove(item)
-        return [item[0] for item in chosen], [Scatter(item[1]) for item in chosen]
-
-    def keep_sums(names, found):
-        for name, item in zip(names, found):
-            reduced[name] = item
-
-    sums_d, sums_w, sums_f = [], [], []
+    small = [None] * LAYERS
     context_part = jnp.zeros(context.shape, F32)
+    above = None
     for layer in reversed(range(LAYERS)):
         (hidden, a1, sq, sk, q_rot, kv, stat1, others, o1, lse1, tot1, ck, ckb, cvb, stat_t) = saved[
             layer
@@ -1721,42 +2189,83 @@
         (h1, a3, cq, cqb, o2, lse2, stat2, h2, a2, gelu_b, slope, tot3) = saved[layer][15:]
         pack_d, pack_w, pack_f = packs[layer]
         w_self, w_cross, w_out, w_up, w_down = [
-            weights[name][layer] for name in ("self", "cross", "out", "up", "down")
+            weights[name][layer] for name in (SELF, CROSS, OUT, UP, DOWN)
         ]
-        names, jobs = scatter_some([("self", layer + 1), ("text", layer + 1), ("out0", layer + 1)])
-        (dy3, dz, da2, sums3, dz_sum), found = run(
-            "ffn_back",
-            ffn_back_kernel,
-            (grad, tot3, pack_d, w_down, w_up, slope),
+        joined = above is not None
+        matrix = (features, hidden_width)
+        results, found = run(
+            "ffn_back" + str(joined),
+            functools.partial(ffn_back_kernel, joined),
+            (Late(GRAD, grad),)
+            + (above if joined else (teacher, counts))
+            + (
+                tot3,
+                pack_d,
+                Late(DOWN, w_down),
+                Late(UP, w_up),
+                Late(SLOPE, slope),
+                Late(NORMAL, a2),
+                Late(GELU_B_NAME, gelu_b),
+            ),
             (
-                (rows_d, BF16),
-                (rows_f, BF16),
+                Early(NEW_GRAD, rows_d, F32, over=0),
+                ((8, features), F32) if joined else Early(OUTPUT, rows_d, F32),
+            )
+            + (
                 (rows_d, BF16),
                 ((8, features), F32),
                 ((8, hidden_width), F32),
+                (matrix, BF16, True),
+                (matrix, BF16, True),
             ),
-            chain_scratch,
-            jobs=jobs,
-            micros=55,
+            [
+                pltpu.VMEM(rows_d, BF16),
+                pltpu.VMEM(rows_f, BF16),
+                pltpu.VMEM((2, 256, hidden_width), BF16),
+                pltpu.SemaphoreType.DMA((2,)),
+            ]
+            + chain_scratch,
+            jobs=[Scatter(text_matrix), Scatter(self_matrix)] if joined else [],
+            micros=60,
         )
-        keep_sums(names, found)
-        pending.append((("up", layer), weight_grad(a2, dz)))
-        pending.append((("down", layer), weight_grad(dy3, gelu_b)))
-        names, jobs = scatter_some([("up", layer), ("down", layer)])
-        (grad, dy2, dct, dcq, sums2, wsums2, da3), found = run(
+        grad = results[0]
+        if not joined:
+            output = results[1]
+        else:
+            sums_above = results[1]
+            reduced[TEXT, layer + 1], reduced[SELF, layer + 1] = found
+        da2, sums3, dz_sum, up_grad, down_grad = results[2:]
+        (grad, dct, sums2, wsums2, da3, cross_matrix), found = run(
             "cross_back",
             cross_back_kernel,
-            (grad, da2, h2, pack_d, pack_w, w_out, cq, cqb, lse2, stat2, ckb, cvb, w_cross),
             (
-                (rows_d, F32),
-                (rows_d, BF16),
-                ((2, text_all, width), F32),
-                (rows_w, BF16),
+                grad,
+                da2,
+                h2,
+                pack_d,
+                pack_w,
+                Late(OUT, w_out, 1),
+                Late(QUERY, cq),
+                Late(QUERY_B, cqb),
+                lse2,
+                stat2,
+                Late(TEXT_KB, ckb),
+                Late(TEXT_VB, cvb),
+                Late(WEIGHT, w_cross, 0),
+                Late(NORMAL, a3),
+                Late(RESULT, o2),
+            ),
+            (
+                Early(NEW_GRAD, rows_d, F32),
+                Early(TEXT_GRAD, (2, text_all, width), F32),
                 ((8, features), F32),
                 ((8, width), F32),
                 (rows_d, BF16),
+                Early(MATRIX_GRAD, (features, 2 * width), BF16),
             ),
             [
+                pltpu.VMEM(rows_d, BF16),
+                pltpu.VMEM(rows_w, BF16),
                 pltpu.VMEM(rows_w, BF16),
                 pltpu.VMEM(rows_w, F32),
                 pltpu.VMEM(stats, F32),
@@ -1764,23 +2273,38 @@
                 three,
             ]
             + chain_scratch,
-            jobs=jobs,
+            jobs=[Scatter(up_grad, UP)],
             micros=60,
         )
-        keep_sums(names, found)
-        (grad, dy1, sums1, dq_rot, dkv, dtext), unused = run(
+        reduced[UP, layer] = found[0]
+        (grad, out0, sums1, dq_rot, dkv, dtext), found = run(
             "attend_back",
             attend_back_kernel,
-            (counts, grad, da3, h1, pack_d, tot1, w_out, q_rot, kv, others, lse1, dct),
             (
-                (rows_d, F32),
-                (rows_d, BF16),
+                counts,
+                grad,
+                da3,
+                h1,
+                pack_d,
+                tot1,
+                Late(OUT, w_out, 0),
+                Late(QUERY, q_rot),
+                Late(KEY_VALUE, kv),
+                Late(OTHERS, others),
+                lse1,
+                dct,
+                Late(RESULT, o1),
+            ),
+            (
+                Early(NEW_GRAD, rows_d, F32),
+                Early(MATRIX_GRAD, (features, width), BF16),
                 ((8, features), F32),
-                (rows_w, F32),
+                Early(QUERY_GRAD, rows_w, F32),
                 ((2,) + rows_w, F32),
                 ((2, text_rows, width), F32),
             ),
             [
+                pltpu.VMEM(rows_d, BF16),
                 pltpu.VMEM(rows_w, BF16),
                 pltpu.VMEM((HOLD, tokens, tokens), F32),
                 pltpu.VMEM((HOLD, tokens, tokens), F32),
@@ -1793,21 +2317,37 @@
             ],
             micros=35,
         )
-        pending.append((("crossq", layer), weight_grad(a3, dcq)))
-        pending.append((("out1", layer), weight_grad(dy2, o2)))
-        pending.append((("out0", layer), weight_grad(dy1, o1)))
-        names, jobs = scatter_some([("crossq", layer), ("out1", layer)] + [("out0", 0)])
-        (ds, dt, wsums1, da1), found = run(
+        (wsums1, context_part, da1, self_matrix, text_matrix), found = run(
             "qkv_back",
             qkv_back_kernel,
-            (dq_rot, dkv, dtext, sq, sk, ck, stat1, stat_t, pack_w, cosine, sine, w_self),
             (
-                ((tokens, 3 * width), BF16),
-                ((text_rows, 2 * width), BF16),
+                dq_rot,
+                dkv,
+                dtext,
+                sq,
+                sk,
+                ck,
+                stat1,
+                stat_t,
+                pack_w,
+                cosine,
+                sine,
+                Late(WEIGHT, w_self),
+                Late(NORMAL, a1),
+                Late(CONTEXT, context),
+                Late(TEXT_WEIGHT, w_cross, 1, 3),
+                context_part,
+            ),
+            (
                 ((16, width), F32),
+                (context.shape, F32),
                 (rows_d, BF16),
+                Early(SELF_GRAD, (features, 3 * width), BF16),
+                Early(TEXT_MATRIX, (features, 2 * width), BF16),
             ),
             [
+                pltpu.VMEM((tokens, 3 * width), BF16),
+                pltpu.VMEM((text_rows, 2 * width), BF16),
                 pltpu.VMEM(rows_w, F32),
                 pltpu.VMEM(rows_w, F32),
                 pltpu.VMEM(stats, F32),
@@ -1815,132 +2355,114 @@
                 three,
             ]
             + chain_scratch,
-            jobs=jobs,
-            micros=50,
+            jobs=[Scatter(down_grad), Scatter(cross_matrix), Scatter(out0)],
+            micros=60,
         )
-        keep_sums(names, found)
-        pending.append((("self", layer), weight_grad(a1, ds)))
-        pending.append((("text", layer), weight_grad(context, dt)))
-        context_part = (
-            context_part
-            + dot(dt[:, :width], w_cross[1], NT)
-            + dot(dt[:, width:], w_cross[2], NT)
+        reduced[DOWN, layer], reduced[CROSS, layer], reduced[OUT0, layer] = found
+        small[layer] = (sums1, sums2, sums3, wsums1, wsums2, dz_sum)
+        above = (da1, hidden, pack_d)
+    places, count = small_rows(clip_count)
+    small_shapes = ((count, features), (24 * LAYERS, width), (16, hidden_width))
+    travel = [pltpu.VMEM(shape, BF16) for shape in small_shapes]
+    bits = bits_of_dp()
+    (grad, context_sum, packed_d, packed_w, packed_f), found = run(
+        "last",
+        functools.partial(last_kernel, clip_count),
+        (
+            context_part,
+            Late(GRAD, grad),
+            Late(BRANCH, above[0]),
+            Late(HIDDEN, above[1]),
+            above[2],
+            sums_above,
         )
-        (grad, sums0), unused = run(
-            "norm_back",
-            norm_back_kernel,
-            (grad, da1, hidden, pack_d),
-            ((rows_d, F32), ((8, features), F32)),
-            remote=False,
-            micros=6,
-        )
-        sums_d = [sums0, sums1, sums2, sums3] + sums_d
-        sums_w = [wsums1, wsums2] + sums_w
-        sums_f = [dz_sum] + sums_f
-    names, jobs = scatter_some([("self", 0), ("text", 0), ("out0", 0)])
-    unused, found = run("scatter", scatter_kernel, (), (), jobs=jobs, micros=40)
-    keep_sums(names, found)
-
-    sums_d = jnp.stack(sums_d).reshape(LAYERS, 4, 8, features)
-    onehot = (jnp.arange(clip_count, dtype=jnp.int32) == clip).astype(F32)
-    mod_sums = jnp.stack(
-        [
-            sums_d[:, 0, 0],
-            sums_d[:, 0, 1],
-            sums_d[:, 1, 2],
-            sums_d[:, 2, 0],
-            sums_d[:, 2, 1],
-            sums_d[:, 3, 0],
-        ],
-        axis=1,
+        + tuple(item for layer in range(LAYERS) for item in small[layer]),
+        (Early(NEW_GRAD, rows_d, F32), (context.shape, BF16))
+        + tuple((shape, F32) for shape in small_shapes),
+        [pltpu.VMEM((8, features), F32)]
+        + Chain.scratch(text_rows, features)
+        + travel * (2 * bits)
+        + [pltpu.SemaphoreType.DMA((bits, 3)), pltpu.SemaphoreType.DMA((bits, 3))],
+        jobs=[Scatter(text_matrix), Scatter(self_matrix)],
+        micros=30,
     )
-    time_sums = onehot[:, None, None] * jnp.sum(mod_sums, axis=0)[None]
-    packed_d = jnp.concatenate(
-        [
-            mod_sums.reshape(-1, features),
-            time_sums.reshape(-1, features),
-            jnp.stack([sums_d[:, 1, 3], sums_d[:, 2, 2], sums_d[:, 3, 1]], axis=1).reshape(
-                -1, features
-            ),
-            sums_d[:, 1, 0],
-            sums_d[:, 1, 1],
-            jnp.full((1, features), sse / features, F32),
-        ]
+    reduced[TEXT, 0], reduced[SELF, 0] = found
+    unpacked, unused = run(
+        "unpack",
+        functools.partial(unpack_kernel, clip_count),
+        (lengths, packed_d, packed_w, packed_f),
+        (
+            ((1, 128), F32),
+            ((6, clip_count, features), F32),
+            ((5, LAYERS, width), F32),
+            ((LAYERS, width), F32),
+            ((LAYERS, 4, width), F32),
+            ((LAYERS, hidden_width), F32),
+            ((3, LAYERS, features), F32),
+            ((LAYERS, features), F32),
+            ((LAYERS, features), F32),
+            ((6, LAYERS, features), F32),
+        ),
+        remote=False,
+        scalars=1,
+        micros=3,
     )
-    packed_w = jnp.concatenate(sums_w)
-    packed_f = jnp.concatenate([item[0:1] for item in sums_f])
-    packed_d, packed_w, packed_f = lax.psum(
-        (packed_d.astype(BF16), packed_w.astype(BF16), packed_f.astype(BF16)), "dp"
-    )
-    packed_d, packed_w, packed_f = (
-        packed_d.astype(F32),
-        packed_w.astype(F32).reshape(LAYERS, 24, width),
-        packed_f.astype(F32),
-    )
-    context_grad = lax.psum(context_part.astype(BF16), "tensor").astype(F32)
-    low = 6 * LAYERS
-    modulation_grad = packed_d[:low].reshape(LAYERS, 6, features)
-    time_grad = packed_d[low : low + 6 * clip_count].reshape(clip_count, 6, features)
-    low += 6 * clip_count
-    out_bias_grad = packed_d[low : low + 3 * LAYERS].reshape(LAYERS, 3, features)
-    low += 3 * LAYERS
-    cross_gain_grad = packed_d[low : low + LAYERS]
-    cross_shift_grad = packed_d[low + LAYERS : low + 2 * LAYERS]
-    loss = jnp.sum(packed_d[low + 2 * LAYERS]) / (jnp.sum(lengths).astype(F32) * features)
-    proj_bias_grad = jnp.stack([packed_w[:, row] for row in (4, 6, 17, 7, 8)], axis=1)
-    gains_grad = jnp.stack([packed_w[:, row] for row in (0, 1, 16, 3)], axis=1)
+    loss, time, bias, key_sums, gain_sums, hidden_sums, out_sums, gain, shift, mods = unpacked
+    context_grad = context_sum.astype(F32)
 
     def split(block):
         return jnp.swapaxes(block.reshape(block.shape[0], -1, width), 0, 1)
 
-    self_grad = jnp.stack([split(reduced["self", layer]) for layer in range(LAYERS)])
+    self_grad = jnp.stack([split(reduced[SELF, layer]) for layer in range(LAYERS)])
     cross_grad = jnp.stack(
         [
-            jnp.concatenate([reduced["crossq", layer][None], split(reduced["text", layer])])
+            jnp.concatenate(
+                [split(reduced[CROSS, layer])[:1], split(reduced[TEXT, layer])]
+            )
             for layer in range(LAYERS)
         ]
     )
     out_grad = jnp.stack(
         [
-            jnp.stack([reduced["out0", layer].T, reduced["out1", layer].T])
+            jnp.stack([reduced[OUT0, layer].T, reduced[CROSS, layer][:, width:].T])
             for layer in range(LAYERS)
         ]
     )
-    up_grad = jnp.stack([reduced["up", layer] for layer in range(LAYERS)])
-    down_grad = jnp.stack([reduced["down", layer].T for layer in range(LAYERS)])
+    up_grad = jnp.stack([reduced[UP, layer] for layer in range(LAYERS)])
+    down_grad = jnp.stack([reduced[DOWN, layer].T for layer in range(LAYERS)])
     return (
         output,
-        loss,
+        loss[0, 0],
         grad,
         context_grad,
-        time_grad,
+        jnp.swapaxes(time, 0, 1),
         self_grad,
         cross_grad,
         out_grad,
         up_grad,
         down_grad,
-        proj_bias_grad,
-        packed_w[:, 5],
-        gains_grad,
-        packed_f,
-        out_bias_grad,
-        cross_gain_grad,
-        cross_shift_grad,
-        modulation_grad,
+        jnp.swapaxes(bias, 0, 1),
+        key_sums,
+        gain_sums,
+        hidden_sums,
+        jnp.swapaxes(out_sums, 0, 1),
+        gain,
+        shift,
+        jnp.swapaxes(mods, 0, 1),
     )
 
 
 def solution(mesh):
     COLLECTIVES.clear()
-    rows = P("dp", None)
-    col_in = P(None, None, "dp", "tensor")
-    col_out = P(None, None, "tensor", "dp")
-    up, down = P(None, "dp", "tensor"), P(None, "tensor", "dp")
-    vec, mat = P(None, "tensor"), P(None, None, "tensor")
+    rows = P(DP, None)
+    col_in = P(None, None, DP, TENSOR)
+    col_out = P(None, None, TENSOR, DP)
+    up, down = P(None, DP, TENSOR), P(None, TENSOR, DP)
+    vec, mat = P(None, TENSOR), P(None, None, TENSOR)
     return jax.shard_map(
         per_device,
         mesh=mesh,
-        in_specs=(rows, rows, P(), rows, P(), P("dp"), P(None, "dp"))
+        in_specs=(rows, rows, P(), rows, P(), P(DP), P(None, DP))
         + (col_in, col_in, col_out, up, down)
         + (mat, vec, mat, vec, P(), P(), P(), P()),
         out_specs=(rows, P(), rows, rows, P())

time: 1300 us -> 1010 us (0.78)
  Pallas kernels: 1070 us -> 982 us
  local copies, waits for them, and re-layouts: 82.2 us -> 9.47 us
  matrix products: 64.2 us -> 0 us
  blocking collectives: 23.1 us -> 0 us
  between operations: 18.9 us -> 1.87 us
  other arithmetic: 25.9 us -> 9.8 us
    pallas_call x22 -> x17, Pallas kernels: 1070 us -> 982 us  [run(): pl.pallas_call(body, out_shape=tuple((jax.ShapeDtypeStruct(shape, kind) f...]
    dot_general x18 -> x0, matrix products: 64.2 us -> none  [dot(): lax.dot_general(left, right, dims, precision=precision, preferred_element...]
    convert_element_type x4 -> x0, local copies, waits for them, and re-layouts: 40 us -> none  [weight_grad(): return dot(left, right, TN).astype(BF16)]
    psum x1 -> x0, blocking collectives: 23.1 us -> none  [per_device(): lax.psum((packed_d.astype(BF16), packed_w.astype(BF16), packed_f.astype(B...]
  transfers between devices with their start and end apart: 2 -> 0, of which waited for: 0 -> 0; matrix products, arithmetic and copies ran while one was open for 3% -> 0% of each run, Pallas kernels for 3% -> 0%
where the time goes in v2:
time: 1010 us; the launch traced here: 1000 us
  Pallas kernels  982 us (97%)
    pallas_call x17, Pallas kernels, run(): pl.pallas_call(body, out_shape=tuple((jax.ShapeDtypeStruct(shape, kind) f...  982 us

profile of v2, /device:TPU:8, one launch (start us, length us, event | category | flops | bytes accessed | tf_op | source)
XLA Modules:
  0.0 1003.4 jit_solution(14895855816089827747)
XLA Ops:
  1.3 23.7 %shard_map.340 = (f32[4,8,512]{2,1,0:T(8,128)}, f32[512,128]{1,0:T(8,128)}, f32[512,128]{1,0:T(8,128)}, f32[16,1536]{1,0:T(8,128)}, f32[16,384]{1,0:T(8,128)}, /...) custom-call(s32[2]{0:T(128)} %refs_0_.5, ...), custom_call_target="tpu_custom_call" | custom-call | bytes 75000000 | tf_op jit(solution)/shard_map/pallas_call | solution.py:735
  25.0 58.0 %shard_map.341 = (f32[512,1536]{1,0:T(8,128)}, bf16[512,1536]{1,0:T(8,128)(2,1)}, f32[512,384]{1,0:T(8,128)}, f32[512,384]{1,0:T(8,128)}, bf16[512,384]{1,0:T(8,...) custom-call(bf16[512,1536]{1,0:T(8,128)(2,1)} %refs_1_.3, ...), custom_call_target="tpu_custom_call" | custom-call | bytes 120000000 | tf_op jit(solution)/shard_map/pallas_call | solution.py:735
  83.0 56.5 %shard_map.342 = (bf16[512,1536]{1,0:T(8,128)(2,1)}, f32[512,384]{1,0:T(8,128)}, bf16[512,384]{1,0:T(8,128)(2,1)}, bf16[512,384]{1,0:T(8,128)(2,1)}, f32[4,8,512...) custom-call(bf16[512,384]{1,0:T(8,128)(2,1)} %get-tuple-element.174.refs_0_.refs_12_, ...), custom_call_target="tpu_custom_call" | custom-call | bytes 135000000 | tf_op jit(solution)/shard_map/pallas_call | solution.py:735
  139.5 112.8 %shard_map.343 = (f32[512,1536]{1,0:T(8,128)}, bf16[512,1536]{1,0:T(8,128)(2,1)}, f32[512,384]{1,0:T(8,128)}, bf16[512,384]{1,0:T(8,128)(2,1)}, bf16[512,384]{1,...) custom-call(f32[512,1536]{1,0:T(8,128)} %get-tuple-element.173.refs_, ...), custom_call_target="tpu_custom_call" | custom-call | bytes 270000000 | tf_op jit(solution)/shard_map/pallas_call | solution.py:735
  252.3 33.6 %shard_map.344 = (f32[512,1536]{1,0:T(8,128)}, bf16[512,1536]{1,0:T(8,128)(2,1)}, f32[512,384]{1,0:T(8,128)}, f32[512,384]{1,0:T(8,128)}, bf16[512,384]{1,0:T(8,...) custom-call(f32[512,1536]{1,0:T(8,128)} %get-tuple-element.183.refs_, ...), custom_call_target="tpu_custom_call" | custom-call | bytes 120000000 | tf_op jit(solution)/shard_map/pallas_call | solution.py:735
  285.9 56.3 %shard_map.345 = (bf16[512,1536]{1,0:T(8,128)(2,1)}, f32[512,384]{1,0:T(8,128)}, bf16[512,384]{1,0:T(8,128)(2,1)}, bf16[512,384]{1,0:T(8,128)(2,1)}, f32[4,8,512]{2,1,0:T(8,128)}, /*index=5*/bf16[1536,2240]{1,0:T(8,128)(2,1)}) custom-call(bf16[512,384]{1,0:T(8,128)(2,1)} %get-tuple-element.189.refs_0_.refs_12_, ...), custom_call_target="tpu_custom_call" | custom-call | bytes 135000000 | tf_op jit(solution)/shard_map/pallas_call | solution.py:735
  342.2 108.3 %shard_map.346 = (f32[512,1536]{1,0:T(8,128)}, bf16[512,1536]{1,0:T(8,128)(2,1)}, f32[512,384]{1,0:T(8,128)}, bf16[512,384]{1,0:T(8,128)(2,1)}, bf16[512,384]{1,...) custom-call(f32[512,1536]{1,0:T(8,128)} %get-tuple-element.188.refs_, ...), custom_call_target="tpu_custom_call" | custom-call | bytes 270000000 | tf_op jit(solution)/shard_map/pallas_call | solution.py:735
  450.5 70.4 %shard_map.347 = (f32[512,1536]{1,0:T(8,128)}, f32[512,1536]{1,0:T(8,128)}, bf16[512,1536]{1,0:T(8,128)(2,1)}, f32[8,1536]{1,0:T(8,128)}, f32[8,2240]{1,0:T(8,12...) custom-call(f32[512,1536]{1,0:T(8,128)} %get-tuple-element.198.refs_0_.refs_2_, bf16[512,1536]{1,0:T(8,128)(2,1)} %refs_1_.4, ...), custom_call_target="tpu_custom_call" | custom-call | bytes 180000000 | tf_op jit(solution)/shard_map/pallas_call | solution.py:735
  520.9 63.1 %shard_map.348 = (f32[512,1536]{1,0:T(8,128)}, f32[2,512,384]{2,1,0:T(8,128)}, f32[8,1536]{1,0:T(8,128)}, f32[8,384]{1,0:T(8,128)}, bf16[512,1536]{1,0:T(8,128)(...) custom-call(f32[512,1536]{1,0:T(8,128)} %get-tuple-element.204.refs_0_, ...), custom_call_target="tpu_custom_call" | custom-call | bytes 180000000 | tf_op jit(solution)/shard_map/pallas_call | solution.py:735
  584.0 32.8 %shard_map.349 = (f32[512,1536]{1,0:T(8,128)}, bf16[1536,384]{1,0:T(8,128)(2,1)}, f32[8,1536]{1,0:T(8,128)}, f32[512,384]{1,0:T(8,128)}, f32[2,512,384]{2,1,0:T(8,128)}, /*index=5*/f32[2,128,384]{2,1,0:T(8,128)}) custom-call(f32[4,8,512]{2,1,0:T(8,128)} %get-tuple-element.172.refs_8_.refs_2_.refs_0_, f32[512,1536]{1,0:T(8,128)} %get-tuple-element.213.refs_1_, ...), custom_call_target="tpu_custom_call" | custom-call | bytes 105000000 | tf_op jit(solution)/shard_map/pallas_call | solution.py:735
  616.8 1.0 broadcast_in_dim.3.refs_15_
  617.8 70.8 %shard_map.350 = (f32[16,384]{1,0:T(8,128)}, f32[128,1536]{1,0:T(8,128)}, bf16[512,1536]{1,0:T(8,128)(2,1)}, bf16[1536,1152]{1,0:T(8,128)(2,1)}, bf16[1536,768]{...) custom-call(f32[512,384]{1,0:T(8,128)} %get-tuple-element.222.refs_0_, ...), custom_call_target="tpu_custom_call" | custom-call | bytes 180000000 | tf_op jit(solution)/shard_map/pallas_call | solution.py:735
  688.6 75.2 %shard_map.351 = (f32[512,1536]{1,0:T(8,128)}, f32[8,1536]{1,0:T(8,128)}, bf16[512,1536]{1,0:T(8,128)(2,1)}, f32[8,1536]{1,0:T(8,128)}, f32[8,2240]{1,0:T(8,128)...) custom-call(f32[512,1536]{1,0:T(8,128)} %get-tuple-element.221.refs_0_, ...), custom_call_target="tpu_custom_call" | custom-call | bytes 180000000 | tf_op jit(solution)/shard_map/pallas_call | solution.py:735
  763.8 62.5 %shard_map.352 = (f32[512,1536]{1,0:T(8,128)}, f32[2,512,384]{2,1,0:T(8,128)}, f32[8,1536]{1,0:T(8,128)}, f32[8,384]{1,0:T(8,128)}, bf16[512,1536]{1,0:T(8,128)(...) custom-call(f32[512,1536]{1,0:T(8,128)} %get-tuple-element.241.refs_0_, ...), custom_call_target="tpu_custom_call" | custom-call | bytes 180000000 | tf_op jit(solution)/shard_map/pallas_call | solution.py:735
  826.3 34.7 %shard_map.353 = (f32[512,1536]{1,0:T(8,128)}, bf16[1536,384]{1,0:T(8,128)(2,1)}, f32[8,1536]{1,0:T(8,128)}, f32[512,384]{1,0:T(8,128)}, f32[2,512,384]{2,1,0:T(8,128)}, /*index=5*/f32[2,128,384]{2,1,0:T(8,128)}) custom-call(f32[4,8,512]{2,1,0:T(8,128)} %get-tuple-element.172.refs_8_.refs_2_.refs_0_, f32[512,1536]{1,0:T(8,128)} %get-tuple-element.250.refs_1_, ...), custom_call_target="tpu_custom_call" | custom-call | bytes 105000000 | tf_op jit(solution)/shard_map/pallas_call | solution.py:735
  861.0 69.1 %shard_map.354 = (f32[16,384]{1,0:T(8,128)}, f32[128,1536]{1,0:T(8,128)}, bf16[512,1536]{1,0:T(8,128)(2,1)}, bf16[1536,1152]{1,0:T(8,128)(2,1)}, bf16[1536,768]{...) custom-call(f32[512,384]{1,0:T(8,128)} %get-tuple-element.258.refs_0_, ...), custom_call_target="tpu_custom_call" | custom-call | bytes 180000000 | tf_op jit(solution)/shard_map/pallas_call | solution.py:735
  930.1 3.6 pad_maximum_fusion.1
  933.8 2.0 pad_maximum_fusion
  936.1 1.1 pad_maximum_fusion.4
  937.2 52.8 %shard_map.355 = (f32[512,1536]{1,0:T(8,128)}, bf16[128,1536]{1,0:T(8,128)(2,1)}, f32[48,1536]{1,0:T(8,128)}, f32[48,384]{1,0:T(8,128)}, f32[16,2240]{1,0:T(8,12...) custom-call(f32[128,1536]{1,0:T(8,128)} %get-tuple-element.271.refs_0_, f32[512,1536]{1,0:T(8,128)} %get-tuple-element.272.refs_1_, ...), custom_call_target="tpu_custom_call" | custom-call | bytes 90000000 | tf_op jit(solution)/shard_map/pallas_call | solution.py:735
  989.9 1.2 copy.60
  991.5 1.3 pad_maximum_fusion.3
  992.9 0.4 reshape.54
  993.2 0.3 copy-done.7
  993.5 0.4 reshape.55
  993.9 0.5 pad_maximum_fusion.2
  994.4 1.3 copy.49
  995.7 1.0 convert_element_type.3
  996.7 1.8 shard_map.356
  998.5 1.7 copy.65
  1000.1 1.4 copy-done.1
  1001.5 1.7 copy.66
  (33 shorter events, 0.6 us)
Async XLA Ops:
  861.0 69.1 %copy-start.3 = (f32[192,2240]{1,0:T(8,128)S(1)}, f32[192,2240]{1,0:T(8,128)}, u32[]{:S(2)}) copy-start(f32[192,2240]{1,0:T(8,128)} %get-tuple-element.307) | copy-start | bytes 5160964
  930.1 3.7 copy-start.2
  930.1 3.7 copy-start.4
  933.8 2.1 copy-start.6
  933.8 2.1 copy-start.5
  933.8 2.1 copy-start.11
  933.8 2.1 copy-start.12
  989.9 1.3 copy-start.9
  991.4 1.5 copy-start.8
  991.4 2.1 copy-start.7
  994.4 1.3 copy-start.10
  994.4 4.1 copy-start
  998.5 3.0 copy-start.1

commit v3 on v2

--- a/solution.py
+++ b/solution.py
@@ -9,6 +9,7 @@
 from jax.experimental.pallas import tpu as pltpu
 from jax.sharding import PartitionSpec as P
 
+BEFORE = "before"
 BIAS = "bias"
 BRANCH = "branch"
 CONTEXT = "context"
@@ -106,13 +107,14 @@
     return result
 
 
-def greet(tensor, masks):
+def greet(side, tensor, masks):
     place, me = lax.axis_index(TENSOR), lax.axis_index(DP)
     if tensor:
         for step in range(1, CHAIN):
             signal(tensor=lax.rem(place + step, CHAIN))
     for mask in masks:
         signal(dp=flip(me, mask))
+    side.load(False)
     pl.semaphore_wait(
         pltpu.get_barrier_semaphore(), (CHAIN - 1 if tensor else 0) + len(masks)
     )
@@ -415,8 +417,9 @@
 
 
 class Late:
-    def __init__(self, name, value, low=None, high=None):
+    def __init__(self, name, value, low=None, high=None, lazy=False):
         self.name, self.value, self.low, self.high = name, value, low, high
+        self.lazy = lazy
         shape = value.shape
         if high is not None:
             shape = (high - low,) + shape[1:]
@@ -443,7 +446,13 @@
         self.jobs = jobs
         self.masks = [1 << bit for bit in range(bits_of_dp())] if jobs else []
         self.loads, self.stores, self.open = {}, {}, []
-        self.first_loads = []
+        self.first_loads, self.waiting = [], []
+        self.late_after = False
+
+    def load(self, lazy):
+        for item in [item for item in self.waiting if item[0] == lazy]:
+            item[1].start()
+            self.waiting.remove(item)
 
     def need(self, *names):
         for name in names:
@@ -460,6 +469,8 @@
                 job.start()
         while self.first_loads:
             self.first_loads.pop(0).wait()
+            if not self.first_loads and not self.late_after:
+                self.load(True)
 
     def launch(self, name, source):
         for job in self.jobs:
@@ -714,7 +725,7 @@
             if isinstance(item, Late):
                 held, sem = take(2)
                 copy = pltpu.make_async_copy(item.source(own_in[place]), held, sem)
-                copy.start()
+                side.waiting.append((item.lazy, copy))
                 if item.name is None:
                     side.first_loads.append(copy)
                 side.loads[item.name] = copy
@@ -725,6 +736,8 @@
                 sem = take(1)[0]
                 side.stores[item.name] = pltpu.make_async_copy(held, own_out[place], sem)
                 own_out[place] = held
+        if not remote:
+            side.load(False)
         kernel(side, *own_in, *own_out, *own)
         side.close()
 
@@ -815,7 +828,7 @@
     return ref[index : index + 1]
 
 
-def entry_kernel(
+def first_kernel(
     side,
     lengths,
     block_order,
@@ -830,13 +843,19 @@
     ffn_bias,
     positions,
     table,
+    base,
+    context,
     counts,
     cosine,
     sine,
+    nothing,
     *rest,
 ):
-    packs, (send_sems, recv_sems) = rest[:-2], rest[-2:]
-    greet(False, side.masks)
+    rest = list(rest)
+    packs = rest[: 3 * LAYERS]
+    send_sems, recv_sems = rest[-2:]
+    rest = rest[3 * LAYERS : -2]
+    greet(side, True, side.masks)
     near, far = holders()
     tokens = counts.shape[2]
     clip = lax.axis_index(DP) // HOLD
@@ -874,18 +893,22 @@
         rows_w[KEY_BIAS : KEY_BIAS + 1] = row_of(key_bias, layer)
         rows_w[GAINS : GAINS + 4] = norm_gains[layer]
         rows_f[...] = row_of(ffn_bias, layer)
+    nothing[...] = jnp.zeros(nothing.shape, F32)
     angles = dot(positions[...].astype(F32), table[...], TN, exact=True)
     cosine[...] = jnp.cos(angles)
     sine[...] = jnp.sin(angles)
     to_far.wait_recv()
     onward.start()
-    side.early()
-    side.late()
+    side.move(1, SELF)
+    side.start(1)
     to_near.wait_recv()
     onward.wait_recv()
     for copy in (to_near, to_far, onward):
         copy.wait_send()
-    side.finish()
+    side.finish(SELF)
+    attend_body(
+        side, base, None, None, packs[0], packs[1], side.jobs[0].out, cosine, sine, counts, context, rest
+    )
 
 
 def add_branch(base, tot, bias_row, gate_row):
@@ -893,27 +916,23 @@
 
 
 def attend_kernel(
-    first,
-    side,
-    base,
-    tot,
-    rows_before,
-    rows_d,
-    rows_w,
-    weight,
-    cosine,
-    sine,
-    counts,
-    *refs,
+    side, base, tot, rows_before, rows_d, rows_w, weight, cosine, sine, counts, *refs
 ):
-    refs = list(refs)
-    context = refs.pop(0) if first else None
+    greet(side, True, [1, 2])
+    side.start()
+    attend_body(
+        side, base, tot, rows_before, rows_d, rows_w, weight, cosine, sine, counts, None, list(refs)
+    )
+
+
+def attend_body(
+    side, base, tot, rows_before, rows_d, rows_w, weight, cosine, sine, counts, context, refs
+):
+    first = context is not None
     hidden, normal, query, key, query_rot, key_value, slots = refs[:7]
     others, result, lse = refs[7:10]
     clip_context = refs[10] if first else None
     scores, send_sems, recv_sems, hold_sends, hold_recvs = refs[-5:]
-    greet(True, side.masks or [1, 2])
-    side.start()
     tokens, width = query.shape
     features = hidden.shape[1]
     heads = width // HEAD_DIM
@@ -936,7 +955,8 @@
         for head in range(heads):
             key_value[head, 1, rows] = value[:, head_cols(head)]
 
-    side.need(WEIGHT)
+    if not first:
+        side.need(WEIGHT)
     loop_rows(tokens, 256, project)
     side.store(HIDDEN, NORMAL, QUERY, KEY)
     exchange = Exchange(slots, send_sems, recv_sems)
@@ -960,7 +980,8 @@
     exchange.finish()
     query_inv = inverse_rms(stat_column(slots, 0, HEAD_DIM), features)
     key_inv = inverse_rms(stat_column(slots, 1, HEAD_DIM), features)
-    side.need(COSINE, SINE)
+    if not first:
+        side.need(COSINE, SINE)
     for head in range(heads):
         cols = head_cols(head)
         rows = key[:, cols] * key_inv * rows_w[GAINS + 1 : GAINS + 2, cols]
@@ -1061,7 +1082,7 @@
     peers,
     sems,
 ):
-    greet(True, side.masks)
+    greet(side, True, side.masks)
     side.start()
     chain = Chain(part, total, (came, pair, peers), sems)
     tokens, features = total.shape
@@ -1124,7 +1145,8 @@
     send_sems, recv_sems, total = refs[12:15]
     part, came, pair, peers, sems = refs[15:20]
     part_f, came_f, pair_f, peers_f, sems_f = refs[20:25]
-    greet(True, side.masks)
+    greet(side, True, side.masks)
+    side.late_after = True
     side.start()
     chain = Chain(part, total, (came, pair, peers), sems)
     chain_f = Chain(part_f, total_f, (came_f, pair_f, peers_f), sems_f)
@@ -1143,6 +1165,7 @@
         query[rows] = dot(block, weight[...]) + row_of(rows_w, 2)
 
     side.need(WEIGHT)
+    side.load(True)
     loop_rows(tokens, 256, project)
     side.store(HIDDEN, NORMAL, QUERY)
     exchange = Exchange(slots, send_sems, recv_sems)
@@ -1347,7 +1370,8 @@
         new_grad, output = take(2)
     (total, sums, bias_sum, up_grad, down_grad) = take(5)
     down_in, inner_b, stage, stage_sems, part, came, pair, peers, sems = refs
-    greet(True, side.masks)
+    greet(side, True, side.masks)
+    side.late_after = True
     side.start()
     chain = Chain(part, total, (came, pair, peers), sems)
     tokens = grad.shape[0]
@@ -1422,6 +1446,7 @@
         return chain.chunks
 
     side.need(GRAD, DOWN, SLOPE)
+    side.load(True)
     mlp_loop(
         side, tokens, rows_of, inner, up, chain, inner_b, lambda: side.need(UP), after
     )
@@ -1463,7 +1488,8 @@
     peers,
     sems,
 ):
-    greet(True, side.masks)
+    greet(side, True, side.masks)
+    side.late_after = True
     side.start()
     chain = Chain(part, total, (came, pair, peers), sems)
     tokens, width = query.shape
@@ -1487,6 +1513,7 @@
         out_grad[rows] = dot(block, out_weight[...]).astype(BF16)
 
     side.need(OUT)
+    side.load(True)
     loop_rows(tokens, 256, enter)
     side.store(NEW_GRAD)
     side.need(QUERY, QUERY_B, TEXT_KB, TEXT_VB)
@@ -1572,7 +1599,7 @@
     send_sems,
     recv_sems,
 ):
-    greet(False, [1, 2])
+    greet(side, False, [1, 2])
     side.start()
     near, far = holders()
     tokens, width = query.shape
@@ -1732,7 +1759,7 @@
     peers,
     sems,
 ):
-    greet(True, side.masks)
+    greet(side, True, side.masks)
     side.start()
     chain = Chain(part, total, (came, pair, peers), sems)
     tokens, width = query.shape
@@ -1827,6 +1854,7 @@
     tiled_grad(context, text_b, keep(text_matrix), lambda tile: None)
     side.store(TEXT_MATRIX)
     chain.serve(4)
+    side.need(BEFORE)
     context_part[...] = (
         context_before[...]
         + dot(text_b[:, :width], text_weight[0], NT)
@@ -1869,7 +1897,7 @@
     away = [take(3) for _ in range(bits)]
     landed = [take(3) for _ in range(bits)]
     send_sems, recv_sems = take(2)
-    greet(True, side.masks)
+    greet(side, True, side.masks)
     side.start()
     me = lax.axis_index(DP)
     clip = me // HOLD
@@ -1942,10 +1970,46 @@
     side.finish()
 
 
-def unpack_kernel(
-    clips, side, lengths, rows_d, rows_w, rows_f, loss, time, bias, key_bias, gains, hidden, out,
-    gain, shift, mods
-):
+def unpack_kernel(clips, side, *refs):
+    refs = list(refs)
+
+    def take(count):
+        taken = refs[:count]
+        del refs[:count]
+        return taken
+
+    lengths, rows_d, rows_w, rows_f, context_sum = take(5)
+    parts = [take(6) for _ in range(LAYERS)]
+    whole = take(2)
+    loss, time, bias, key_bias, gains, hidden, out, gain, shift, mods = take(10)
+    context_grad = take(1)[0]
+    self_all, cross_all, out_all, up_all, down_all = take(5)
+    whole_out = take(2)
+    (sems,) = refs
+    width = key_bias.shape[1]
+    context_grad[...] = context_sum[...].astype(F32)
+    copies = []
+
+    def copy(source, target):
+        item = pltpu.make_async_copy(source, target, sems.at[len(copies)])
+        item.start()
+        copies.append(item)
+
+    for layer in range(LAYERS):
+        side.need(*range(6 * layer, 6 * layer + 6))
+        up, down, cross, text, self_part, out0 = parts[layer]
+        copy(up, up_all.at[layer])
+        copy(down, down_all.at[layer])
+        for member in range(3):
+            copy(self_part.at[:, member * width : (member + 1) * width], self_all.at[layer, member])
+        copy(cross.at[:, :width], cross_all.at[layer, 0])
+        copy(text.at[:, :width], cross_all.at[layer, 1])
+        copy(text.at[:, width:], cross_all.at[layer, 2])
+        copy(out0, out_all.at[layer, 0])
+        copy(cross.at[:, width:], out_all.at[layer, 1])
+    side.need(6 * LAYERS, 6 * LAYERS + 1)
+    for source, target in zip(whole, whole_out):
+        copy(source, target)
     places, count = small_rows(clips)
     for layer in range(LAYERS):
         for row in range(6):
@@ -1969,6 +2033,8 @@
         count = count + lengths[index]
     total = jnp.sum(row_of(rows_d, places[LOSS]), axis=1, keepdims=True)
     loss[...] = jnp.broadcast_to(total, loss.shape) / (count.astype(F32) * rows_d.shape[1])
+    for item in copies:
+        item.wait()
 
 
 def per_device(
@@ -2013,9 +2079,28 @@
     kv_shape = (heads, 2, tokens, HEAD_DIM)
 
     pack = (((16, features), F32), ((16, width), F32), ((1, hidden_width), F32))
-    results, (self_w,) = run(
-        "entry",
-        entry_kernel,
+    attend_outs = (
+        Early(HIDDEN, rows_d, F32),
+        Early(NORMAL, rows_d, BF16),
+        Early(QUERY, rows_w, F32),
+        Early(KEY, rows_w, F32),
+        Early(QUERY_ROT, rows_w, BF16),
+        (kv_shape, BF16),
+        (stats, F32),
+        ((HOLD - 1,) + kv_shape, BF16),
+        (rows_w, BF16),
+        ((8, tokens), F32),
+    )
+    attend_scratch = [
+        pltpu.VMEM((heads, HOLD, tokens, tokens), F32),
+        three,
+        three,
+        pltpu.SemaphoreType.DMA((4 + 2 * heads,)),
+        pltpu.SemaphoreType.DMA((4 + 2 * heads,)),
+    ]
+    results, found = run(
+        "first",
+        first_kernel,
         (
             lengths,
             block_order,
@@ -2030,19 +2115,33 @@
             ffn_bias,
             positions,
             rope_table(HEAD_DIM),
+            latents,
+            context,
         ),
-        (((HOLD, 8, tokens), F32), ((tokens, HEAD_DIM), F32), ((tokens, HEAD_DIM), F32))
-        + pack * LAYERS,
-        [three, three],
-        jobs=[Gather(self_proj, 0)],
+        (
+            ((HOLD, 8, tokens), F32),
+            ((tokens, HEAD_DIM), F32),
+            ((tokens, HEAD_DIM), F32),
+            (context.shape, F32),
+        )
+        + pack * LAYERS
+        + attend_outs
+        + (((text_all, features), BF16),),
+        attend_scratch + [three, three],
+        jobs=[
+            Gather(self_proj, 0, name=SELF, held=True),
+            Gather(cross_proj, 0, wave=1),
+            Gather(out_t, 0, wave=1),
+        ],
         scalars=2,
-        micros=25,
+        micros=70,
     )
-    counts, cosine, sine = results[:3]
-    packs = [results[3 + 3 * layer : 6 + 3 * layer] for layer in range(LAYERS)]
-
+    counts, cosine, sine, context_part = results[:4]
+    packs = [results[4 + 3 * layer : 7 + 3 * layer] for layer in range(LAYERS)]
+    attended = results[4 + 3 * LAYERS :]
+    clip_context = attended[10]
+    weights = {SELF: [found[0]], CROSS: [found[1]], OUT: [found[2]], UP: [], DOWN: []}
     saved = []
-    weights = {SELF: [self_w], CROSS: [], OUT: [], UP: [], DOWN: []}
     sources = {
         SELF: self_proj,
         CROSS: cross_proj,
@@ -2061,57 +2160,34 @@
     base, tot, before = latents, latents, packs[0][0]
     for layer in range(LAYERS):
         pack_d, pack_w, pack_f = packs[layer]
-        names = (CROSS, OUT) if layer == 0 else ()
-        results, found = run(
-            "attend" + str(layer > 0),
-            functools.partial(attend_kernel, layer == 0),
-            (
-                base,
-                tot,
-                before,
-                pack_d,
-                pack_w,
-                Late(WEIGHT, weights[SELF][layer]),
-                Late(COSINE, cosine),
-                Late(SINE, sine),
-                counts,
+        if layer > 0:
+            attended, unused = run(
+                "attend",
+                attend_kernel,
+                (
+                    base,
+                    tot,
+                    before,
+                    pack_d,
+                    pack_w,
+                    Late(WEIGHT, weights[SELF][layer]),
+                    Late(COSINE, cosine, lazy=True),
+                    Late(SINE, sine, lazy=True),
+                    counts,
+                ),
+                attend_outs,
+                attend_scratch,
+                micros=35,
             )
-            + ((context,) if layer == 0 else ()),
-            (
-                Early(HIDDEN, rows_d, F32),
-                Early(NORMAL, rows_d, BF16),
-                Early(QUERY, rows_w, F32),
-                Early(KEY, rows_w, F32),
-                Early(QUERY_ROT, rows_w, BF16),
-                (kv_shape, BF16),
-                (stats, F32),
-                ((HOLD - 1,) + kv_shape, BF16),
-                (rows_w, BF16),
-                ((8, tokens), F32),
-            )
-            + ((((text_all, features), BF16),) if layer == 0 else ()),
-            [
-                pltpu.VMEM((heads, HOLD, tokens, tokens), F32),
-                three,
-                three,
-                pltpu.SemaphoreType.DMA((4 + 2 * heads,)),
-                pltpu.SemaphoreType.DMA((4 + 2 * heads,)),
-            ],
-            jobs=gathers(layer, *names),
-            micros=40,
-        )
-        keep(found, *names)
-        hidden, a1, sq, sk, q_rot, kv, stat1, others, o1, lse1 = results[:10]
-        if layer == 0:
-            clip_context = results[10]
+        hidden, a1, sq, sk, q_rot, kv, stat1, others, o1, lse1 = attended[:10]
         (tot1, ck, ckb, cvb, stat_t), found = run(
             "out_sum",
             out_sum_kernel,
             (
                 o1,
                 Late(OUT, weights[OUT][layer], 0),
-                Late(CONTEXT, clip_context),
-                Late(TEXT_WEIGHT, weights[CROSS][layer], 1, 3),
+                Late(CONTEXT, clip_context, lazy=True),
+                Late(TEXT_WEIGHT, weights[CROSS][layer], 1, 3, lazy=True),
                 pack_w,
             ),
             (
@@ -2145,12 +2221,12 @@
                 pack_w,
                 pack_f,
                 Late(WEIGHT, weights[CROSS][layer], 0),
-                Late(TEXT_KB, ckb),
-                Late(TEXT_VB, cvb),
-                Late(OUT, weights[OUT][layer], 1),
-                Late(UP, weights[UP][layer]),
+                Late(TEXT_KB, ckb, lazy=True),
+                Late(TEXT_VB, cvb, lazy=True),
+                Late(OUT, weights[OUT][layer], 1, lazy=True),
+                Late(UP, weights[UP][layer], lazy=True),
             )
-            + (() if gathered else (Late(DOWN, weights[DOWN][layer]),)),
+            + (() if gathered else (Late(DOWN, weights[DOWN][layer], lazy=True),)),
             (
                 Early(HIDDEN, rows_d, F32),
                 Early(NORMAL, rows_d, BF16),
@@ -2180,7 +2256,6 @@
     grad = base
     reduced = {}
     small = [None] * LAYERS
-    context_part = jnp.zeros(context.shape, F32)
     above = None
     for layer in reversed(range(LAYERS)):
         (hidden, a1, sq, sk, q_rot, kv, stat1, others, o1, lse1, tot1, ck, ckb, cvb, stat_t) = saved[
@@ -2202,10 +2277,10 @@
                 tot3,
                 pack_d,
                 Late(DOWN, w_down),
-                Late(UP, w_up),
+                Late(UP, w_up, lazy=True),
                 Late(SLOPE, slope),
-                Late(NORMAL, a2),
-                Late(GELU_B_NAME, gelu_b),
+                Late(NORMAL, a2, lazy=True),
+                Late(GELU_B_NAME, gelu_b, lazy=True),
             ),
             (
                 Early(NEW_GRAD, rows_d, F32, over=0),
@@ -2245,15 +2320,15 @@
                 pack_d,
                 pack_w,
                 Late(OUT, w_out, 1),
-                Late(QUERY, cq),
-                Late(QUERY_B, cqb),
+                Late(QUERY, cq, lazy=True),
+                Late(QUERY_B, cqb, lazy=True),
                 lse2,
                 stat2,
-                Late(TEXT_KB, ckb),
-                Late(TEXT_VB, cvb),
-                Late(WEIGHT, w_cross, 0),
-                Late(NORMAL, a3),
-                Late(RESULT, o2),
+                Late(TEXT_KB, ckb, lazy=True),
+                Late(TEXT_VB, cvb, lazy=True),
+                Late(WEIGHT, w_cross, 0, lazy=True),
+                Late(NORMAL, a3, lazy=True),
+                Late(RESULT, o2, lazy=True),
             ),
             (
                 Early(NEW_GRAD, rows_d, F32),
@@ -2288,12 +2363,12 @@
                 pack_d,
                 tot1,
                 Late(OUT, w_out, 0),
-                Late(QUERY, q_rot),
-                Late(KEY_VALUE, kv),
-                Late(OTHERS, others),
+                Late(QUERY, q_rot, lazy=True),
+                Late(KEY_VALUE, kv, lazy=True),
+                Late(OTHERS, others, lazy=True),
                 lse1,
                 dct,
-                Late(RESULT, o1),
+                Late(RESULT, o1, lazy=True),
             ),
             (
                 Early(NEW_GRAD, rows_d, F32),
@@ -2332,11 +2407,11 @@
                 pack_w,
                 cosine,
                 sine,
-                Late(WEIGHT, w_self),
-                Late(NORMAL, a1),
-                Late(CONTEXT, context),
-                Late(TEXT_WEIGHT, w_cross, 1, 3),
-                context_part,
+                Late(WEIGHT, w_self, lazy=True),
+                Late(NORMAL, a1, lazy=True),
+                Late(CONTEXT, context, lazy=True),
+                Late(TEXT_WEIGHT, w_cross, 1, 3, lazy=True),
+                Late(BEFORE, context_part, lazy=True),
             ),
             (
                 ((16, width), F32),
@@ -2387,10 +2462,24 @@
         micros=30,
     )
     reduced[TEXT, 0], reduced[SELF, 0] = found
+    names = (UP, DOWN, CROSS, TEXT, SELF, OUT0)
+    size = features // lax.axis_size(DP)
+    far_outs = (
+        ((LAYERS, 3, size, width), F32, True),
+        ((LAYERS, 3, size, width), F32, True),
+        ((LAYERS, 2, size, width), F32, True),
+        ((LAYERS, size, hidden_width), F32, True),
+        ((LAYERS, size, hidden_width), F32, True),
+        (rows_d, F32, True),
+        (rows_d, F32, True),
+    )
+    far_ins = [
+        reduced[name, layer] for layer in range(LAYERS) for name in names
+    ] + [output, grad]
     unpacked, unused = run(
         "unpack",
         functools.partial(unpack_kernel, clip_count),
-        (lengths, packed_d, packed_w, packed_f),
+        (lengths, packed_d, packed_w, packed_f, context_sum) + tuple(Late(place, item) for place, item in enumerate(far_ins)),
         (
             ((1, 128), F32),
             ((6, clip_count, features), F32),
@@ -2402,34 +2491,18 @@
             ((LAYERS, features), F32),
             ((LAYERS, features), F32),
             ((6, LAYERS, features), F32),
-        ),
+            (context.shape, F32),
+        )
+        + far_outs,
+        [pltpu.SemaphoreType.DMA((2 + 10 * LAYERS,))],
         remote=False,
         scalars=1,
-        micros=3,
+        micros=10,
     )
-    loss, time, bias, key_sums, gain_sums, hidden_sums, out_sums, gain, shift, mods = unpacked
-    context_grad = context_sum.astype(F32)
-
-    def split(block):
-        return jnp.swapaxes(block.reshape(block.shape[0], -1, width), 0, 1)
-
-    self_grad = jnp.stack([split(reduced[SELF, layer]) for layer in range(LAYERS)])
-    cross_grad = jnp.stack(
-        [
-            jnp.concatenate(
-                [split(reduced[CROSS, layer])[:1], split(reduced[TEXT, layer])]
-            )
-            for layer in range(LAYERS)
-        ]
-    )
-    out_grad = jnp.stack(
-        [
-            jnp.stack([reduced[OUT0, layer].T, reduced[CROSS, layer][:, width:].T])
-            for layer in range(LAYERS)
-        ]
-    )
-    up_grad = jnp.stack([reduced[UP, layer] for layer in range(LAYERS)])
-    down_grad = jnp.stack([reduced[DOWN, layer].T for layer in range(LAYERS)])
+    loss, time, bias, key_sums, gain_sums, hidden_sums, out_sums, gain, shift, mods = unpacked[:10]
+    context_grad, self_grad, cross_grad, out_grad, up_grad, down_grad, output, grad = unpacked[10:]
+    out_grad = jnp.swapaxes(out_grad, 2, 3)
+    down_grad = jnp.swapaxes(down_grad, 1, 2)
     return (
         output,
         loss[0, 0],

time: 1010 us -> 999 us (0.989)
    pallas_call x17 -> x16, Pallas kernels: 982 us -> 987 us  [run(): pl.pallas_call(body, out_shape=tuple((jax.ShapeDtypeStruct(shape, kind) f...]
where the time goes in v3:
time: 999 us; the launch traced here: 989 us
  Pallas kernels  987 us (99%)
    pallas_call x16, Pallas kernels, run(): pl.pallas_call(body, out_shape=tuple((jax.ShapeDtypeStruct(shape, kind) f...  987 us

profile of v3, /device:TPU:8, one launch (start us, length us, event | category | flops | bytes accessed | tf_op | source)
XLA Modules:
  0.0 989.0 jit_solution(10753321719450288602)
XLA Ops:
  1.3 74.7 %shard_map.340 = (f32[4,8,512]{2,1,0:T(8,128)}, f32[512,128]{1,0:T(8,128)}, f32[512,128]{1,0:T(8,128)}, f32[128,1536]{1,0:T(8,128)}, f32[16,1536]{1,0:T(8,128)},...) custom-call(s32[2]{0:T(128)} %refs_0_.3, ...), custom_call_target="tpu_custom_call" | custom-call | bytes 210000000 | tf_op jit(solution)/shard_map/pallas_call | solution.py:748
  76.0 57.0 %shard_map.341 = (bf16[512,1536]{1,0:T(8,128)(2,1)}, f32[512,384]{1,0:T(8,128)}, bf16[512,384]{1,0:T(8,128)(2,1)}, bf16[512,384]{1,0:T(8,128)(2,1)}, f32[4,8,512...) custom-call(bf16[512,384]{1,0:T(8,128)(2,1)} %get-tuple-element.178.refs_0_.refs_12_, ...), custom_call_target="tpu_custom_call" | custom-call | bytes 135000000 | tf_op jit(solution)/shard_map/pallas_call | solution.py:748
  133.0 113.0 %shard_map.342 = (f32[512,1536]{1,0:T(8,128)}, bf16[512,1536]{1,0:T(8,128)(2,1)}, f32[512,384]{1,0:T(8,128)}, bf16[512,384]{1,0:T(8,128)(2,1)}, bf16[512,384]{1,...) custom-call(f32[512,1536]{1,0:T(8,128)} %get-tuple-element.177.refs_, ...), custom_call_target="tpu_custom_call" | custom-call | bytes 270000000 | tf_op jit(solution)/shard_map/pallas_call | solution.py:748
  246.0 34.5 %shard_map.343 = (f32[512,1536]{1,0:T(8,128)}, bf16[512,1536]{1,0:T(8,128)(2,1)}, f32[512,384]{1,0:T(8,128)}, f32[512,384]{1,0:T(8,128)}, bf16[512,384]{1,0:T(8,...) custom-call(f32[512,1536]{1,0:T(8,128)} %get-tuple-element.189.refs_, ...), custom_call_target="tpu_custom_call" | custom-call | bytes 105000000 | tf_op jit(solution)/shard_map/pallas_call | solution.py:748
  280.5 54.8 %shard_map.344 = (bf16[512,1536]{1,0:T(8,128)(2,1)}, f32[512,384]{1,0:T(8,128)}, bf16[512,384]{1,0:T(8,128)(2,1)}, bf16[512,384]{1,0:T(8,128)(2,1)}, f32[4,8,512]{2,1,0:T(8,128)}, /*index=5*/bf16[1536,2240]{1,0:T(8,128)(2,1)}) custom-call(bf16[512,384]{1,0:T(8,128)(2,1)} %get-tuple-element.197.refs_0_.refs_12_, ...), custom_call_target="tpu_custom_call" | custom-call | bytes 135000000 | tf_op jit(solution)/shard_map/pallas_call | solution.py:748
  335.3 107.9 %shard_map.345 = (f32[512,1536]{1,0:T(8,128)}, bf16[512,1536]{1,0:T(8,128)(2,1)}, f32[512,384]{1,0:T(8,128)}, bf16[512,384]{1,0:T(8,128)(2,1)}, bf16[512,384]{1,...) custom-call(f32[512,1536]{1,0:T(8,128)} %get-tuple-element.196.refs_, ...), custom_call_target="tpu_custom_call" | custom-call | bytes 270000000 | tf_op jit(solution)/shard_map/pallas_call | solution.py:748
  443.2 69.2 %shard_map.346 = (f32[512,1536]{1,0:T(8,128)}, f32[512,1536]{1,0:T(8,128)}, bf16[512,1536]{1,0:T(8,128)(2,1)}, f32[8,1536]{1,0:T(8,128)}, f32[8,2240]{1,0:T(8,12...) custom-call(f32[512,1536]{1,0:T(8,128)} %get-tuple-element.206.refs_0_.refs_2_, bf16[512,1536]{1,0:T(8,128)(2,1)} %refs_1_.2, ...), custom_call_target="tpu_custom_call" | custom-call | bytes 180000000 | tf_op jit(solution)/shard_map/pallas_call | solution.py:748
  512.4 62.7 %shard_map.347 = (f32[512,1536]{1,0:T(8,128)}, f32[2,512,384]{2,1,0:T(8,128)}, f32[8,1536]{1,0:T(8,128)}, f32[8,384]{1,0:T(8,128)}, bf16[512,1536]{1,0:T(8,128)(...) custom-call(f32[512,1536]{1,0:T(8,128)} %get-tuple-element.211.refs_0_, ...), custom_call_target="tpu_custom_call" | custom-call | bytes 180000000 | tf_op jit(solution)/shard_map/pallas_call | solution.py:748
  575.2 33.3 %shard_map.348 = (f32[512,1536]{1,0:T(8,128)}, bf16[1536,384]{1,0:T(8,128)(2,1)}, f32[8,1536]{1,0:T(8,128)}, f32[512,384]{1,0:T(8,128)}, f32[2,512,384]{2,1,0:T(8,128)}, /*index=5*/f32[2,128,384]{2,1,0:T(8,128)}) custom-call(f32[4,8,512]{2,1,0:T(8,128)} %get-tuple-element.176.refs_8_.refs_2_.refs_0_, f32[512,1536]{1,0:T(8,128)} %get-tuple-element.220.refs_1_, ...), custom_call_target="tpu_custom_call" | custom-call | bytes 105000000 | tf_op jit(solution)/shard_map/pallas_call | solution.py:748
  608.4 71.1 %shard_map.349 = (f32[16,384]{1,0:T(8,128)}, f32[128,1536]{1,0:T(8,128)}, bf16[512,1536]{1,0:T(8,128)(2,1)}, bf16[1536,1152]{1,0:T(8,128)(2,1)}, bf16[1536,768]{...) custom-call(f32[512,384]{1,0:T(8,128)} %get-tuple-element.229.refs_0_, ...), custom_call_target="tpu_custom_call" | custom-call | bytes 180000000 | tf_op jit(solution)/shard_map/pallas_call | solution.py:748
  679.5 76.0 %shard_map.350 = (f32[512,1536]{1,0:T(8,128)}, f32[8,1536]{1,0:T(8,128)}, bf16[512,1536]{1,0:T(8,128)(2,1)}, f32[8,1536]{1,0:T(8,128)}, f32[8,2240]{1,0:T(8,128)...) custom-call(f32[512,1536]{1,0:T(8,128)} %get-tuple-element.228.refs_0_, ...), custom_call_target="tpu_custom_call" | custom-call | bytes 180000000 | tf_op jit(solution)/shard_map/pallas_call | solution.py:748
  755.5 62.5 %shard_map.351 = (f32[512,1536]{1,0:T(8,128)}, f32[2,512,384]{2,1,0:T(8,128)}, f32[8,1536]{1,0:T(8,128)}, f32[8,384]{1,0:T(8,128)}, bf16[512,1536]{1,0:T(8,128)(...) custom-call(f32[512,1536]{1,0:T(8,128)} %get-tuple-element.249.refs_0_, ...), custom_call_target="tpu_custom_call" | custom-call | bytes 180000000 | tf_op jit(solution)/shard_map/pallas_call | solution.py:748
  818.0 32.7 %shard_map.352 = (f32[512,1536]{1,0:T(8,128)}, bf16[1536,384]{1,0:T(8,128)(2,1)}, f32[8,1536]{1,0:T(8,128)}, f32[512,384]{1,0:T(8,128)}, f32[2,512,384]{2,1,0:T(8,128)}, /*index=5*/f32[2,128,384]{2,1,0:T(8,128)}) custom-call(f32[4,8,512]{2,1,0:T(8,128)} %get-tuple-element.176.refs_8_.refs_2_.refs_0_, f32[512,1536]{1,0:T(8,128)} %get-tuple-element.258.refs_1_, ...), custom_call_target="tpu_custom_call" | custom-call | bytes 105000000 | tf_op jit(solution)/shard_map/pallas_call | solution.py:748
  850.7 70.1 %shard_map.353 = (f32[16,384]{1,0:T(8,128)}, f32[128,1536]{1,0:T(8,128)}, bf16[512,1536]{1,0:T(8,128)(2,1)}, bf16[1536,1152]{1,0:T(8,128)(2,1)}, bf16[1536,768]{...) custom-call(f32[512,384]{1,0:T(8,128)} %get-tuple-element.266.refs_0_, ...), custom_call_target="tpu_custom_call" | custom-call | bytes 180000000 | tf_op jit(solution)/shard_map/pallas_call | solution.py:748
  920.9 52.2 %shard_map.354 = (f32[512,1536]{1,0:T(8,128)}, bf16[128,1536]{1,0:T(8,128)(2,1)}, f32[48,1536]{1,0:T(8,128)}, f32[48,384]{1,0:T(8,128)}, f32[16,2240]{1,0:T(8,12...) custom-call(f32[128,1536]{1,0:T(8,128)} %get-tuple-element.280.refs_0_, f32[512,1536]{1,0:T(8,128)} %get-tuple-element.281.refs_1_, ...), custom_call_target="tpu_custom_call" | custom-call | bytes 90000000 | tf_op jit(solution)/shard_map/pallas_call | solution.py:748
  973.1 15.7 %shard_map.355 = (f32[1,128]{1,0:T(1,128)}, f32[6,2,1536]{2,1,0:T(2,128)}, f32[5,2,384]{2,1,0:T(2,128)}, f32[2,384]{1,0:T(2,128)}, f32[2,4,384]{2,1,0:T(4,128)},...) custom-call(s32[2]{0:T(128)} %refs_0_.3, ...), custom_call_target="tpu_custom_call" | custom-call | bytes 30000000 | tf_op jit(solution)/shard_map/pallas_call | solution.py:748

commit v4 on v3

--- a/solution.py
+++ b/solution.py
@@ -170,7 +170,7 @@
 
 
 class Gather(Job):
-    def __init__(self, source, layer, name=None, wave=0, held=False):
+    def __init__(self, source, layer, name=None, wave=0, held=False, skewed=False):
         self.layer, self.name, self.wave, self.is_held = layer, name, wave, held
         self.operands = [source]
         shape = source.shape[1:]
@@ -181,7 +181,10 @@
         self.spaces = [pl.ANY]
         self.bits = bits_of_dp()
         plan = []
-        for half, order in enumerate(half_orders(self.bits)):
+        orders = half_orders(self.bits)
+        if skewed:
+            orders = (orders[0], orders[0])
+        for half, order in enumerate(orders):
             for phase, bit in enumerate(order):
                 for mask in masks_over(order[:phase]):
                     plan.append((phase, half, bit, mask))
@@ -844,7 +847,6 @@
     positions,
     table,
     base,
-    context,
     counts,
     cosine,
     sine,
@@ -907,7 +909,7 @@
         copy.wait_send()
     side.finish(SELF)
     attend_body(
-        side, base, None, None, packs[0], packs[1], side.jobs[0].out, cosine, sine, counts, context, rest
+        side, base, None, None, packs[0], packs[1], side.jobs[0].out, cosine, sine, counts, True, rest
     )
 
 
@@ -921,17 +923,15 @@
     greet(side, True, [1, 2])
     side.start()
     attend_body(
-        side, base, tot, rows_before, rows_d, rows_w, weight, cosine, sine, counts, None, list(refs)
+        side, base, tot, rows_before, rows_d, rows_w, weight, cosine, sine, counts, False, list(refs)
     )
 
 
 def attend_body(
-    side, base, tot, rows_before, rows_d, rows_w, weight, cosine, sine, counts, context, refs
+    side, base, tot, rows_before, rows_d, rows_w, weight, cosine, sine, counts, first, refs
 ):
-    first = context is not None
     hidden, normal, query, key, query_rot, key_value, slots = refs[:7]
     others, result, lse = refs[7:10]
-    clip_context = refs[10] if first else None
     scores, send_sems, recv_sems, hold_sends, hold_recvs = refs[-5:]
     tokens, width = query.shape
     features = hidden.shape[1]
@@ -959,24 +959,34 @@
         side.need(WEIGHT)
     loop_rows(tokens, 256, project)
     side.store(HIDDEN, NORMAL, QUERY, KEY)
+    near, far = holders()
+
+    def copy(source, target, number, device):
+        return send(source, target, hold_sends.at[number], hold_recvs.at[number], dp=device)
+
+    to_near = copy(key_value, others.at[0], 0, near)
+    values_far, keys_far = [
+        [
+            copy(
+                key_value.at[head, member],
+                others.at[1, head, member],
+                1 + (1 + member) * heads + head,
+                far,
+            )
+            for head in range(heads)
+        ]
+        for member in (1, 0)
+    ]
+    onward = [
+        copy(others.at[1, head], others.at[2, head], 1 + head, near) for head in range(heads)
+    ]
+    for item in values_far:
+        item.start()
     exchange = Exchange(slots, send_sems, recv_sems)
     exchange.start(
         stat_rows(query[...] * query[...], 0) + stat_rows(key[...] * key[...], 1)
     )
     side.early()
-    near, far = holders()
-
-    def copy(source, target, number, device):
-        return send(source, target, hold_sends.at[number], hold_recvs.at[number], dp=device)
-
-    to_near = copy(key_value, others.at[0], 0, near)
-    to_far = [
-        copy(key_value.at[head], others.at[1, head], 1 + head, far) for head in range(heads)
-    ]
-    onward = [
-        copy(others.at[1, head], others.at[2, head], 1 + heads + head, near)
-        for head in range(heads)
-    ]
     exchange.finish()
     query_inv = inverse_rms(stat_column(slots, 0, HEAD_DIM), features)
     key_inv = inverse_rms(stat_column(slots, 1, HEAD_DIM), features)
@@ -986,25 +996,8 @@
         cols = head_cols(head)
         rows = key[:, cols] * key_inv * rows_w[GAINS + 1 : GAINS + 2, cols]
         key_value[head, 0] = (rows * cosine[...] + turned(rows) * sine[...]).astype(BF16)
-        to_far[head].start()
+        keys_far[head].start()
     to_near.start()
-    text = []
-    if first:
-        place = lax.rem(lax.axis_index(DP), HOLD)
-        size = context.shape[0]
-
-        def block(index):
-            return clip_context.at[pl.ds(pl.multiple_of(index * size, 16), size)]
-
-        low = 1 + 2 * heads
-        clip_context[pl.ds(pl.multiple_of(place * size, 16), size)] = context[...]
-        text = [
-            copy(block(place), block(place), low, near),
-            copy(block(place), block(place), low + 1, far),
-            copy(block(flip(place, 2)), block(flip(place, 2)), low + 2, near),
-        ]
-        text[0].start()
-        text[1].start()
     for head in range(heads):
         cols = head_cols(head)
         rows = query[:, cols] * query_inv * rows_w[GAINS : GAINS + 1, cols]
@@ -1023,7 +1016,8 @@
         score(head, 1, others[0, head, 0])
     lse[...] = jnp.zeros(lse.shape, F32)
     for head in range(heads):
-        to_far[head].wait_recv()
+        values_far[head].wait_recv()
+        keys_far[head].wait_recv()
         onward[head].start()
         if head == 0:
             side.late()
@@ -1042,12 +1036,7 @@
             summed = summed + dot(values, probs.astype(BF16), TN)
         result[:, head_cols(head)] = (summed / total).T.astype(BF16)
         lse[head : head + 1] = top + jnp.log2(total)
-    if first:
-        text[1].wait_recv()
-        text[2].start()
-        text[0].wait_recv()
-        text[2].wait_recv()
-    for item in [to_near] + to_far + onward + text:
+    for item in [to_near] + values_far + keys_far + onward:
         item.wait_send()
     side.finish()
 
@@ -1063,6 +1052,7 @@
 
 
 def out_sum_kernel(
+    first,
     side,
     rows_in,
     weight,
@@ -1074,15 +1064,34 @@
     text_kb,
     text_vb,
     slots,
-    send_sems,
-    recv_sems,
-    part,
-    came,
-    pair,
-    peers,
-    sems,
+    *refs,
 ):
+    refs = list(refs)
+    own, arrived = context, []
+    if first:
+        context = refs.pop(0)
+        clip_sends, clip_recvs = refs[-2:]
+        refs = refs[:-2]
+    send_sems, recv_sems, part, came, pair, peers, sems = refs
     greet(side, True, side.masks)
+    if first:
+        near, far = holders()
+        place = lax.rem(lax.axis_index(DP), HOLD)
+        size = own.shape[0]
+
+        def block(index):
+            return context.at[pl.ds(pl.multiple_of(index * size, 16), size)]
+
+        def copy(number, index, device):
+            return send(
+                block(index), block(index), clip_sends.at[number], clip_recvs.at[number], dp=device
+            )
+
+        arrived = [copy(0, place, near), copy(1, place, far), copy(2, flip(place, 2), near)]
+        side.need(CONTEXT)
+        context[pl.ds(pl.multiple_of(place * size, 16), size)] = own[...]
+        arrived[1].start()
+        arrived[0].start()
     side.start()
     chain = Chain(part, total, (came, pair, peers), sems)
     tokens, features = total.shape
@@ -1094,16 +1103,28 @@
 
     side.need(OUT)
     loop_rows(tokens, 128, project)
-    side.need(CONTEXT, TEXT_WEIGHT)
+    low = 0
+    if first:
+        low = 4
+        chain.segment(0, low, 0, 0)
+        arrived[1].wait_recv()
+        arrived[2].start()
+        arrived[0].wait_recv()
+        arrived[2].wait_recv()
+        for item in arrived:
+            item.wait_send()
+    else:
+        side.need(CONTEXT)
+    side.need(TEXT_WEIGHT)
     text_count, width = text_key.shape
     blocks = text_count // 128
 
     def text(rows, index):
         block = context[rows]
         text_key[rows] = dot(block, text_weight[0]) + row_of(rows_w, 3)
-        chain.serve(2 * index)
+        chain.serve(low + 2 * index)
         text_vb[rows] = (dot(block, text_weight[1]) + row_of(rows_w, 4)).astype(BF16)
-        chain.serve(2 * index + 1)
+        chain.serve(low + 2 * index + 1)
 
     loop_rows(text_count, 128, text)
     exchange = Exchange(slots, send_sems, recv_sems)
@@ -1112,7 +1133,7 @@
         side.early()
         exchange.start(stat_rows(text_key[...] * text_key[...], 0))
 
-    chain.drain(2 * blocks, early, side.middle)
+    chain.drain(low + 2 * blocks, early, side.middle)
     exchange.finish()
     text_inv = inverse_rms(stat_column(slots, 0, HEAD_DIM), features)
     for head in range(width // HEAD_DIM):
@@ -2095,8 +2116,8 @@
         pltpu.VMEM((heads, HOLD, tokens, tokens), F32),
         three,
         three,
-        pltpu.SemaphoreType.DMA((4 + 2 * heads,)),
-        pltpu.SemaphoreType.DMA((4 + 2 * heads,)),
+        pltpu.SemaphoreType.DMA((1 + 3 * heads,)),
+        pltpu.SemaphoreType.DMA((1 + 3 * heads,)),
     ]
     results, found = run(
         "first",
@@ -2116,7 +2137,6 @@
             positions,
             rope_table(HEAD_DIM),
             latents,
-            context,
         ),
         (
             ((HOLD, 8, tokens), F32),
@@ -2125,13 +2145,12 @@
             (context.shape, F32),
         )
         + pack * LAYERS
-        + attend_outs
-        + (((text_all, features), BF16),),
+        + attend_outs,
         attend_scratch + [three, three],
         jobs=[
             Gather(self_proj, 0, name=SELF, held=True),
-            Gather(cross_proj, 0, wave=1),
-            Gather(out_t, 0, wave=1),
+            Gather(cross_proj, 0, wave=1, skewed=True),
+            Gather(out_t, 0, wave=1, skewed=True),
         ],
         scalars=2,
         micros=70,
@@ -2139,7 +2158,6 @@
     counts, cosine, sine, context_part = results[:4]
     packs = [results[4 + 3 * layer : 7 + 3 * layer] for layer in range(LAYERS)]
     attended = results[4 + 3 * LAYERS :]
-    clip_context = attended[10]
     weights = {SELF: [found[0]], CROSS: [found[1]], OUT: [found[2]], UP: [], DOWN: []}
     saved = []
     sources = {
@@ -2180,13 +2198,13 @@
                 micros=35,
             )
         hidden, a1, sq, sk, q_rot, kv, stat1, others, o1, lse1 = attended[:10]
-        (tot1, ck, ckb, cvb, stat_t), found = run(
-            "out_sum",
-            out_sum_kernel,
+        results, found = run(
+            "out_sum" + str(layer),
+            functools.partial(out_sum_kernel, layer == 0),
             (
                 o1,
                 Late(OUT, weights[OUT][layer], 0),
-                Late(CONTEXT, clip_context, lazy=True),
+                Late(CONTEXT, context) if layer == 0 else Late(CONTEXT, clip_context, lazy=True),
                 Late(TEXT_WEIGHT, weights[CROSS][layer], 1, 3, lazy=True),
                 pack_w,
             ),
@@ -2196,14 +2214,18 @@
                 ((text_all, width), BF16),
                 ((text_all, width), BF16),
                 ((CHAIN, 8, text_all), F32),
-            ),
-            [three, three] + chain_scratch,
-            jobs=gathers(layer, UP) + gathers(1, SELF)
+            )
+            + ((((text_all, features), BF16),) if layer == 0 else ()),
+            [three, three] + chain_scratch + ([three, three] if layer == 0 else []),
+            jobs=gathers(layer, UP) + [Gather(self_proj, 1)]
             if layer == 0
             else gathers(layer, DOWN),
             micros=45,
         )
         keep(found, *((UP, SELF) if layer == 0 else (DOWN,)))
+        tot1, ck, ckb, cvb, stat_t = results[:5]
+        if layer == 0:
+            clip_context = results[5]
         gathered = layer == 0
         jobs = [
             Gather(sources[DOWN], 0, name=DOWN, held=True),

time: 999 us -> 988 us (0.989)
  Pallas kernels: 987 us -> 977 us
    pallas_call x16, Pallas kernels: 987 us -> 977 us  [run(): pl.pallas_call(body, out_shape=tuple((jax.ShapeDtypeStruct(shape, kind) f...]
where the time goes in v4:
time: 988 us; the launch traced here: 978 us
  Pallas kernels  977 us (99%)
    pallas_call x16, Pallas kernels, run(): pl.pallas_call(body, out_shape=tuple((jax.ShapeDtypeStruct(shape, kind) f...  977 us

profile of v4, /device:TPU:8, one launch (start us, length us, event | category | flops | bytes accessed | tf_op | source)
XLA Modules:
  0.0 978.4 jit_solution(15774616594123400845)
XLA Ops:
  1.3 64.1 %shard_map.340 = (f32[4,8,512]{2,1,0:T(8,128)}, f32[512,128]{1,0:T(8,128)}, f32[512,128]{1,0:T(8,128)}, f32[128,1536]{1,0:T(8,128)}, f32[16,1536]{1,0:T(8,128)},...) custom-call(s32[2]{0:T(128)} %refs_0_.3, ...), custom_call_target="tpu_custom_call" | custom-call | bytes 210000000 | tf_op jit(solution)/shard_map/pallas_call | solution.py:751
  65.4 59.4 %shard_map.341 = (bf16[512,1536]{1,0:T(8,128)(2,1)}, f32[512,384]{1,0:T(8,128)}, bf16[512,384]{1,0:T(8,128)(2,1)}, bf16[512,384]{1,0:T(8,128)(2,1)}, f32[4,8,512...) custom-call(bf16[512,384]{1,0:T(8,128)(2,1)} %get-tuple-element.178.refs_0_.r, ...), custom_call_target="tpu_custom_call" | custom-call | bytes 135000000 | tf_op jit(solution)/shard_map/pallas_call | solution.py:751
  124.9 113.8 %shard_map.342 = (f32[512,1536]{1,0:T(8,128)}, bf16[512,1536]{1,0:T(8,128)(2,1)}, f32[512,384]{1,0:T(8,128)}, bf16[512,384]{1,0:T(8,128)(2,1)}, bf16[512,384]{1,...) custom-call(f32[512,1536]{1,0:T(8,128)} %get-tuple-element.177.refs_, ...), custom_call_target="tpu_custom_call" | custom-call | bytes 270000000 | tf_op jit(solution)/shard_map/pallas_call | solution.py:751
  238.6 29.9 %shard_map.343 = (f32[512,1536]{1,0:T(8,128)}, bf16[512,1536]{1,0:T(8,128)(2,1)}, f32[512,384]{1,0:T(8,128)}, f32[512,384]{1,0:T(8,128)}, bf16[512,384]{1,0:T(8,...) custom-call(f32[512,1536]{1,0:T(8,128)} %get-tuple-element.188.refs_, ...), custom_call_target="tpu_custom_call" | custom-call | bytes 105000000 | tf_op jit(solution)/shard_map/pallas_call | solution.py:751
  268.6 56.0 %shard_map.344 = (bf16[512,1536]{1,0:T(8,128)(2,1)}, f32[512,384]{1,0:T(8,128)}, bf16[512,384]{1,0:T(8,128)(2,1)}, bf16[512,384]{1,0:T(8,128)(2,1)}, f32[4,8,512]{2,1,0:T(8,128)}, /*index=5*/bf16[1536,2240]{1,0:T(8,128)(2,1)}) custom-call(bf16[512,384]{1,0:T(8,128)(2,1)} %get-tuple-element.196.refs_0_.refs_12_, ...), custom_call_target="tpu_custom_call" | custom-call | bytes 135000000 | tf_op jit(solution)/shard_map/pallas_call | solution.py:751
  324.6 107.3 %shard_map.345 = (f32[512,1536]{1,0:T(8,128)}, bf16[512,1536]{1,0:T(8,128)(2,1)}, f32[512,384]{1,0:T(8,128)}, bf16[512,384]{1,0:T(8,128)(2,1)}, bf16[512,384]{1,...) custom-call(f32[512,1536]{1,0:T(8,128)} %get-tuple-element.195.refs_, ...), custom_call_target="tpu_custom_call" | custom-call | bytes 270000000 | tf_op jit(solution)/shard_map/pallas_call | solution.py:751
  431.9 69.7 %shard_map.346 = (f32[512,1536]{1,0:T(8,128)}, f32[512,1536]{1,0:T(8,128)}, bf16[512,1536]{1,0:T(8,128)(2,1)}, f32[8,1536]{1,0:T(8,128)}, f32[8,2240]{1,0:T(8,12...) custom-call(f32[512,1536]{1,0:T(8,128)} %get-tuple-element.206.refs_0_.refs_2_, bf16[512,1536]{1,0:T(8,128)(2,1)} %refs_1_.2, ...), custom_call_target="tpu_custom_call" | custom-call | bytes 180000000 | tf_op jit(solution)/shard_map/pallas_call | solution.py:751
  501.6 62.5 %shard_map.347 = (f32[512,1536]{1,0:T(8,128)}, f32[2,512,384]{2,1,0:T(8,128)}, f32[8,1536]{1,0:T(8,128)}, f32[8,384]{1,0:T(8,128)}, bf16[512,1536]{1,0:T(8,128)(...) custom-call(f32[512,1536]{1,0:T(8,128)} %get-tuple-element.211.refs_0_, ...), custom_call_target="tpu_custom_call" | custom-call | bytes 180000000 | tf_op jit(solution)/shard_map/pallas_call | solution.py:751
  564.1 32.9 %shard_map.348 = (f32[512,1536]{1,0:T(8,128)}, bf16[1536,384]{1,0:T(8,128)(2,1)}, f32[8,1536]{1,0:T(8,128)}, f32[512,384]{1,0:T(8,128)}, f32[2,512,384]{2,1,0:T(8,128)}, /*index=5*/f32[2,128,384]{2,1,0:T(8,128)}) custom-call(f32[4,8,512]{2,1,0:T(8,128)} %get-tuple-element.176.refs_8_.refs_2_.refs_0_, f32[512,1536]{1,0:T(8,128)} %get-tuple-element.220.refs_1_, ...), custom_call_target="tpu_custom_call" | custom-call | bytes 105000000 | tf_op jit(solution)/shard_map/pallas_call | solution.py:751
  597.0 70.6 %shard_map.349 = (f32[16,384]{1,0:T(8,128)}, f32[128,1536]{1,0:T(8,128)}, bf16[512,1536]{1,0:T(8,128)(2,1)}, bf16[1536,1152]{1,0:T(8,128)(2,1)}, bf16[1536,768]{...) custom-call(f32[512,384]{1,0:T(8,128)} %get-tuple-element.229.refs_0_, ...), custom_call_target="tpu_custom_call" | custom-call | bytes 180000000 | tf_op jit(solution)/shard_map/pallas_call | solution.py:751
  667.6 76.2 %shard_map.350 = (f32[512,1536]{1,0:T(8,128)}, f32[8,1536]{1,0:T(8,128)}, bf16[512,1536]{1,0:T(8,128)(2,1)}, f32[8,1536]{1,0:T(8,128)}, f32[8,2240]{1,0:T(8,128)...) custom-call(f32[512,1536]{1,0:T(8,128)} %get-tuple-element.228.refs_0_, ...), custom_call_target="tpu_custom_call" | custom-call | bytes 180000000 | tf_op jit(solution)/shard_map/pallas_call | solution.py:751
  743.9 62.7 %shard_map.351 = (f32[512,1536]{1,0:T(8,128)}, f32[2,512,384]{2,1,0:T(8,128)}, f32[8,1536]{1,0:T(8,128)}, f32[8,384]{1,0:T(8,128)}, bf16[512,1536]{1,0:T(8,128)(...) custom-call(f32[512,1536]{1,0:T(8,128)} %get-tuple-element.249.refs_0_, ...), custom_call_target="tpu_custom_call" | custom-call | bytes 180000000 | tf_op jit(solution)/shard_map/pallas_call | solution.py:751
  806.6 32.2 %shard_map.352 = (f32[512,1536]{1,0:T(8,128)}, bf16[1536,384]{1,0:T(8,128)(2,1)}, f32[8,1536]{1,0:T(8,128)}, f32[512,384]{1,0:T(8,128)}, f32[2,512,384]{2,1,0:T(8,128)}, /*index=5*/f32[2,128,384]{2,1,0:T(8,128)}) custom-call(f32[4,8,512]{2,1,0:T(8,128)} %get-tuple-element.176.refs_8_.refs_2_.refs_0_, f32[512,1536]{1,0:T(8,128)} %get-tuple-element.258.refs_1_, ...), custom_call_target="tpu_custom_call" | custom-call | bytes 105000000 | tf_op jit(solution)/shard_map/pallas_call | solution.py:751
  838.8 70.5 %shard_map.353 = (f32[16,384]{1,0:T(8,128)}, f32[128,1536]{1,0:T(8,128)}, bf16[512,1536]{1,0:T(8,128)(2,1)}, bf16[1536,1152]{1,0:T(8,128)(2,1)}, bf16[1536,768]{...) custom-call(f32[512,384]{1,0:T(8,128)} %get-tuple-element.266.refs_0_, ...), custom_call_target="tpu_custom_call" | custom-call | bytes 180000000 | tf_op jit(solution)/shard_map/pallas_call | solution.py:751
  909.3 53.1 %shard_map.354 = (f32[512,1536]{1,0:T(8,128)}, bf16[128,1536]{1,0:T(8,128)(2,1)}, f32[48,1536]{1,0:T(8,128)}, f32[48,384]{1,0:T(8,128)}, f32[16,2240]{1,0:T(8,12...) custom-call(f32[128,1536]{1,0:T(8,128)} %get-tuple-element.280.refs_0_, f32[512,1536]{1,0:T(8,128)} %get-tuple-element.281.refs_1_, ...), custom_call_target="tpu_custom_call" | custom-call | bytes 90000000 | tf_op jit(solution)/shard_map/pallas_call | solution.py:751
  962.5 15.7 %shard_map.355 = (f32[1,128]{1,0:T(1,128)}, f32[6,2,1536]{2,1,0:T(2,128)}, f32[5,2,384]{2,1,0:T(2,128)}, f32[2,384]{1,0:T(2,128)}, f32[2,4,384]{2,1,0:T(4,128)},...) custom-call(s32[2]{0:T(128)} %refs_0_.3, ...), custom_call_target="tpu_custom_call" | custom-call | bytes 30000000 | tf_op jit(solution)/shard_map/pallas_call | solution.py:751

commit v5 on v4

--- a/solution.py
+++ b/solution.py
@@ -1628,12 +1628,12 @@
     text_rows = text_sum.shape[1]
     sums[...] = jnp.zeros(sums.shape, F32)
 
-    def copy(kind, head):
+    def copy(kind, head, member):
         return send(
-            away.at[kind, head],
-            landed.at[kind, head],
-            send_sems.at[kind, head],
-            recv_sems.at[kind, head],
+            away.at[kind, head, member],
+            landed.at[kind, head, member],
+            send_sems.at[kind, member * heads + head],
+            recv_sems.at[kind, member * heads + head],
             dp=far if kind == 1 else near,
         )
 
@@ -1641,8 +1641,8 @@
         return send(
             text_away.at[kind],
             text_landed.at[kind],
-            send_sems.at[kind, heads],
-            recv_sems.at[kind, heads],
+            send_sems.at[kind, 2 * heads],
+            recv_sems.at[kind, 2 * heads],
             dp=far if kind == 1 else near,
         )
 
@@ -1687,8 +1687,18 @@
                 return key_value[head, 0], key_value[head, 1]
             return others[slot - 1, head, 0], others[slot - 1, head, 1]
 
+        def share(slot, member, block, head=head, cols=cols):
+            if slot == 0:
+                key_value_grad[member, :, cols] = block
+                return
+            if slot == 2:
+                copy(2, head, member).wait_recv()
+                block = block + landed[2, head, member].astype(F32)
+            away[slot - 1, head, member] = block.astype(BF16)
+            copy(slot - 1, head, member).start()
+
         inner = jnp.zeros((1, tokens), F32)
-        for slot in range(HOLD):
+        for slot in (3, 2, 1, 0):
             keys, values = pair_of(slot)
             block = softmax_back(
                 dot(keys, query_h, NT),
@@ -1699,26 +1709,14 @@
             block_grad = dot(values, out_grad_h, NT)
             prob_grads[slot] = block_grad
             inner = inner + jnp.sum(block * block_grad, axis=0, keepdims=True)
+            share(slot, 1, dot(block.astype(BF16), out_grad_h))
         query_n = jnp.zeros((HEAD_DIM, tokens), F32)
         for slot in (3, 2, 1, 0):
             keys, values = pair_of(slot)
             block = probs[slot]
             score_b = (block * (prob_grads[slot] - inner) * SCALE).astype(BF16)
             query_n = query_n + dot(keys, score_b, TN)
-            key_g = dot(score_b, query_h)
-            value_g = dot(block.astype(BF16), out_grad_h)
-            if slot == 0:
-                key_value_grad[0, :, cols] = key_g
-                key_value_grad[1, :, cols] = value_g
-            elif slot == 2:
-                copy(2, head).wait_recv()
-                away[1, head, 0] = (key_g + landed[2, head, 0].astype(F32)).astype(BF16)
-                away[1, head, 1] = (value_g + landed[2, head, 1].astype(F32)).astype(BF16)
-                copy(1, head).start()
-            else:
-                away[slot - 1, head, 0] = key_g.astype(BF16)
-                away[slot - 1, head, 1] = value_g.astype(BF16)
-                copy(slot - 1, head).start()
+            share(slot, 0, dot(score_b, query_h))
         query_grad[:, cols] = query_n.T
     side.store(QUERY_GRAD)
 
@@ -1732,16 +1730,17 @@
     text_sum[...] = text_part(0) + text_landed[0].astype(F32) + text_landed[1].astype(F32)
     for head in range(heads):
         cols = head_cols(head)
-        copy(0, head).wait_recv()
-        copy(1, head).wait_recv()
         for member in range(2):
+            copy(0, head, member).wait_recv()
+            copy(1, head, member).wait_recv()
             key_value_grad[member, :, cols] += landed[0, head, member].astype(F32) + landed[
                 1, head, member
             ].astype(F32)
     for kind in range(3):
         text_copy(kind).wait_send()
         for head in range(heads):
-            copy(kind, head).wait_send()
+            for member in range(2):
+                copy(kind, head, member).wait_send()
 
 
 def qkv_back_kernel(
@@ -2409,8 +2408,8 @@
                 pltpu.VMEM((3,) + kv_shape, BF16),
                 pltpu.VMEM((3, 2, text_rows, width), BF16),
                 pltpu.VMEM((3, 2, text_rows, width), BF16),
-                pltpu.SemaphoreType.DMA((3, heads + 1)),
-                pltpu.SemaphoreType.DMA((3, heads + 1)),
+                pltpu.SemaphoreType.DMA((3, 2 * heads + 1)),
+                pltpu.SemaphoreType.DMA((3, 2 * heads + 1)),
             ],
             micros=35,
         )

time: 988 us -> 985 us (level)
  no operation moved by 1% of the time
where the time goes in v5:
time: 985 us; the launch traced here: 976 us
  Pallas kernels  974 us (99%)
    pallas_call x16, Pallas kernels, run(): pl.pallas_call(body, out_shape=tuple((jax.ShapeDtypeStruct(shape, kind) f...  974 us

profile of v5, /device:TPU:8, one launch (start us, length us, event | category | flops | bytes accessed | tf_op | source)
XLA Modules:
  0.0 975.6 jit_solution(4032508430736275985)
XLA Ops:
  1.3 64.1 %shard_map.340 = (f32[4,8,512]{2,1,0:T(8,128)}, f32[512,128]{1,0:T(8,128)}, f32[512,128]{1,0:T(8,128)}, f32[128,1536]{1,0:T(8,128)}, f32[16,1536]{1,0:T(8,128)},...) custom-call(s32[2]{0:T(128)} %refs_0_.3, ...), custom_call_target="tpu_custom_call" | custom-call | bytes 210000000 | tf_op jit(solution)/shard_map/pallas_call | solution.py:751
  65.4 59.4 %shard_map.341 = (bf16[512,1536]{1,0:T(8,128)(2,1)}, f32[512,384]{1,0:T(8,128)}, bf16[512,384]{1,0:T(8,128)(2,1)}, bf16[512,384]{1,0:T(8,128)(2,1)}, f32[4,8,512...) custom-call(bf16[512,384]{1,0:T(8,128)(2,1)} %get-tuple-element.178.refs_0_.r, ...), custom_call_target="tpu_custom_call" | custom-call | bytes 135000000 | tf_op jit(solution)/shard_map/pallas_call | solution.py:751
  124.9 113.8 %shard_map.342 = (f32[512,1536]{1,0:T(8,128)}, bf16[512,1536]{1,0:T(8,128)(2,1)}, f32[512,384]{1,0:T(8,128)}, bf16[512,384]{1,0:T(8,128)(2,1)}, bf16[512,384]{1,...) custom-call(f32[512,1536]{1,0:T(8,128)} %get-tuple-element.177.refs_, ...), custom_call_target="tpu_custom_call" | custom-call | bytes 270000000 | tf_op jit(solution)/shard_map/pallas_call | solution.py:751
  238.6 29.9 %shard_map.343 = (f32[512,1536]{1,0:T(8,128)}, bf16[512,1536]{1,0:T(8,128)(2,1)}, f32[512,384]{1,0:T(8,128)}, f32[512,384]{1,0:T(8,128)}, bf16[512,384]{1,0:T(8,...) custom-call(f32[512,1536]{1,0:T(8,128)} %get-tuple-element.188.refs_, ...), custom_call_target="tpu_custom_call" | custom-call | bytes 105000000 | tf_op jit(solution)/shard_map/pallas_call | solution.py:751
  268.6 56.0 %shard_map.344 = (bf16[512,1536]{1,0:T(8,128)(2,1)}, f32[512,384]{1,0:T(8,128)}, bf16[512,384]{1,0:T(8,128)(2,1)}, bf16[512,384]{1,0:T(8,128)(2,1)}, f32[4,8,512]{2,1,0:T(8,128)}, /*index=5*/bf16[1536,2240]{1,0:T(8,128)(2,1)}) custom-call(bf16[512,384]{1,0:T(8,128)(2,1)} %get-tuple-element.196.refs_0_.refs_12_, ...), custom_call_target="tpu_custom_call" | custom-call | bytes 135000000 | tf_op jit(solution)/shard_map/pallas_call | solution.py:751
  324.6 107.3 %shard_map.345 = (f32[512,1536]{1,0:T(8,128)}, bf16[512,1536]{1,0:T(8,128)(2,1)}, f32[512,384]{1,0:T(8,128)}, bf16[512,384]{1,0:T(8,128)(2,1)}, bf16[512,384]{1,...) custom-call(f32[512,1536]{1,0:T(8,128)} %get-tuple-element.195.refs_, ...), custom_call_target="tpu_custom_call" | custom-call | bytes 270000000 | tf_op jit(solution)/shard_map/pallas_call | solution.py:751
  431.9 69.7 %shard_map.346 = (f32[512,1536]{1,0:T(8,128)}, f32[512,1536]{1,0:T(8,128)}, bf16[512,1536]{1,0:T(8,128)(2,1)}, f32[8,1536]{1,0:T(8,128)}, f32[8,2240]{1,0:T(8,12...) custom-call(f32[512,1536]{1,0:T(8,128)} %get-tuple-element.206.refs_0_.refs_2_, bf16[512,1536]{1,0:T(8,128)(2,1)} %refs_1_.2, ...), custom_call_target="tpu_custom_call" | custom-call | bytes 180000000 | tf_op jit(solution)/shard_map/pallas_call | solution.py:751
  501.6 62.5 %shard_map.347 = (f32[512,1536]{1,0:T(8,128)}, f32[2,512,384]{2,1,0:T(8,128)}, f32[8,1536]{1,0:T(8,128)}, f32[8,384]{1,0:T(8,128)}, bf16[512,1536]{1,0:T(8,128)(...) custom-call(f32[512,1536]{1,0:T(8,128)} %get-tuple-element.211.refs_0_, ...), custom_call_target="tpu_custom_call" | custom-call | bytes 180000000 | tf_op jit(solution)/shard_map/pallas_call | solution.py:751
  564.1 32.1 %shard_map.348 = (f32[512,1536]{1,0:T(8,128)}, bf16[1536,384]{1,0:T(8,128)(2,1)}, f32[8,1536]{1,0:T(8,128)}, f32[512,384]{1,0:T(8,128)}, f32[2,512,384]{2,1,0:T(8,128)}, /*index=5*/f32[2,128,384]{2,1,0:T(8,128)}) custom-call(f32[4,8,512]{2,1,0:T(8,128)} %get-tuple-element.176.refs_8_.refs_2_.refs_0_, f32[512,1536]{1,0:T(8,128)} %get-tuple-element.220.refs_1_, ...), custom_call_target="tpu_custom_call" | custom-call | bytes 105000000 | tf_op jit(solution)/shard_map/pallas_call | solution.py:751
  596.2 69.9 %shard_map.349 = (f32[16,384]{1,0:T(8,128)}, f32[128,1536]{1,0:T(8,128)}, bf16[512,1536]{1,0:T(8,128)(2,1)}, bf16[1536,1152]{1,0:T(8,128)(2,1)}, bf16[1536,768]{...) custom-call(f32[512,384]{1,0:T(8,128)} %get-tuple-element.229.refs_0_, ...), custom_call_target="tpu_custom_call" | custom-call | bytes 180000000 | tf_op jit(solution)/shard_map/pallas_call | solution.py:751
  666.1 75.3 %shard_map.350 = (f32[512,1536]{1,0:T(8,128)}, f32[8,1536]{1,0:T(8,128)}, bf16[512,1536]{1,0:T(8,128)(2,1)}, f32[8,1536]{1,0:T(8,128)}, f32[8,2240]{1,0:T(8,128)...) custom-call(f32[512,1536]{1,0:T(8,128)} %get-tuple-element.228.refs_0_, ...), custom_call_target="tpu_custom_call" | custom-call | bytes 180000000 | tf_op jit(solution)/shard_map/pallas_call | solution.py:751
  741.4 62.5 %shard_map.351 = (f32[512,1536]{1,0:T(8,128)}, f32[2,512,384]{2,1,0:T(8,128)}, f32[8,1536]{1,0:T(8,128)}, f32[8,384]{1,0:T(8,128)}, bf16[512,1536]{1,0:T(8,128)(...) custom-call(f32[512,1536]{1,0:T(8,128)} %get-tuple-element.249.refs_0_, ...), custom_call_target="tpu_custom_call" | custom-call | bytes 180000000 | tf_op jit(solution)/shard_map/pallas_call | solution.py:751
  803.9 31.4 %shard_map.352 = (f32[512,1536]{1,0:T(8,128)}, bf16[1536,384]{1,0:T(8,128)(2,1)}, f32[8,1536]{1,0:T(8,128)}, f32[512,384]{1,0:T(8,128)}, f32[2,512,384]{2,1,0:T(8,128)}, /*index=5*/f32[2,128,384]{2,1,0:T(8,128)}) custom-call(f32[4,8,512]{2,1,0:T(8,128)} %get-tuple-element.176.refs_8_.refs_2_.refs_0_, f32[512,1536]{1,0:T(8,128)} %get-tuple-element.258.refs_1_, ...), custom_call_target="tpu_custom_call" | custom-call | bytes 105000000 | tf_op jit(solution)/shard_map/pallas_call | solution.py:751
  835.3 69.7 %shard_map.353 = (f32[16,384]{1,0:T(8,128)}, f32[128,1536]{1,0:T(8,128)}, bf16[512,1536]{1,0:T(8,128)(2,1)}, bf16[1536,1152]{1,0:T(8,128)(2,1)}, bf16[1536,768]{...) custom-call(f32[512,384]{1,0:T(8,128)} %get-tuple-element.266.refs_0_, ...), custom_call_target="tpu_custom_call" | custom-call | bytes 180000000 | tf_op jit(solution)/shard_map/pallas_call | solution.py:751
  905.1 54.6 %shard_map.354 = (f32[512,1536]{1,0:T(8,128)}, bf16[128,1536]{1,0:T(8,128)(2,1)}, f32[48,1536]{1,0:T(8,128)}, f32[48,384]{1,0:T(8,128)}, f32[16,2240]{1,0:T(8,12...) custom-call(f32[128,1536]{1,0:T(8,128)} %get-tuple-element.280.refs_0_, f32[512,1536]{1,0:T(8,128)} %get-tuple-element.281.refs_1_, ...), custom_call_target="tpu_custom_call" | custom-call | bytes 90000000 | tf_op jit(solution)/shard_map/pallas_call | solution.py:751
  959.7 15.7 %shard_map.355 = (f32[1,128]{1,0:T(1,128)}, f32[6,2,1536]{2,1,0:T(2,128)}, f32[5,2,384]{2,1,0:T(2,128)}, f32[2,384]{1,0:T(2,128)}, f32[2,4,384]{2,1,0:T(4,128)},...) custom-call(s32[2]{0:T(128)} %refs_0_.3, ...), custom_call_target="tpu_custom_call" | custom-call | bytes 30000000 | tf_op jit(solution)/shard_map/pallas_call | solution.py:751
